TPU v7x, 32 devices: a whole 2x2x4 slice. The times are simulated.
32 devices in a mesh: pitch: 8 (over z, x), span: 2 (over y), row: 2 (over core).
Axes of the slice: x: 2, y: 2, z: 4, core: 2. Of those that a mesh axis runs over, the one named last changes fastest.
Arguments:
- fields: float32 [3, 128, 32, 512], P(None, 'pitch', 'span', 'row'), may hold values from -6 to 6
- diffusivity: float32 [128, 32, 512], P('pitch', 'span', 'row'), may hold values from 0.01 to 0.1
- mean_flow: bfloat16 [32, 2, 512], P('span', None, 'row'), may hold values from -6 to 6
- radial_kernel: bfloat16 [32, 32], replicated
- tracer_values: float32 [10, 65536], P(None, ('pitch', 'span', 'row')), may hold values from -6 to 6
- tracer_cells: int32 [65536], P(('pitch', 'span', 'row')), may hold values from 0 to 65535
- tracer_dest: int32 [65536, 1], P(('pitch', 'span', 'row')), may hold values from 0 to 7; in each aligned block of 2048 rows (0 to 2047, 2048 to 4095, ...) at most 512 rows name the same one
- interface_map: int32 [2, 128], P('row', 'pitch'), may hold values from 0 to 127, as said below
Outputs:
- advected: float32 [3, 128, 32, 512], P(None, 'pitch', 'span', 'row')
- arrived: float32 [10, 131072], P(None, ('pitch', 'span', 'row'))
Inputs may be any that keep to these rules, and one draw needn't show every extreme that they name: `tracer_cells`: the local index of the owning cell within the block of the device that holds the tracer, i * 16 * 256 + r * 256 + a for local indices i, r, a. `tracer_dest`: at most 512 of the tracers of one device go to one pitch index. `interface_map`: for one offset o of each draw, row 0 holds (i + o) mod 128 and row 1 holds (i - o) mod 128, so the two rows are inverse permutations.
All inputs are finite; a program needn't handle non-finite values.
Results may differ from a plain program's by a relative error of at most 0.0015.
Values may be sent and summed in bfloat16 or wider, within the bound.
No kernel may reach another device: no remote copies, remote signals or barrier semaphores. Data moves between devices by JAX's collectives and lax.ppermute only.
A program may use at most 128 MiB of HBM per device.

v0:
```python
import jax
import jax.numpy as jnp
from jax import lax
from jax.sharding import PartitionSpec as P

SUB = 2


TIME_STEP = 0.9
AXIAL_SPEED = 0.15
PITCH_SPEED = 0.15


def swapped(block, axis, apart):
    count = lax.axis_size(axis)
    route = []
    for low in range(count):
        high = low | 1 << apart
        if high != low and high < count:
            route += [(low, high), (high, low)]
    return lax.ppermute(block, axis, route)


def padded(cells, sides, width):
    for axis, dim in sides:
        count = lax.axis_size(axis)
        head = lax.slice_in_dim(cells, 0, width, axis=dim)
        tail = lax.slice_in_dim(cells, cells.shape[dim] - width, cells.shape[dim], axis=dim)
        cells = jnp.concatenate(
            [
                lax.ppermute(tail, axis, [(i, (i + 1) % count) for i in range(count)]),
                cells,
                lax.ppermute(head, axis, [((i + 1) % count, i) for i in range(count)]),
            ],
            axis=dim,
        )
    return cells


def face_flux(left_values, right_values, left_kappa, right_kappa, face_speed):
    diffusion = -0.5 * (left_kappa + right_kappa) * (right_values - left_values)
    if face_speed is None:
        return diffusion
    return (
        jnp.maximum(face_speed, 0.0) * left_values
        + jnp.minimum(face_speed, 0.0) * right_values
        + diffusion
    )


def interface_ghost(own_face, local_map):
    across = swapped(own_face, "row", 0)
    picked = lax.all_gather(across, "pitch", axis=1, tiled=True)
    return jnp.take(picked, local_map, axis=1)


def update_core(extended, speed_axial, speed_pitch, ghost_face, wall_mask, row_id):
    along_pitch = extended[:, :, 1:-1, :]
    pitch_flux = face_flux(
        along_pitch[:3, :-1],
        along_pitch[:3, 1:],
        along_pitch[3, :-1],
        along_pitch[3, 1:],
        speed_pitch,
    )
    along_radius = extended[:, 1:-1]
    radial_flux = (
        face_flux(
            along_radius[:3, :, :-1],
            along_radius[:3, :, 1:],
            along_radius[3, :, :-1],
            along_radius[3, :, 1:],
            None,
        )
        * wall_mask[:, None]
    )
    core = extended[:, 1:-1, 1:-1]
    pitch_cells = core.shape[1]
    full_stack = jnp.concatenate(
        [core, jnp.broadcast_to(speed_axial[None, None], (1, pitch_cells) + speed_axial.shape)], 0
    )
    upstream = jnp.where(row_id == 0, full_stack[..., 0], ghost_face)
    downstream = jnp.where(row_id == 0, ghost_face, full_stack[..., -1])
    line = jnp.concatenate([upstream[..., None], full_stack, downstream[..., None]], -1)
    face_speed = 0.5 * (line[4, ..., :-1] + line[4, ..., 1:])
    axial_flux = face_flux(
        line[:3, ..., :-1], line[:3, ..., 1:], line[3, ..., :-1], line[3, ..., 1:], face_speed
    )
    divergence = (
        pitch_flux[:, 1:]
        - pitch_flux[:, :-1]
        + radial_flux[:, :, 1:]
        - radial_flux[:, :, :-1]
        + axial_flux[..., 1:]
        - axial_flux[..., :-1]
    )
    return core[:3] - TIME_STEP * divergence


def advance(state, diffusivity, speed_axial, speed_pitch, local_map, wall_mask):
    pitch_cells = state.shape[1]
    stacked = jnp.concatenate([state, diffusivity[None]], 0)
    extended = padded(stacked, (("pitch", 1), ("span", 2)), 1)
    full_stack = jnp.concatenate(
        [stacked, jnp.broadcast_to(speed_axial[None, None], (1, pitch_cells) + speed_axial.shape)],
        0,
    )
    row_id = lax.axis_index("row")
    own_face = jnp.where(row_id == 0, full_stack[..., -1], full_stack[..., 0])
    ghost_face = interface_ghost(own_face, local_map)
    return update_core(extended, speed_axial, speed_pitch, ghost_face, wall_mask, row_id)


def local(
    fields,
    diffusivity,
    mean_flow,
    radial_kernel,
    tracer_values,
    tracer_cells,
    tracer_dest,
    interface_map,
):
    radial_cells = mean_flow.shape[0]
    axial_cells = mean_flow.shape[2]
    flat_width = 2 * axial_cells
    span_id = lax.axis_index("span")
    kernel_cols = lax.dynamic_slice_in_dim(radial_kernel, span_id * radial_cells, radial_cells, 1)
    flat_rows = mean_flow.reshape(radial_cells, flat_width)
    smoothed = lax.psum_scatter(
        jnp.dot(kernel_cols, flat_rows, preferred_element_type=jnp.float32),
        "span",
        scatter_dimension=0,
        tiled=True,
    )
    smoothed = smoothed.reshape(radial_cells, 2, axial_cells)
    speed_axial = AXIAL_SPEED * (1.0 + 0.5 * jnp.tanh(smoothed[:, 0]))
    speed_pitch = PITCH_SPEED * jnp.tanh(smoothed[:, 1])
    plane_size = radial_cells * axial_cells
    sample_fields = jnp.take(fields.reshape(fields.shape[0], -1), tracer_cells, axis=1)
    sample_speed = jnp.take(
        jnp.stack([speed_axial, speed_pitch]).reshape(2, plane_size),
        tracer_cells % plane_size,
        axis=1,
    )
    sampled = jnp.concatenate([sample_fields, sample_speed], 0)
    head_rows = tracer_values[:5]
    tail_rows = tracer_values[5:]
    updated = jnp.concatenate(
        [head_rows + 0.5 * (sampled - head_rows), tail_rows + 0.8 * sampled], 0
    )
    npitch = lax.axis_size("pitch")
    capacity = 2 * tracer_values.shape[1] // npitch
    targets = tracer_dest[:, 0]
    onehot = (targets[:, None] == jnp.arange(npitch, dtype=jnp.int32)[None]).astype(jnp.int32)
    slot_index = jnp.sum((jnp.cumsum(onehot, 0) - onehot) * onehot, 1)
    position = targets * capacity + slot_index
    outgoing = (
        jnp.zeros((tracer_values.shape[0], npitch * capacity), jnp.float32)
        .at[:, position]
        .set(updated)
    )
    arrived = lax.all_to_all(outgoing, "pitch", split_axis=1, concat_axis=1, tiled=True)
    face_index = span_id * radial_cells + jnp.arange(radial_cells + 1, dtype=jnp.int32)
    total_radial = radial_cells * lax.axis_size("span")
    wall_mask = ((face_index > 0) & (face_index < total_radial)).astype(jnp.float32)
    local_map = interface_map[0]
    current = fields
    for substep in range(SUB):
        current = advance(current, diffusivity, speed_axial, speed_pitch, local_map, wall_mask)
    return (current, arrived)


def solution(mesh):
    placed = (
        P(None, "pitch", "span", "row"),
        P("pitch", "span", "row"),
        P("span", None, "row"),
        P(),
        P(None, ("pitch", "span", "row")),
        P(("pitch", "span", "row")),
        P(("pitch", "span", "row"), None),
        P("row", "pitch"),
    )
    return jax.shard_map(
        local,
        mesh=mesh,
        in_specs=placed,
        out_specs=(P(None, "pitch", "span", "row"), P(None, ("pitch", "span", "row"))),
        check_vma=False,
    )
```

profile of v0, /device:TPU:0, one launch (start us, length us, event | category | flops | bytes accessed | tf_op | source)
XLA Modules:
  0.0 211.6 jit_solution(12652539309823100505)
XLA Ops:
  7.2 1.1 copy.897
  8.4 1.3 constant_dynamic-update-slice_fusion
  9.8 3.0 %collective-permute-start = (f32[4,1,16,256]{3,2,1,0:T(8,128)S(1)}, f32[4,1,16,256]{3,2,1,0:T(8,128)S(1)}, u32[]{:S(2)}, u32[]{:S(2)}) collective-permute-start(f32[4,1,16,256]{3,2,1,0:T(8,128)S(1)} %get-tuple-element.57), channel_id=1, source_target_pairs={{0,4},{4,8},{8,12},{12,16},{16,20},{20,24},{24,28},{28,0},{1,5},{5... | collective-permute-start | bytes 196616 | tf_op jit(solution)/shard_map/ppermute | solution.py:31
  12.8 3.1 %collective-permute-start.1 = (f32[4,1,16,256]{3,2,1,0:T(8,128)S(1)}, f32[4,1,16,256]{3,2,1,0:T(8,128)S(1)}, u32[]{:S(2)}, u32[]{:S(2)}) collective-permute-start(f32[4,1,16,256]{3,2,1,0:T(8,128)S(1)} %get-tuple-element.58), channel_id=1, source_target_pairs={{4,0},{8,4},{12,8},{16,12},{20,16},{24,20},{28,24},{0,28},{5,1},{9... | collective-permute-start | bytes 196616 | tf_op jit(solution)/shard_map/ppermute | solution.py:33
  15.9 0.8 fusion.56
  16.8 0.5 copy.763
  17.3 0.7 compare_and_fusion.2
  18.0 16.6 %copy.788 = f32[3,16,16,256]{0,3,2,1:T(8,128)} copy(f32[3,16,16,256]{3,2,1,0:T(8,128)S(1)} %copy-done.2) | data formatting | bytes 1572864 | tf_op args[0]
  34.6 18.1 %gather_fusion = f32[2048,3]{1,0:T(8,128)} fusion(f32[3,65536]{0,1:T(8,128)} %bitcast.120, s32[2048]{0:T(1024)S(1)} %get-tuple-element.74), kind=kCustom, calls=%fused_computation.2 | custom fusion | bytes 57344 | tf_op jit(solution)/shard_map/jit(_take)/gather | solution.py:140
  52.8 2.5 %select_bitcast_fusion.1 = f32[3,2048]{0,1:T(8,128)} fusion(f32[2048,3]{1,0:T(8,128)} %gather_fusion, pred[2048]{0:T(1024)(128)(4,1)S(1)} %get-tuple-element.72), kind=kLoop, calls=%fused_computation.50 | loop fusion | flops 6144 | bytes 51200 | tf_op jit(solution)/shard_map/jit(_take)/select_n | solution.py:140
  55.3 1.6 copy.790
  56.9 2.3 %reduce-window.6 = s32[8,16,128]{2,1,0:T(8,128)S(1)} reduce-window(s32[8,16,128]{2,1,0:T(8,128)S(1)} %fusion.47, s32[]{:T(128)} %constant.36.clone.1), window={size=1x1x128 pad=0_0x0_0x127_0}, to_apply=%region_1.0 | reduce-window | flops 2080768 | bytes 131076 | tf_op jit(solution)/shard_map/reduce-window
  60.0 1.0 copy-done.5
  61.1 0.7 copy.815
  61.7 1.6 collective-permute-start.2
  63.4 0.7 copy.816
  64.4 0.9 copy.741
  65.4 1.4 fusion.14
  66.8 0.8 reshape.138
  68.0 0.8 copy.796
  68.9 0.8 copy.797
  69.7 0.6 bitcast_select_fusion.5
  70.4 0.6 fusion.54
  71.1 0.6 copy.789
  71.7 7.6 %gather_fusion.1 = f32[2048,2]{1,0:T(8,128)} fusion(f32[2,4096]{0,1:T(8,128)S(1)} %copy.789, s32[2048]{0:T(1024)S(1)} %get-tuple-element.75), kind=kCustom, calls=%fused_computation.3 | custom fusion | bytes 40960 | tf_op jit(solution)/shard_map/jit(_take)/gather | solution.py:141
  79.3 1.6 select_bitcast_fusion
  81.4 1.4 copy.792
  82.7 6.5 %scatter_custom_fusion = f32[10,4096]{0,1:T(8,128)S(1)} fusion(s32[2048]{0:T(1024)S(1)} %bitcast.138, f32[2048,10]{1,0:T(8,128)} %copy.792, f32[]{:T(128)} %constant.44.clone.1), kind=kCustom, calls=%fused_computation.51 | custom fusion | bytes 164352 | tf_op jit(solution)/shard_map/scatter | solution.py:161
  89.2 1.3 copy.793
  90.5 3.4 %all-to-all-start = ((f32[10,8,512]{2,0,1:T(8,128)}), f32[10,8,512]{2,0,1:T(8,128)S(1)}, u32[]{:S(2)}, u32[]{:S(2)}) async-start(f32[10,8,512]{2,0,1:T(8,128)} %copy.793), calls=%async_computation.1 | async-start | bytes 524288 | tf_op jit(solution)/shard_map/all_to_all | solution.py:163
  93.9 2.5 %fusion.5 = f32[3,17,16,256]{3,1,2,0:T(8,128)S(1)} fusion(f32[3,17,16,256]{3,2,1,0:T(8,128)} %get-tuple-element.56, f32[3,17,16,256]{3,2,1,0:T(8,128)} %get-tuple-element.55, f32[17,16,256]{2,0,1:T(8,128)} %copy.741, f32[16,256]{1,0:T(8,128)} %get-tuple-element.70, f32[16,256]{1,0:T(8,128)} %get-tuple-element.71), kind=kLoop, calls=%fused_computation.32 | loop fusion | flops 1253376 | bytes 2818048 | tf_op jit(solution)/shard_map/add | solution.py:45
  96.5 0.8 copy.754
  97.3 31.6 %all_gather.6 = f32[5,128,16]{2,1,0:T(8,128)S(1)} all-gather(f32[5,16,16]{2,1,0:T(8,128)S(1)} %copy.754), channel_id=1, replica_groups=mesh['pitch'=8,'span'=2,'row'=2] {'pitch'}, dimensions={1}, use_global_device_ids=true | all-gather | bytes 46080 | tf_op jit(solution)/shard_map/all_gather | solution.py:53
  128.9 1.0 copy.755
  129.9 2.2 %gather_fusion.2 = f32[16,5,16]{2,1,0:T(8,128)} fusion(f32[5,128,16]{2,0,1:T(8,128)} %copy.755, s32[1024]{0:T(1024)S(1)} %pad_clamp_fusion), kind=kCustom, calls=%fused_computation.clone | custom fusion | bytes 10304 | tf_op jit(solution)/shard_map/jit(_take)/gather | solution.py:54
  132.2 1.6 fusion.45
  133.8 2.2 %copy.758 = f32[5,16,16,1]{3,1,2,0:T(8,128)} copy(f32[5,16,16,1]{2,0,1,3:T(8,128)} %get-tuple-element.63) | data formatting | bytes 10240 | tf_op jit(solution)/shard_map/broadcast_in_dim | solution.py:84
  136.0 2.2 %copy.761 = f32[5,16,16,1]{3,1,2,0:T(8,128)} copy(f32[5,16,16,1]{2,0,1,3:T(8,128)} %get-tuple-element.64) | data formatting | bytes 10240 | tf_op jit(solution)/shard_map/broadcast_in_dim | solution.py:84
  138.3 2.0 fusion.2
  140.7 1.0 copy_dynamic-update-slice_fusion.10
  141.7 0.7 copy_dynamic-update-slice_fusion.2
  142.4 0.9 copy_dynamic-update-slice_fusion.9
  143.6 0.9 fusion.23
  145.3 1.0 fusion.60
  146.3 1.9 copy.804
  148.2 0.8 copy.805
  149.2 0.7 fusion.64
  149.8 1.4 collective-permute-start.5
  151.2 3.4 %collective-permute-start.6 = (f32[4,1,16,256]{3,2,1,0:T(8,128)}, f32[4,1,16,256]{3,2,1,0:T(8,128)S(1)}, u32[]{:S(2)}, u32[]{:S(2)}) collective-permute-start(f32[4,1,16,256]{3,2,1,0:T(8,128)} %get-tuple-element.54), channel_id=1, source_target_pairs={{4,0},{8,4},{12,8},{16,12},{20,16},{24,20},{28,24},{0,28},{5,1},{9... | collective-permute-start | bytes 196616 | tf_op jit(solution)/shard_map/ppermute | solution.py:33
  154.6 31.1 %all_gather.7 = f32[5,128,16]{2,1,0:T(8,128)S(1)} all-gather(f32[5,16,16]{2,1,0:T(8,128)S(1)} %copy.779), channel_id=1, replica_groups=mesh['pitch'=8,'span'=2,'row'=2] {'pitch'}, dimensions={1}, use_global_device_ids=true | all-gather | bytes 46080 | tf_op jit(solution)/shard_map/all_gather | solution.py:53
  185.7 1.0 copy.780
  186.7 1.6 gather_fusion.3
  188.3 0.7 fusion.43
  189.0 1.4 copy.783
  190.4 2.2 %copy.786 = f32[5,16,16,1]{3,1,2,0:T(8,128)} copy(f32[5,16,16,1]{2,0,1,3:T(8,128)} %get-tuple-element.62) | data formatting | bytes 10240 | tf_op jit(solution)/shard_map/broadcast_in_dim | solution.py:84
  192.6 1.8 fusion.3
  195.3 1.7 collective-permute-start.7
  197.7 1.0 fusion.8
  198.7 0.9 collective-permute-done.7
  199.7 0.7 copy_dynamic-update-slice_fusion
  200.4 1.0 collective-permute-done.8
  201.9 0.5 fusion.21
  202.4 1.3 copy.795
  203.9 0.9 copy.826
  (101 shorter events, 6.1 us)
Async XLA Ops:
  7.2 8.8 %copy-start = (bf16[32,32]{1,0:T(8,128)(2,1)S(1)}, bf16[32,32]{1,0:T(8,128)(2,1)}, u32[]{:S(2)}) copy-start(bf16[32,32]{1,0:T(8,128)(2,1)} %param.13) | copy-start | bytes 6148
  7.2 59.6 %reduce-scatter.2.cloned.1.call-start = ((), (), s32[]{:S(2)}) async-start(), calls=%async_computation.2 | async-start | bytes 98304 | tf_op jit(solution)/shard_map/reduce_scatter | solution.py:130
  8.3 7.6 %copy-start.14 = (bf16[16,2,256]{2,1,0:T(2,128)(2,1)S(1)}, bf16[16,2,256]{2,1,0:T(2,128)(2,1)}, u32[]{:S(2)}) copy-start(bf16[16,2,256]{2,1,0:T(2,128)(2,1)} %param.12) | copy-start | bytes 49156
  8.3 8.4 %copy-start.2 = (f32[3,16,16,256]{3,2,1,0:T(8,128)S(1)}, f32[3,16,16,256]{3,2,1,0:T(8,128)}, u32[]{:S(2)}) copy-start(f32[3,16,16,256]{3,2,1,0:T(8,128)} %param.10) | copy-start | bytes 2359300
  9.6 7.7 %copy-start.16 = (s32[1,16]{1,0:T(1,128)S(1)}, s32[1,16]{1,0:T(1,128)}, u32[]{:S(2)}) copy-start(s32[1,16]{1,0:T(1,128)} %param.17) | copy-start | bytes 196
  9.6 8.3 %copy-start.13 = (s32[2048]{0:T(1024)S(1)}, s32[2048]{0:T(1024)}, u32[]{:S(2)}) copy-start(s32[2048]{0:T(1024)} %param.15) | copy-start | bytes 24580
  9.8 50.0 %collective-permute-start = (f32[4,1,16,256]{3,2,1,0:T(8,128)S(1)}, f32[4,1,16,256]{3,2,1,0:T(8,128)S(1)}, u32[]{:S(2)}, u32[]{:S(2)}) collective-permute-start(f32[4,1,16,256]{3,2,1,0:T(8,128)S(1)} %get-tuple-element.57), channel_id=1, source_target_pairs={{0,4},{4,8},{8,12},{12,16},{16,20},{20,24},{24,28},{28,0},{1,5},{5... | collective-permute-start | bytes 196616 | tf_op jit(solution)/shard_map/ppermute | solution.py:31
  12.8 47.0 %collective-permute-start.1 = (f32[4,1,16,256]{3,2,1,0:T(8,128)S(1)}, f32[4,1,16,256]{3,2,1,0:T(8,128)S(1)}, u32[]{:S(2)}, u32[]{:S(2)}) collective-permute-start(f32[4,1,16,256]{3,2,1,0:T(8,128)S(1)} %get-tuple-element.58), channel_id=1, source_target_pairs={{4,0},{8,4},{12,8},{16,12},{20,16},{24,20},{28,24},{0,28},{5,1},{9... | collective-permute-start | bytes 196616 | tf_op jit(solution)/shard_map/ppermute | solution.py:33
  17.3 50.4 %copy-start.3 = (f32[3,16,16,256]{3,1,2,0:T(8,128)}, f32[3,16,16,256]{3,1,2,0:T(8,128)S(1)}, u32[]{:S(2)}) copy-start(f32[3,16,16,256]{3,1,2,0:T(8,128)S(1)} %copy.763) | copy-start | bytes 2359300
  52.8 4.1 %copy-start.12 = (s32[2048,1]{0,1:T(1,128)S(1)}, s32[2048,1]{0,1:T(1,128)}, u32[]{:S(2)}) copy-start(s32[2048,1]{0,1:T(1,128)} %param.16) | copy-start | bytes 24580
  59.9 1.0 copy-start.5
  61.7 78.9 %collective-permute-start.2 = (f32[4,18,1,256]{3,0,2,1:T(4,128)}, f32[4,18,1,256]{3,0,2,1:T(4,128)}, u32[]{:S(2)}, u32[]{:S(2)}) collective-permute-start(f32[4,18,1,256]{3,0,2,1:T(4,128)} %copy.815), channel_id=1, source_target_pairs={{0,2},{2,0},{1,3},{3,1},{4,6},{6,4},{5,7},{7,5},{8,10},{10,8},{9,1... | collective-permute-start | bytes 221192 | tf_op jit(solution)/shard_map/ppermute | solution.py:31
  64.0 78.3 %collective-permute-start.3 = (f32[4,18,1,256]{3,0,2,1:T(4,128)}, f32[4,18,1,256]{3,0,2,1:T(4,128)}, u32[]{:S(2)}, u32[]{:S(2)}) collective-permute-start(f32[4,18,1,256]{3,0,2,1:T(4,128)} %copy.816), channel_id=1, source_target_pairs={{2,0},{0,2},{3,1},{1,3},{6,4},{4,6},{7,5},{5,7},{10,8},{8,10},{11,... | collective-permute-start | bytes 221192 | tf_op jit(solution)/shard_map/ppermute | solution.py:33
  68.9 2.2 %copy-start.7 = (f32[5,16,16,1]{2,0,1,3:T(8,128)}, f32[5,16,16,1]{2,0,1,3:T(8,128)S(1)}, u32[]{:S(2)}) copy-start(f32[5,16,16,1]{2,0,1,3:T(8,128)S(1)} %copy.796) | copy-start | bytes 15364
  69.7 1.3 copy-start.8
  70.4 26.1 %collective-permute-start.4 = (f32[5,16,16]{2,0,1:T(8,128)}, f32[5,16,16]{2,0,1:T(8,128)}, u32[]{:S(2)}, u32[]{:S(2)}) collective-permute-start(f32[5,16,16]{2,0,1:T(8,128)} %bitcast_select_fusion.5), channel_id=1, source_target_pairs={{0,1},{1,0},{2,3},{3,2},{4,5},{5,4},{6,7},{7,6},{8,9},{9,8},{10,11... | collective-permute-start | bytes 15368 | tf_op jit(solution)/shard_map/ppermute | solution.py:21
  79.3 1.9 copy-start.11
  90.5 113.2 %all-to-all-start = ((f32[10,8,512]{2,0,1:T(8,128)}), f32[10,8,512]{2,0,1:T(8,128)S(1)}, u32[]{:S(2)}, u32[]{:S(2)}) async-start(f32[10,8,512]{2,0,1:T(8,128)} %copy.793), calls=%async_computation.1 | async-start | bytes 524288 | tf_op jit(solution)/shard_map/all_to_all | solution.py:163
  96.4 35.7 %copy-start.15 = (pred[16]{0:T(512)(128)(4,1)S(1)}, pred[16]{0:T(512)(128)(4,1)}, u32[]{:S(2)}) copy-start(pred[16]{0:T(512)(128)(4,1)} %compare_and_fusion.2) | copy-start | bytes 52
  128.9 9.3 %copy-start.4 = (f32[3,16,16,256]{3,1,2,0:T(8,128)S(1)}, f32[3,16,16,256]{3,1,2,0:T(8,128)}, u32[]{:S(2)}) copy-start(f32[3,16,16,256]{3,1,2,0:T(8,128)} %copy-done.3) | copy-start | bytes 2359300
  140.4 1.3 copy-start.6
  149.1 5.5 %collective-permute-start.9 = (f32[5,16,16]{2,0,1:T(8,128)S(1)}, f32[5,16,16]{2,0,1:T(8,128)S(1)}, u32[]{:S(2)}, u32[]{:S(2)}) collective-permute-start(f32[5,16,16]{2,0,1:T(8,128)S(1)} %bitcast_select_fusion.2), channel_id=1, source_target_pairs={{0,1},{1,0},{2,3},{3,2},{4,5},{5,4},{6,7},{7,6},{8,9},{9,8},{10,11... | collective-permute-start | bytes 15368 | tf_op jit(solution)/shard_map/ppermute | solution.py:21
  149.8 45.0 %collective-permute-start.5 = (f32[4,1,16,256]{3,2,1,0:T(8,128)}, f32[4,1,16,256]{3,2,1,0:T(8,128)S(1)}, u32[]{:S(2)}, u32[]{:S(2)}) collective-permute-start(f32[4,1,16,256]{3,2,1,0:T(8,128)} %get-tuple-element.53), channel_id=1, source_target_pairs={{0,4},{4,8},{8,12},{12,16},{16,20},{20,24},{24,28},{28,0},{1,5},{5... | collective-permute-start | bytes 196616 | tf_op jit(solution)/shard_map/ppermute | solution.py:31
  151.2 43.6 %collective-permute-start.6 = (f32[4,1,16,256]{3,2,1,0:T(8,128)}, f32[4,1,16,256]{3,2,1,0:T(8,128)S(1)}, u32[]{:S(2)}, u32[]{:S(2)}) collective-permute-start(f32[4,1,16,256]{3,2,1,0:T(8,128)} %get-tuple-element.54), channel_id=1, source_target_pairs={{4,0},{8,4},{12,8},{16,12},{20,16},{24,20},{28,24},{0,28},{5,1},{9... | collective-permute-start | bytes 196616 | tf_op jit(solution)/shard_map/ppermute | solution.py:33
  195.3 4.4 %collective-permute-start.7 = (f32[4,18,1,256]{3,0,2,1:T(4,128)S(1)}, f32[4,18,1,256]{3,0,2,1:T(4,128)S(1)}, u32[]{:S(2)}, u32[]{:S(2)}) collective-permute-start(f32[4,18,1,256]{3,0,2,1:T(4,128)S(1)} %copy.820), channel_id=1, source_target_pairs={{0,2},{2,0},{1,3},{3,1},{4,6},{6,4},{5,7},{7,5},{8,10},{10,8},{9,1... | collective-permute-start | bytes 221192 | tf_op jit(solution)/shard_map/ppermute | solution.py:31
  197.0 0.7 copy-start.9
  197.0 0.7 copy-start.10
  197.0 4.4 %collective-permute-start.8 = (f32[4,18,1,256]{3,0,2,1:T(4,128)S(1)}, f32[4,18,1,256]{3,0,2,1:T(4,128)S(1)}, u32[]{:S(2)}, u32[]{:S(2)}) collective-permute-start(f32[4,18,1,256]{3,0,2,1:T(4,128)S(1)} %copy.821), channel_id=1, source_target_pairs={{2,0},{0,2},{3,1},{1,3},{6,4},{4,6},{7,5},{5,7},{10,8},{8,10},{11,... | collective-permute-start | bytes 221192 | tf_op jit(solution)/shard_map/ppermute | solution.py:33
  201.9 2.8 %copy-start.1 = (bf16[32,32]{1,0:T(8,128)(2,1)S(1)}, bf16[32,32]{1,0:T(8,128)(2,1)}, u32[]{:S(2)}) copy-start(bf16[32,32]{1,0:T(8,128)(2,1)} %param.13) | copy-start | bytes 6148
Sparse Core Ops, SparseCore 0:
  16.9 8.5 reduce-scatter.1
where the time goes:
time: 213 us; the launch traced here: 212 us
  local copies, waits for them, and re-layouts  89.4 us (42%)
  blocking collectives  62.8 us (29%)
  other arithmetic  23.4 us (11%)
  starting transfers between devices  18.5 us (9%)
  between operations  14.7 us (7%)
    all_gather x2, blocking collectives, interface_ghost(): picked = lax.all_gather(across, 'pitch', axis=1, tiled=True)  62.8 us
    unnamed x53, local copies, waits for them, and re-layouts  27.2 us
    gather x1, local copies, waits for them, and re-layouts, local(): jnp.take(fields.reshape(fields.shape[0], -1), tracer_cells, axis=1)  18.1 us
    ppermute x4, starting transfers between devices, padded(): lax.ppermute(tail, axis, [(i, (i + 1) % count) for i in range(count)])  7.7 us
    gather x1, local copies, waits for them, and re-layouts, local(): jnp.take(jnp.stack([speed_axial, speed_pitch]).reshape(2, plane_size), tr...  7.59 us
    ppermute x4, starting transfers between devices, padded(): lax.ppermute(head, axis, [((i + 1) % count, i) for i in range(count)])  7.3 us
    scatter x1, local copies, waits for them, and re-layouts, local(): outgoing = jnp.zeros((tracer_values.shape[0], npitch * capacity), jnp.flo...  6.46 us
    broadcast_in_dim x2, local copies, waits for them, and re-layouts, update_core(): downstream[..., None]  4.43 us
  transfers between devices with their start and end apart: 12, of which 2 were waited for; matrix products, arithmetic and copies ran while one was open for 51% of the time, Pallas kernels for 0%

commit v1 on v0

v1 whole, which is shorter than its diff:
```python
import jax
import jax.numpy as jnp
from jax import lax
from jax.experimental import pallas as pl
from jax.experimental.pallas import tpu as pltpu
from jax.sharding import PartitionSpec as P

SUB = 2
TIME_STEP = 0.9
AXIAL_SPEED = 0.15
PITCH_SPEED = 0.15
LANES = 128
EXTRA = 8
SLAB = 32
F32 = jnp.float32
BF16 = jnp.bfloat16
VMEM = pl.BlockSpec(memory_space=pltpu.VMEM)
SMEM = pl.BlockSpec(memory_space=pltpu.SMEM)
VMEM_LIMIT = 48 * 1024 * 1024


def iota(shape, dim):
    return lax.broadcasted_iota(jnp.int32, shape, dim)


def split(x):
    high = x.astype(BF16)
    return high, (x - high.astype(F32)).astype(BF16)


def power(n):
    assert n & (n - 1) == 0
    return n.bit_length() - 1


def call(body, outs, args, specs, scratch=(), flops=0, nbytes=0):
    return pl.pallas_call(
        body,
        out_shape=tuple(jax.ShapeDtypeStruct(s, d) for s, d in outs),
        in_specs=list(specs),
        out_specs=tuple(VMEM for _ in outs),
        scratch_shapes=list(scratch),
        compiler_params=pltpu.CompilerParams(vmem_limit_bytes=VMEM_LIMIT),
        cost_estimate=pl.CostEstimate(flops=flops, bytes_accessed=nbytes, transcendentals=0),
    )(*args)


def edge_rows(f_ref, k_ref, rows):
    parts = []
    for r in rows:
        parts.append(f_ref[:, :, r, :].reshape(-1, f_ref.shape[3]))
        parts.append(k_ref[:, r, :])
    return jnp.concatenate(parts, 0)


def pack_span(f_ref, k_ref, m_ref, *outs):
    radial = f_ref.shape[2]
    top = edge_rows(f_ref, k_ref, (radial - 2, radial - 1))
    bottom = edge_rows(f_ref, k_ref, (0, 1))
    flow = m_ref[...].astype(F32)
    flow = jnp.concatenate([flow[:, 0, :], flow[:, 1, :]], 0).astype(BF16)
    if len(outs) == 1:
        edge = top.shape[0]
        first = lax.axis_index("span") == 0
        outs[0][:edge] = jnp.where(first, top, bottom).astype(BF16)
        outs[0][edge:] = flow
    else:
        outs[0][...] = top.astype(BF16)
        outs[1][...] = bottom.astype(BF16)
        outs[2][...] = flow


def sample_fields(npitch, f_ref, cell_ref, dest_ref, samp_ref, slot_ref):
    nfield, pitch, radial, axial = f_ref.shape
    lines = pitch * radial
    chunks = cell_ref.shape[0]
    table = f_ref[...].reshape(nfield * lines, axial)
    high, low = split(table)
    samp_ref[...] = jnp.zeros(samp_ref.shape, F32)
    for c in range(0, chunks, 2):
        cells = jnp.concatenate([cell_ref[c : c + 1, :], cell_ref[c + 1 : c + 2, :]], 1)
        width = cells.shape[1]
        lane = cells & (axial - 1)
        line = lax.shift_right_logical(cells, power(axial))
        pick = (iota((axial, width), 0) == lane).astype(F32).astype(BF16)
        got = jnp.dot(high, pick, preferred_element_type=F32) + jnp.dot(
            low, pick, preferred_element_type=F32
        )
        mine = iota((lines, width), 0) == line
        for f in range(nfield):
            part = jnp.where(mine, got[f * lines : (f + 1) * lines], 0.0)
            samp_ref[f : f + 1, c * LANES : c * LANES + width] = jnp.sum(part, 0, keepdims=True)
    ones = []
    for c in range(chunks):
        ones.append((iota((npitch, LANES), 0) == dest_ref[c : c + 1, :]).astype(F32))
    stacked = jnp.concatenate(ones, 0)
    before = (iota((LANES, LANES), 0) < iota((LANES, LANES), 1)).astype(F32).astype(BF16)
    prefix = jnp.dot(stacked.astype(BF16), before, preferred_element_type=F32)
    carry = jnp.zeros((npitch, 1), F32)
    for c in range(chunks):
        rank = prefix[c * npitch : (c + 1) * npitch] + carry
        slot = jnp.sum(rank * ones[c], 0, keepdims=True)
        slot_ref[:, c * LANES : (c + 1) * LANES] = slot.astype(jnp.int32)
        carry = carry + jnp.sum(ones[c], 1, keepdims=True)


def dispatch(
    npitch,
    nspan,
    f_ref,
    k_ref,
    m_ref,
    kern_ref,
    tv_ref,
    cell_ref,
    dest_ref,
    samp_ref,
    slot_ref,
    *refs,
):
    nfield, pitch, radial, axial = f_ref.shape
    planes = nfield + 1
    edge = planes * pitch
    if nspan == 2:
        (got_ref,) = refs[:1]
        refs = refs[1:]
        low_ref = high_ref = got_ref
    else:
        low_ref, high_ref, all_ref = refs[:3]
        refs = refs[3:]
    buf_ref, a_ref, b_ref, speed_ref, halo_ref, kern_s, upd_s, lhs_s, face_s = refs
    s = lax.axis_index("span")
    q = lax.axis_index("row")
    even = lax.rem(lax.axis_index("pitch"), 2) == 0

    total = kern_ref.shape[0]
    kern_s[...] = kern_ref[...].astype(F32)
    main = kern_s[pl.ds(pl.multiple_of(s * radial, 8), radial), :]
    above = kern_s[pl.ds(pl.multiple_of(jnp.minimum((s + 1) * radial, total - 8), 8), 8), :]
    below = kern_s[pl.ds(pl.multiple_of(jnp.maximum(s * radial - 8, 0), 8), 8), :]
    wide = jnp.concatenate([main, jnp.where(iota((EXTRA, total), 0) < 4, above, below)], 0).astype(BF16)
    smoothed = []
    flow = m_ref[...].astype(F32)
    for c in range(2):
        if nspan == 2:
            own = flow[:, c, :]
            other = got_ref[2 * edge + c * radial : 2 * edge + (c + 1) * radial, :].astype(F32)
            rows = [jnp.where(s == 0, own, other), jnp.where(s == 0, other, own)]
        else:
            rows = [all_ref[n, c * radial : (c + 1) * radial, :].astype(F32) for n in range(nspan)]
        smoothed.append(
            jnp.dot(wide, jnp.concatenate(rows, 0).astype(BF16), preferred_element_type=F32)
        )
    sa = AXIAL_SPEED * (1.0 + 0.5 * jnp.tanh(smoothed[0]))
    sp = PITCH_SPEED * jnp.tanh(smoothed[1])
    speed_ref[0] = sa
    speed_ref[1] = sp

    chunks = cell_ref.shape[0]
    high, low = split(jnp.concatenate([sa[:radial], sp[:radial]], 0))
    upd_s[...] = jnp.zeros(upd_s.shape, F32)
    for c in range(0, chunks, 2):
        cells = jnp.concatenate([cell_ref[c : c + 1, :], cell_ref[c + 1 : c + 2, :]], 1)
        width = cells.shape[1]
        span = slice(c * LANES, c * LANES + width)
        lane = cells & (axial - 1)
        line = lax.shift_right_logical(cells, power(axial)) & (radial - 1)
        pick = (iota((axial, width), 0) == lane).astype(F32).astype(BF16)
        got = jnp.dot(high, pick, preferred_element_type=F32) + jnp.dot(
            low, pick, preferred_element_type=F32
        )
        mine = iota((radial, width), 0) == line
        sampled = [samp_ref[f : f + 1, span] for f in range(nfield)]
        for n in range(2):
            part = jnp.where(mine, got[n * radial : (n + 1) * radial], 0.0)
            sampled.append(jnp.sum(part, 0, keepdims=True))
        count = len(sampled)
        for v, value in enumerate(sampled):
            head = tv_ref[v : v + 1, span]
            upd_s[v : v + 1, span] = head + 0.5 * (value - head)
            upd_s[count + v : count + v + 1, span] = tv_ref[count + v : count + v + 1, span] + 0.8 * value

    values = tv_ref.shape[0]
    tracers = tv_ref.shape[1]
    capacity = 2 * tracers // npitch
    pad = upd_s.shape[0]
    both = upd_s[...]
    rounded = both.astype(BF16).astype(F32)
    both = jnp.concatenate([rounded, both - rounded], 0)
    dest = jnp.concatenate([dest_ref[c : c + 1, :] for c in range(chunks)], 1)
    for d in range(npitch):
        lhs_s[d * 2 * pad : (d + 1) * 2 * pad, :] = jnp.where(dest == d, both, 0.0).astype(BF16)
    place = (iota((capacity, tracers), 0) == slot_ref[...]).astype(F32).astype(BF16)
    out = lax.dot_general(
        lhs_s[...], place, (((1,), (1,)), ((), ())), preferred_element_type=F32
    )
    for d in range(npitch):
        both = out[d * 2 * pad : (d + 1) * 2 * pad]
        mine = both[:pad] + both[pad:]
        for j in range(capacity // LANES):
            buf_ref[d, q, j * values : (j + 1) * values, :] = mine[
                :values, j * LANES : (j + 1) * LANES
            ]

    sub = iota((EXTRA, axial), 0)
    up0, up1 = high_ref[:edge].astype(F32), high_ref[edge : 2 * edge].astype(F32)
    dn0, dn1 = low_ref[:edge].astype(F32), low_ref[edge : 2 * edge].astype(F32)
    for n in range(edge):
        tile = jnp.where(sub == 0, up0[n : n + 1], 0.0)
        tile = jnp.where(sub == 1, up1[n : n + 1], tile)
        tile = jnp.where(sub == 6, dn0[n : n + 1], tile)
        halo_ref[n] = jnp.where(sub == 7, dn1[n : n + 1], tile)

    stator = q == 0
    tile = pl.ds(pl.multiple_of((1 - q) * (axial - LANES), LANES), LANES)
    blank = jnp.zeros((SLAB - radial - EXTRA, LANES), F32)
    face_s[...] = jnp.zeros(face_s.shape, F32)

    def near(block):
        turned = block.T
        return (
            jnp.where(stator, turned[LANES - 1 : LANES], turned[0:1]),
            jnp.where(stator, turned[LANES - 2 : LANES - 1], turned[1:2]),
        )

    for i in range(pitch):
        parts = []
        for f in range(planes):
            parts.append(f_ref[f, i, :, tile] if f < nfield else k_ref[i, :, tile])
            parts += [halo_ref[f * pitch + i, :, tile], blank]
        first, second = near(jnp.concatenate(parts, 0))
        face_s[i : i + 1] = first
        face_s[pitch + i : pitch + i + 1] = second
    rest = jnp.zeros((LANES - 2 * SLAB, LANES), F32)
    first, second = near(
        jnp.concatenate([speed_ref[0, :, tile], blank, speed_ref[1, :, tile], blank, rest], 0)
    )
    face_s[2 * pitch : 2 * pitch + 1] = first
    face_s[2 * pitch + 1 : 2 * pitch + 2] = second
    face = face_s[...]
    for d in range(npitch):
        buf_ref[d, 1 - q] = face

    def layers(indices, nearest):
        rows = []
        for f in range(planes):
            for i in indices:
                rows.append(f_ref[f, i] if f < nfield else k_ref[i])
        for f in range(planes):
            corner = halo_ref[f * pitch + nearest]
            rows += [corner[0:1], corner[7:8]]
        rows.append(jnp.zeros((8, axial), F32))
        return jnp.concatenate(rows, 0)

    top = layers((pitch - 2, pitch - 1), pitch - 1)
    bottom = layers((0, 1), 0)
    a_ref[...] = jnp.where(even, top, bottom).astype(BF16)
    b_ref[...] = jnp.where(even, bottom, top).astype(BF16)


def transport(
    npitch,
    nspan,
    map_ref,
    f_ref,
    k_ref,
    speed_ref,
    halo_ref,
    a_ref,
    b_ref,
    buf_ref,
    o_ref,
    arr_ref,
    x_s,
    y_s,
    c_s,
    p_s,
):
    nfield, pitch, radial, axial = f_ref.shape
    planes = nfield + 1
    rows = radial + EXTRA
    lanes = axial + LANES
    s = lax.axis_index("span")
    q = lax.axis_index("row")
    even = lax.rem(lax.axis_index("pitch"), 2) == 0
    stator = q == 0

    values = arr_ref.shape[0]
    capacity = arr_ref.shape[1] // npitch
    for p in range(npitch):
        for j in range(capacity // LANES):
            at = p * capacity + j * LANES
            arr_ref[:, at : at + LANES] = buf_ref[p, q, j * values : (j + 1) * values, :]

    x_s[...] = jnp.zeros(x_s.shape, F32)
    ext_hi = jnp.where(even, a_ref[...].astype(F32), b_ref[...].astype(F32))
    ext_lo = jnp.where(even, b_ref[...].astype(F32), a_ref[...].astype(F32))
    sub = iota((EXTRA, axial), 0)
    corner_at = 2 * planes * radial
    for f in range(planes):
        x_s[f, 2 : 2 + pitch, :radial, :axial] = f_ref[f] if f < nfield else k_ref[...]
        x_s[f, 2 : 2 + pitch, radial:, :axial] = halo_ref[f * pitch : (f + 1) * pitch]
        for n in range(2):
            at = (2 * f + n) * radial
            x_s[f, n, :radial, :axial] = ext_lo[at : at + radial]
            x_s[f, 2 + pitch + n, :radial, :axial] = ext_hi[at : at + radial]
        at = corner_at + 2 * f
        for where, ext in ((1, ext_lo), (2 + pitch, ext_hi)):
            tile = jnp.where(sub == 0, ext[at : at + 1], 0.0)
            x_s[f, where, radial:, :axial] = jnp.where(sub == 7, ext[at + 1 : at + 2], tile)

    row = iota((LANES, LANES), 0)
    near_row = jnp.where(stator, 0, LANES - 1)
    far_row = jnp.where(stator, 1, LANES - 2)
    whole = npitch * pitch
    begin = map_ref[0, 0] - 1

    def turned(near, far):
        return jnp.where(row == near_row, near, jnp.where(row == far_row, far, 0.0)).T

    for n in range(pitch + 2):
        j = begin + n
        j = jnp.where(j < 0, j + whole, j)
        j = jnp.where(j >= whole, j - whole, j)
        p = lax.shift_right_logical(j, power(pitch))
        i = j & (pitch - 1)
        block = turned(
            buf_ref[p, 1 - q, pl.ds(i, 1), :], buf_ref[p, 1 - q, pl.ds(pitch + i, 1), :]
        )
        for f in range(planes):
            x_s[f, 1 + n, :, axial:] = block[f * SLAB : f * SLAB + rows]
    block = turned(
        buf_ref[0, 1 - q, 2 * pitch : 2 * pitch + 1, :],
        buf_ref[0, 1 - q, 2 * pitch + 1 : 2 * pitch + 2, :],
    )
    sa = jnp.concatenate([speed_ref[0], block[:rows]], 1)
    sp = jnp.concatenate([speed_ref[1], block[SLAB : SLAB + rows]], 1)

    lane = iota((rows, lanes), 1)
    radius = iota((rows, lanes), 0)
    sa_next = pltpu.roll(sa, lanes - 1, 1)
    wa = 0.5 * TIME_STEP * (sa + sa_next)
    wa_up, wa_dn = jnp.maximum(wa, 0.0), jnp.minimum(wa, 0.0)
    sp = TIME_STEP * sp
    wp_up, wp_dn = jnp.maximum(sp, 0.0), jnp.minimum(sp, 0.0)
    inlet = stator & (lane == lanes - 1)
    outlet = jnp.logical_not(stator) & (lane == axial - 1)
    end = inlet | outlet
    end_a = jnp.where(outlet, TIME_STEP * sa, 0.0)
    end_b = jnp.where(inlet, TIME_STEP * sa_next, 0.0)
    wall = ((radius == radial - 1) & (s == nspan - 1)) | ((radius == rows - 1) & (s == 0))
    half = 0.5 * TIME_STEP

    def pitch_coefficients(k, k_next):
        kappa = half * (k + k_next)
        return wp_up + kappa, wp_dn - kappa

    def stencil(v, v_next, f, aa, ab, kr, pa, pb):
        axial_flux = aa * v + ab * pltpu.roll(v, lanes - 1, 1)
        radial_flux = kr * (v - pltpu.roll(v, rows - 1, 0))
        pitch_flux = pa * v + pb * v_next
        change = (
            axial_flux
            - pltpu.roll(axial_flux, 1, 1)
            + radial_flux
            - pltpu.roll(radial_flux, 1, 0)
            + pitch_flux
            - p_s[f]
        )
        p_s[f] = pitch_flux
        return v - change

    pa, pb = pitch_coefficients(x_s[nfield, 0], x_s[nfield, 1])
    for f in range(nfield):
        p_s[f] = pa * x_s[f, 0] + pb * x_s[f, 1]

    @pl.loop(1, pitch + 3)
    def _(i):
        k = x_s[nfield, i]
        kappa = half * (k + pltpu.roll(k, lanes - 1, 1))
        aa = jnp.where(end, end_a, wa_up + kappa)
        ab = jnp.where(end, end_b, wa_dn - kappa)
        kr = jnp.where(wall, 0.0, half * (k + pltpu.roll(k, rows - 1, 0)))
        pa, pb = pitch_coefficients(k, x_s[nfield, i + 1])
        for n, value in enumerate((aa, ab, kr, pa, pb)):
            c_s[n, i] = value
        for f in range(nfield):
            y_s[f, i] = stencil(x_s[f, i], x_s[f, i + 1], f, aa, ab, kr, pa, pb)

    for f in range(nfield):
        p_s[f] = c_s[3, 1] * y_s[f, 1] + c_s[4, 1] * y_s[f, 2]

    @pl.loop(2, pitch + 2)
    def _(i):
        coefficients = [c_s[n, i] for n in range(5)]
        for f in range(nfield):
            new = stencil(y_s[f, i], y_s[f, i + 1], f, *coefficients)
            o_ref[f, i - 2] = new[:radial, :axial]


def local(
    fields,
    diffusivity,
    mean_flow,
    radial_kernel,
    tracer_values,
    tracer_cells,
    tracer_dest,
    interface_map,
):
    npitch = lax.axis_size("pitch")
    nspan = lax.axis_size("span")
    nfield, pitch, radial, axial = fields.shape
    planes = nfield + 1
    values, tracers = tracer_values.shape
    chunks = tracers // LANES
    capacity = 2 * tracers // npitch
    edge = planes * pitch
    cells = tracer_cells.reshape(chunks, LANES)
    dest = tracer_dest.reshape(chunks, LANES)

    mean_rows = 2 * radial
    if nspan == 2:
        (packed,) = call(
            pack_span,
            [((2 * edge + mean_rows, axial), BF16)],
            (fields, diffusivity, mean_flow),
            [VMEM] * 3,
            nbytes=2**20,
        )
        span_got = (lax.ppermute(packed, "span", [(0, 1), (1, 0)]),)
    else:
        up, down, mean = call(
            pack_span,
            [((2 * edge, axial), BF16)] * 2 + [((mean_rows, axial), BF16)],
            (fields, diffusivity, mean_flow),
            [VMEM] * 3,
            nbytes=2**20,
        )
        span_got = (
            lax.ppermute(up, "span", [(n, n + 1) for n in range(nspan - 1)]),
            lax.ppermute(down, "span", [(n + 1, n) for n in range(nspan - 1)]),
            lax.all_gather(mean, "span"),
        )

    samp, slot = call(
        lambda *refs: sample_fields(npitch, *refs),
        [((8, tracers), F32), ((1, tracers), jnp.int32)],
        (fields, cells, dest),
        [VMEM] * 3,
        flops=4 * nfield * pitch * radial * axial * tracers,
        nbytes=2**20,
    )

    rows = radial + EXTRA
    per_slot = max(values * capacity // LANES, 2 * pitch + 2)
    per_slot = -(-per_slot // 8) * 8
    halo_rows = 2 * planes * radial + 16
    pad = 16
    buf, a_send, b_send, speeds, halo = call(
        lambda *refs: dispatch(npitch, nspan, *refs),
        [
            ((npitch, 2, per_slot, LANES), F32),
            ((halo_rows, axial), BF16),
            ((halo_rows, axial), BF16),
            ((2, rows, axial), F32),
            ((edge, EXTRA, axial), F32),
        ],
        (
            fields,
            diffusivity,
            mean_flow,
            radial_kernel,
            tracer_values,
            cells,
            dest,
            samp,
            slot,
        )
        + span_got,
        [VMEM] * (9 + len(span_got)),
        [
            pltpu.VMEM(radial_kernel.shape, F32),
            pltpu.VMEM((pad, tracers), F32),
            pltpu.VMEM((npitch * 2 * pad, tracers), BF16),
            pltpu.VMEM((per_slot, LANES), F32),
        ],
        flops=2 * npitch * 2 * pad * tracers * capacity,
        nbytes=2**21,
    )
    buf = lax.all_to_all(
        buf.reshape(npitch * 2, per_slot, LANES), ("pitch", "row"), 0, 0
    ).reshape(buf.shape)
    swap = [(n, n ^ 1) for n in range(npitch)]
    turn = [((n + 1) % npitch, ((n ^ 1) + 1) % npitch) for n in range(npitch)]
    a_got = lax.ppermute(a_send, "pitch", swap)
    b_got = lax.ppermute(b_send, "pitch", turn)

    lanes = axial + LANES
    return call(
        lambda *refs: transport(npitch, nspan, *refs),
        [(fields.shape, F32), ((values, npitch * capacity), F32)],
        (interface_map, fields, diffusivity, speeds, halo, a_got, b_got, buf),
        [SMEM] + [VMEM] * 7,
        [
            pltpu.VMEM((planes, pitch + 4, rows, lanes), F32),
            pltpu.VMEM((nfield, pitch + 4, rows, lanes), F32),
            pltpu.VMEM((5, pitch + 4, rows, lanes), F32),
            pltpu.VMEM((nfield, rows, lanes), F32),
        ],
        flops=2**24,
        nbytes=2**22,
    )


def solution(mesh):
    placed = (
        P(None, "pitch", "span", "row"),
        P("pitch", "span", "row"),
        P("span", None, "row"),
        P(),
        P(None, ("pitch", "span", "row")),
        P(("pitch", "span", "row")),
        P(("pitch", "span", "row"), None),
        P("row", "pitch"),
    )
    return jax.shard_map(
        local,
        mesh=mesh,
        in_specs=placed,
        out_specs=(P(None, "pitch", "span", "row"), P(None, ("pitch", "span", "row"))),
        check_vma=False,
    )
```

time: 213 us -> 40.3 us (0.19)
  local copies, waits for them, and re-layouts: 89.4 us -> 3.47 us
  blocking collectives: 62.8 us -> 0 us
  other arithmetic: 23.4 us -> 0 us
  between operations: 14.7 us -> 0.7 us
  Pallas kernels: 0 us -> 13.3 us
  waiting for transfers between devices: 2.01 us -> 7.82 us
  starting transfers between devices: 18.5 us -> 14.6 us
    all_gather x2 -> x0, blocking collectives: 62.8 us -> none  [interface_ghost(): picked = lax.all_gather(across, 'pitch', axis=1, tiled=True)]
    gather x4 -> x0, local copies, waits for them, and re-layouts: 29.5 us -> none  [the longest x1 18.1 us: local(): jnp.take(fields.reshape(fields.shape[0], -1), tracer_cells, axis=1)]
    unnamed x53 -> x20, local copies, waits for them, and re-layouts: 27.2 us -> 3.47 us
    pallas_call x0 -> x4, Pallas kernels: none -> 13.3 us  [call(): pl.pallas_call(body, out_shape=tuple((jax.ShapeDtypeStruct(s, d) for s, d...]
    broadcast_in_dim x5 -> x0, local copies, waits for them, and re-layouts: 8.06 us -> none  [the longest x2 4.43 us: update_core(): downstream[..., None]]
    ppermute x10 -> x3, starting transfers between devices: 15.1 us -> 8.22 us  [the longest x1 3.27 us: local(): b_got = lax.ppermute(b_send, 'pitch', turn)]
    scatter x1 -> x0, local copies, waits for them, and re-layouts: 6.46 us -> none  [local(): outgoing = jnp.zeros((tracer_values.shape[0], npitch * capacity), jnp.flo...]
    ppermute x10 -> x3, waiting for transfers between devices: 1.99 us -> 7.82 us  [the longest x1 5.78 us: local(): b_got = lax.ppermute(b_send, 'pitch', turn)]
  transfers between devices with their start and end apart: 12 -> 4, of which waited for: 2 -> 3; matrix products, arithmetic and copies ran while one was open for 51% -> 0% of each run, Pallas kernels for 0% -> 5%
where the time goes in v1:
time: 40.3 us; the launch traced here: 39.9 us
  starting transfers between devices  14.6 us (36%)
  Pallas kernels  13.3 us (33%)
  waiting for transfers between devices  7.82 us (19%)
  local copies, waits for them, and re-layouts  3.47 us (9%)
  between operations  0.7 us (2%)
    pallas_call x4, Pallas kernels, call(): pl.pallas_call(body, out_shape=tuple((jax.ShapeDtypeStruct(s, d) for s, d...  13.3 us
    all_to_all x1, starting transfers between devices, local(): lax.all_to_all(buf.reshape(npitch * 2, per_slot, LANES), ('pitch', 'row')...  6.38 us
    ppermute x1, waiting for transfers between devices, local(): b_got = lax.ppermute(b_send, 'pitch', turn)  5.78 us
    unnamed x20, local copies, waits for them, and re-layouts  3.47 us
    ppermute x1, starting transfers between devices, local(): b_got = lax.ppermute(b_send, 'pitch', turn)  3.27 us
    ppermute x1, starting transfers between devices, local(): span_got = (lax.ppermute(packed, 'span', [(0, 1), (1, 0)]),)  3.03 us
    ppermute x1, starting transfers between devices, local(): a_got = lax.ppermute(a_send, 'pitch', swap)  1.93 us
    ppermute x1, waiting for transfers between devices, local(): a_got = lax.ppermute(a_send, 'pitch', swap)  1.71 us
  transfers between devices with their start and end apart: 4, of which 3 were waited for; matrix products, arithmetic and copies ran while one was open for 0% of the time, Pallas kernels for 5%

profile of v1, /device:TPU:0, one launch (start us, length us, event | category | flops | bytes accessed | tf_op | source)
XLA Modules:
  0.0 39.9 jit_solution(6297156994620242124)
XLA Ops:
  0.6 0.0 copy-start
  0.6 1.1 %copy-done = f32[3,16,16,256]{3,2,1,0:T(8,128)S(1)} copy-done((f32[3,16,16,256]{3,2,1,0:T(8,128)S(1)}, f32[3,16,16,256]{3,2,1,0:T(8,128)}, u32[]{:S(2)}) %copy-start) | copy-done | bytes 786456
  1.8 0.0 copy-start.2
  1.8 0.9 %copy-done.2 = f32[16,16,256]{2,1,0:T(8,128)S(1)} copy-done((f32[16,16,256]{2,1,0:T(8,128)S(1)}, f32[16,16,256]{2,1,0:T(8,128)}, u32[]{:S(2)}) %copy-start.2) | copy-done | bytes 262168
  2.7 0.0 copy-start.4
  2.7 0.7 %copy-done.4 = bf16[16,2,256]{2,1,0:T(2,128)(2,1)S(1)} copy-done((bf16[16,2,256]{2,1,0:T(2,128)(2,1)S(1)}, bf16[16,2,256]{2,1,0:T(2,128)(2,1)}, u32[]{:S(2)}) %copy-start.4) | copy-done | bytes 16408
  3.4 0.0 copy-start.8
  3.4 0.0 copy-start.9
  3.4 0.1 shard_map.96
  3.6 3.0 %collective-permute-start = (bf16[160,256]{1,0:T(8,128)(2,1)S(1)}, bf16[160,256]{1,0:T(8,128)(2,1)S(1)}, u32[]{:S(2)}, u32[]{:S(2)}) collective-permute-start(bf16[160,256]{1,0:T(8,128)(2,1)S(1)} %shard_map.96), channel_id=1, source_target_pairs={{0,2},{2,0},{1,3},{3,1},{4,6},{6,4},{5,7},{7,5},{8,10},{10,8},{9,1... | collective-permute-start | bytes 245768 | tf_op jit(solution)/shard_map/ppermute | solution.py:431
  6.6 0.0 copy-done.8
  6.6 0.0 copy-done.9
  6.6 0.0 copy-start.3
  6.6 0.0 copy-start.6
  6.6 0.0 copy-start.7
  6.6 2.1 %shard_map.95 = (f32[8,2048]{1,0:T(8,128)S(1)}, s32[1,2048]{1,0:T(1,128)S(1)}) custom-call(f32[3,16,16,256]{3,2,1,0:T(8,128)S(1)} %copy-done, s32[16,128]{1,0:T(8,128)S(1)} %bitcast.5, s32[16,128]{1,0:T(8,128)S(1)} %bitcast.7), custom_call_target="tpu_custom_call" | custom-call | flops 1610612736 | bytes 1048576 | tf_op jit(solution)/shard_map/pallas_call | solution.py:37
  8.7 0.3 collective-permute-done.refs_9_
  9.0 0.0 copy-done.3
  9.0 0.0 copy-done.6
  9.0 0.0 copy-done.7
  9.0 0.0 copy-start.1
  9.0 2.4 %shard_map.97 = (f32[8,2,40,128]{3,2,1,0:T(8,128)}, bf16[144,256]{1,0:T(8,128)(2,1)S(1)}, bf16[144,256]{1,0:T(8,128)(2,1)S(1)}, f32[2,24,256]{2,1,0:T(8,128)S(1)}, f32[64,8,256]{2,1,0:T(8,128)S(1)}) custom-call(f32[3,16,16,256]{3,2,1,0:T(8,128)S(1)} %copy-done, f32[16,16,256]{2,1,0:T(8,128)S(1)} %copy-done.3, bf16[16,2,256]{2,1,0:T(2,128)(2,1)S(1)} %copy-done.4, ...), custom_call_target="tpu_custom_call" | custom-call | flops 536870912 | bytes 2097152 | tf_op jit(solution)/shard_map/pallas_call | solution.py:37
  11.5 6.4 %all-to-all-start = ((f32[16,40,128]{2,1,0:T(8,128)}), f32[16,40,128]{2,1,0:T(8,128)S(1)}, u32[]{:S(2)}, u32[]{:S(2)}) async-start(f32[16,40,128]{2,1,0:T(8,128)} %bitcast.2), calls=%async_computation | async-start | bytes 655360 | tf_op jit(solution)/shard_map/all_to_all | solution.py:491
  17.9 1.9 %collective-permute-start.1 = (bf16[144,256]{1,0:T(8,128)(2,1)S(1)}, bf16[144,256]{1,0:T(8,128)(2,1)S(1)}, u32[]{:S(2)}, u32[]{:S(2)}) collective-permute-start(bf16[144,256]{1,0:T(8,128)(2,1)S(1)} %get-tuple-element.13), channel_id=1, source_target_pairs={{0,4},{4,0},{8,12},{12,8},{16,20},{20,16},{24,28},{28,24},{1,5},{5... | collective-permute-start | bytes 221192 | tf_op jit(solution)/shard_map/ppermute | solution.py:496
  19.8 3.3 %collective-permute-start.2 = (bf16[144,256]{1,0:T(8,128)(2,1)S(1)}, bf16[144,256]{1,0:T(8,128)(2,1)S(1)}, u32[]{:S(2)}, u32[]{:S(2)}) collective-permute-start(bf16[144,256]{1,0:T(8,128)(2,1)S(1)} %get-tuple-element.14), channel_id=1, source_target_pairs={{4,8},{8,4},{12,16},{16,12},{20,24},{24,20},{28,0},{0,28},{5,9},{9... | collective-permute-start | bytes 221192 | tf_op jit(solution)/shard_map/ppermute | solution.py:497
  23.1 1.7 %collective-permute-done.1.refs_5_ = bf16[144,256]{1,0:T(8,128)(2,1)S(1)} collective-permute-done((bf16[144,256]{1,0:T(8,128)(2,1)S(1)}, bf16[144,256]{1,0:T(8,128)(2,1)S(1)}, u32[]{:S(2)}, u32[]{:S(2)}) %collective-permute-start.1) | collective-permute-done | bytes 73760 | tf_op jit(solution)/shard_map/ppermute | solution.py:496
  24.8 5.8 %collective-permute-done.2.refs_6_ = bf16[144,256]{1,0:T(8,128)(2,1)S(1)} collective-permute-done((bf16[144,256]{1,0:T(8,128)(2,1)S(1)}, bf16[144,256]{1,0:T(8,128)(2,1)S(1)}, u32[]{:S(2)}, u32[]{:S(2)}) %collective-permute-start.2) | collective-permute-done | bytes 73760 | tf_op jit(solution)/shard_map/ppermute | solution.py:497
  30.6 0.0 all-to-all-done
  30.6 0.0 copy-start.5
  30.6 0.0 copy-done.1
  30.6 0.6 %copy-done.5 = s32[1,16]{1,0:T(1,128)S(1)} copy-done((s32[1,16]{1,0:T(1,128)S(1)}, s32[1,16]{1,0:T(1,128)}, u32[]{:S(2)}) %copy-start.5) | copy-done | bytes 88
  31.2 8.7 %shard_map.98 = (f32[3,16,16,256]{3,2,1,0:T(8,128)}, f32[10,4096]{1,0:T(8,128)}) custom-call(s32[1,16]{1,0:T(1,128)S(1)} %copy-done.5, f32[3,16,16,256]{3,2,1,0:T(8,128)S(1)} %copy-done.1, f32[16,16,256]{2,1,0:T(8,128)S(1)} %copy-done.3, f32[2,24,256]{2,1,0:T(8,128)S(1)} %get-tuple-element.11.refs_3_, f32[64,8,256]{2,1,0:T(8,128)S(1)} %get-tuple-element.12.refs_4_, ...), custom_call_target="tpu_custom_call" | custom-call | flops 16777216 | bytes 4194304 | tf_op jit(solution)/shard_map/pallas_call | solution.py:37
Async XLA Ops:
  0.6 1.1 %copy-start = (f32[3,16,16,256]{3,2,1,0:T(8,128)S(1)}, f32[3,16,16,256]{3,2,1,0:T(8,128)}, u32[]{:S(2)}) copy-start(f32[3,16,16,256]{3,2,1,0:T(8,128)} %refs_1_.3) | copy-start | bytes 2359300
  1.8 0.9 %copy-start.2 = (f32[16,16,256]{2,1,0:T(8,128)S(1)}, f32[16,16,256]{2,1,0:T(8,128)}, u32[]{:S(2)}) copy-start(f32[16,16,256]{2,1,0:T(8,128)} %refs_2_.3) | copy-start | bytes 786436
  2.7 0.7 %copy-start.4 = (bf16[16,2,256]{2,1,0:T(2,128)(2,1)S(1)}, bf16[16,2,256]{2,1,0:T(2,128)(2,1)}, u32[]{:S(2)}) copy-start(bf16[16,2,256]{2,1,0:T(2,128)(2,1)} %refs_2_.2) | copy-start | bytes 49156
  3.4 3.1 %copy-start.8 = (s32[2048]{0:T(1024)S(1)}, s32[2048]{0:T(1024)}, u32[]{:S(2)}) copy-start(s32[2048]{0:T(1024)} %param.13) | copy-start | bytes 24580
  3.4 3.2 %copy-start.9 = (s32[2048,1]{0,1:T(1,128)S(1)}, s32[2048,1]{0,1:T(1,128)}, u32[]{:S(2)}) copy-start(s32[2048,1]{0,1:T(1,128)} %param.14) | copy-start | bytes 24580
  3.6 5.5 %collective-permute-start = (bf16[160,256]{1,0:T(8,128)(2,1)S(1)}, bf16[160,256]{1,0:T(8,128)(2,1)S(1)}, u32[]{:S(2)}, u32[]{:S(2)}) collective-permute-start(bf16[160,256]{1,0:T(8,128)(2,1)S(1)} %shard_map.96), channel_id=1, source_target_pairs={{0,2},{2,0},{1,3},{3,1},{4,6},{6,4},{5,7},{7,5},{8,10},{10,8},{9,1... | collective-permute-start | bytes 245768 | tf_op jit(solution)/shard_map/ppermute | solution.py:431
  6.6 2.4 %copy-start.3 = (f32[16,16,256]{2,1,0:T(8,128)S(1)}, f32[16,16,256]{2,1,0:T(8,128)}, u32[]{:S(2)}) copy-start(f32[16,16,256]{2,1,0:T(8,128)} %refs_2_.3) | copy-start | bytes 786436
  6.6 2.4 %copy-start.6 = (f32[10,2048]{1,0:T(8,128)S(1)}, f32[10,2048]{1,0:T(8,128)}, u32[]{:S(2)}) copy-start(f32[10,2048]{1,0:T(8,128)} %refs_4_.1) | copy-start | bytes 245764
  6.6 2.4 %copy-start.7 = (bf16[32,32]{1,0:T(8,128)(2,1)S(1)}, bf16[32,32]{1,0:T(8,128)(2,1)}, u32[]{:S(2)}) copy-start(bf16[32,32]{1,0:T(8,128)(2,1)} %refs_3_.1) | copy-start | bytes 6148
  9.0 21.5 %copy-start.1 = (f32[3,16,16,256]{3,2,1,0:T(8,128)S(1)}, f32[3,16,16,256]{3,2,1,0:T(8,128)}, u32[]{:S(2)}) copy-start(f32[3,16,16,256]{3,2,1,0:T(8,128)} %refs_1_.3) | copy-start | bytes 2359300
  11.5 19.1 %all-to-all-start = ((f32[16,40,128]{2,1,0:T(8,128)}), f32[16,40,128]{2,1,0:T(8,128)S(1)}, u32[]{:S(2)}, u32[]{:S(2)}) async-start(f32[16,40,128]{2,1,0:T(8,128)} %bitcast.2), calls=%async_computation | async-start | bytes 655360 | tf_op jit(solution)/shard_map/all_to_all | solution.py:491
  17.9 6.9 %collective-permute-start.1 = (bf16[144,256]{1,0:T(8,128)(2,1)S(1)}, bf16[144,256]{1,0:T(8,128)(2,1)S(1)}, u32[]{:S(2)}, u32[]{:S(2)}) collective-permute-start(bf16[144,256]{1,0:T(8,128)(2,1)S(1)} %get-tuple-element.13), channel_id=1, source_target_pairs={{0,4},{4,0},{8,12},{12,8},{16,20},{20,16},{24,28},{28,24},{1,5},{5... | collective-permute-start | bytes 221192 | tf_op jit(solution)/shard_map/ppermute | solution.py:496
  19.8 10.8 %collective-permute-start.2 = (bf16[144,256]{1,0:T(8,128)(2,1)S(1)}, bf16[144,256]{1,0:T(8,128)(2,1)S(1)}, u32[]{:S(2)}, u32[]{:S(2)}) collective-permute-start(bf16[144,256]{1,0:T(8,128)(2,1)S(1)} %get-tuple-element.14), channel_id=1, source_target_pairs={{4,8},{8,4},{12,16},{16,12},{20,24},{24,20},{28,0},{0,28},{5,9},{9... | collective-permute-start | bytes 221192 | tf_op jit(solution)/shard_map/ppermute | solution.py:497
  30.6 0.7 %copy-start.5 = (s32[1,16]{1,0:T(1,128)S(1)}, s32[1,16]{1,0:T(1,128)}, u32[]{:S(2)}) copy-start(s32[1,16]{1,0:T(1,128)} %refs_0_.5) | copy-start | bytes 196

commit v2 on v1

v2 whole, which is shorter than its diff:
```python
import jax
import jax.numpy as jnp
from jax import lax
from jax.experimental import pallas as pl
from jax.experimental.pallas import tpu as pltpu
from jax.sharding import PartitionSpec as P

SUB = 2
TIME_STEP = 0.9
AXIAL_SPEED = 0.15
PITCH_SPEED = 0.15
LANES = 128
EXTRA = 8
SLAB = 32
F32 = jnp.float32
BF16 = jnp.bfloat16
VMEM = pl.BlockSpec(memory_space=pltpu.VMEM)
ANY = pl.BlockSpec(memory_space=pl.ANY)
HBM = pl.BlockSpec(memory_space=pltpu.HBM)
VMEM_LIMIT = 48 * 1024 * 1024


def iota(shape, dim):
    return lax.broadcasted_iota(jnp.int32, shape, dim)


def split(x):
    high = x.astype(BF16)
    return high, (x - high.astype(F32)).astype(BF16)


def power(n):
    assert n & (n - 1) == 0
    return n.bit_length() - 1


def call(body, outs, args, specs, scratch=(), flops=0, nbytes=0, place=VMEM):
    return pl.pallas_call(
        body,
        out_shape=tuple(jax.ShapeDtypeStruct(s, d) for s, d in outs),
        in_specs=list(specs),
        out_specs=tuple(place for _ in outs),
        scratch_shapes=list(scratch),
        compiler_params=pltpu.CompilerParams(vmem_limit_bytes=VMEM_LIMIT),
        cost_estimate=pl.CostEstimate(flops=flops, bytes_accessed=nbytes, transcendentals=0),
    )(*args)


def pack_span(nspan, f_ref, k_ref, m_ref, *refs):
    radial, axial = f_ref.shape[2:]
    *outs, f_s, k_s, m_s, sems = refs
    s = lax.axis_index("span")
    copies = [pltpu.make_async_copy(m_ref, m_s, sems.at[0])]
    sides = 1 if nspan == 2 else 2
    for n in range(sides):
        first = (1 - s if nspan == 2 else 1 - n) * (radial - 8)
        rows = pl.ds(pl.multiple_of(first, 8), 8)
        copies.append(pltpu.make_async_copy(f_ref.at[:, :, rows, :], f_s.at[n], sems.at[1 + 2 * n]))
        copies.append(pltpu.make_async_copy(k_ref.at[:, rows, :], k_s.at[n], sems.at[2 + 2 * n]))
    for copy in copies:
        copy.start()
    for copy in copies:
        copy.wait()

    def edge(n, rows):
        parts = []
        for r in rows:
            parts += [f_s[n, :, :, r, :].reshape(-1, axial), k_s[n, :, r, :]]
        return jnp.concatenate(parts, 0)

    flow = m_s[...].astype(F32)
    flow = jnp.concatenate([flow[:, 0, :], flow[:, 1, :]], 0).astype(BF16)
    if nspan == 2:
        packed = jnp.where(s == 0, edge(0, (6, 7)), edge(0, (0, 1)))
        outs[0][: packed.shape[0]] = packed.astype(BF16)
        outs[0][packed.shape[0] :] = flow
    else:
        outs[0][...] = edge(0, (6, 7)).astype(BF16)
        outs[1][...] = edge(1, (0, 1)).astype(BF16)
        outs[2][...] = flow


def sample_fields(npitch, f_ref, cell_ref, dest_ref, samp_ref, slot_ref):
    nfield, pitch, radial, axial = f_ref.shape
    lines = pitch * radial
    chunks = cell_ref.shape[0]
    table = f_ref[...].reshape(nfield * lines, axial)
    high, low = split(table)
    samp_ref[...] = jnp.zeros(samp_ref.shape, F32)
    for c in range(0, chunks, 2):
        cells = jnp.concatenate([cell_ref[c : c + 1, :], cell_ref[c + 1 : c + 2, :]], 1)
        width = cells.shape[1]
        lane = cells & (axial - 1)
        line = lax.shift_right_logical(cells, power(axial))
        pick = (iota((axial, width), 0) == lane).astype(F32).astype(BF16)
        got = jnp.dot(high, pick, preferred_element_type=F32) + jnp.dot(
            low, pick, preferred_element_type=F32
        )
        mine = iota((lines, width), 0) == line
        for f in range(nfield):
            part = jnp.where(mine, got[f * lines : (f + 1) * lines], 0.0)
            samp_ref[f : f + 1, c * LANES : c * LANES + width] = jnp.sum(part, 0, keepdims=True)
    ones = []
    for c in range(chunks):
        ones.append((iota((npitch, LANES), 0) == dest_ref[c : c + 1, :]).astype(F32))
    stacked = jnp.concatenate(ones, 0)
    before = (iota((LANES, LANES), 0) < iota((LANES, LANES), 1)).astype(F32).astype(BF16)
    prefix = jnp.dot(stacked.astype(BF16), before, preferred_element_type=F32)
    carry = jnp.zeros((npitch, 1), F32)
    for c in range(chunks):
        rank = prefix[c * npitch : (c + 1) * npitch] + carry
        slot = jnp.sum(rank * ones[c], 0, keepdims=True)
        slot_ref[:, c * LANES : (c + 1) * LANES] = slot.astype(jnp.int32)
        carry = carry + jnp.sum(ones[c], 1, keepdims=True)


def slab(core, extra):
    return [extra, core, extra]


def near(stator, parts):
    turned = jnp.concatenate(parts, 0).T
    return (
        jnp.where(stator, turned[LANES - 1 : LANES], turned[0:1]),
        jnp.where(stator, turned[LANES - 2 : LANES - 1], turned[1:2]),
    )


def dispatch(
    npitch,
    nspan,
    f_ref,
    k_ref,
    m_ref,
    kern_ref,
    tv_ref,
    cell_ref,
    dest_ref,
    samp_ref,
    slot_ref,
    map_ref,
    *refs,
):
    nfield, pitch, radial, axial = f_ref.shape
    planes = nfield + 1
    edge = planes * pitch
    if nspan == 2:
        (got_ref,) = refs[:1]
        refs = refs[1:]
        low_ref = high_ref = got_ref
    else:
        low_ref, high_ref, all_ref = refs[:3]
        refs = refs[3:]
    buf_ref, a_ref, b_ref, speed_ref, halo_ref, face_ref, kern_s, upd_s, lhs_s, face_s = refs
    s = lax.axis_index("span")
    q = lax.axis_index("row")
    even = lax.rem(lax.axis_index("pitch"), 2) == 0

    total = kern_ref.shape[0]
    kern_s[...] = kern_ref[...].astype(F32)
    main = kern_s[pl.ds(pl.multiple_of(s * radial, 8), radial), :]
    above = kern_s[pl.ds(pl.multiple_of(jnp.minimum((s + 1) * radial, total - 8), 8), 8), :]
    below = kern_s[pl.ds(pl.multiple_of(jnp.maximum(s * radial - 8, 0), 8), 8), :]
    wide = jnp.concatenate([main, jnp.where(iota((EXTRA, total), 0) < 4, above, below)], 0).astype(BF16)
    smoothed = []
    flow = m_ref[...].astype(F32)
    for c in range(2):
        if nspan == 2:
            own = flow[:, c, :]
            other = got_ref[2 * edge + c * radial : 2 * edge + (c + 1) * radial, :].astype(F32)
            rows = [jnp.where(s == 0, own, other), jnp.where(s == 0, other, own)]
        else:
            rows = [all_ref[n, c * radial : (c + 1) * radial, :].astype(F32) for n in range(nspan)]
        smoothed.append(
            jnp.dot(wide, jnp.concatenate(rows, 0).astype(BF16), preferred_element_type=F32)
        )
    sa = AXIAL_SPEED * (1.0 + 0.5 * jnp.tanh(smoothed[0]))
    sp = PITCH_SPEED * jnp.tanh(smoothed[1])
    speed_ref[0] = sa
    speed_ref[1] = sp

    chunks = cell_ref.shape[0]
    high, low = split(jnp.concatenate([sa[:radial], sp[:radial]], 0))
    upd_s[...] = jnp.zeros(upd_s.shape, F32)
    for c in range(0, chunks, 2):
        cells = jnp.concatenate([cell_ref[c : c + 1, :], cell_ref[c + 1 : c + 2, :]], 1)
        width = cells.shape[1]
        span = slice(c * LANES, c * LANES + width)
        lane = cells & (axial - 1)
        line = lax.shift_right_logical(cells, power(axial)) & (radial - 1)
        pick = (iota((axial, width), 0) == lane).astype(F32).astype(BF16)
        got = jnp.dot(high, pick, preferred_element_type=F32) + jnp.dot(
            low, pick, preferred_element_type=F32
        )
        mine = iota((radial, width), 0) == line
        sampled = [samp_ref[f : f + 1, span] for f in range(nfield)]
        for n in range(2):
            part = jnp.where(mine, got[n * radial : (n + 1) * radial], 0.0)
            sampled.append(jnp.sum(part, 0, keepdims=True))
        count = len(sampled)
        for v, value in enumerate(sampled):
            head = tv_ref[v : v + 1, span]
            upd_s[v : v + 1, span] = head + 0.5 * (value - head)
            upd_s[count + v : count + v + 1, span] = tv_ref[count + v : count + v + 1, span] + 0.8 * value

    values = tv_ref.shape[0]
    tracers = tv_ref.shape[1]
    capacity = 2 * tracers // npitch
    pad = upd_s.shape[0]
    both = upd_s[...]
    rounded = both.astype(BF16).astype(F32)
    both = jnp.concatenate([rounded, both - rounded], 0)
    dest = jnp.concatenate([dest_ref[c : c + 1, :] for c in range(chunks)], 1)
    for d in range(npitch):
        lhs_s[d * 2 * pad : (d + 1) * 2 * pad, :] = jnp.where(dest == d, both, 0.0).astype(BF16)
    place = (iota((capacity, tracers), 0) == slot_ref[...]).astype(F32).astype(BF16)
    out = lax.dot_general(
        lhs_s[...], place, (((1,), (1,)), ((), ())), preferred_element_type=F32
    )
    for d in range(npitch):
        both = out[d * 2 * pad : (d + 1) * 2 * pad]
        mine = both[:pad] + both[pad:]
        for j in range(capacity // LANES):
            buf_ref[d, q, j * values : (j + 1) * values, :] = mine[
                :values, j * LANES : (j + 1) * LANES
            ]

    sub = iota((EXTRA, axial), 0)
    up0, up1 = high_ref[:edge].astype(F32), high_ref[edge : 2 * edge].astype(F32)
    dn0, dn1 = low_ref[:edge].astype(F32), low_ref[edge : 2 * edge].astype(F32)
    for n in range(edge):
        tile = jnp.where(sub == 0, up0[n : n + 1], 0.0)
        tile = jnp.where(sub == 1, up1[n : n + 1], tile)
        tile = jnp.where(sub == 6, dn0[n : n + 1], tile)
        halo_ref[n] = jnp.where(sub == 7, dn1[n : n + 1], tile)

    stator = q == 0
    tile = pl.ds(pl.multiple_of((1 - q) * (axial - LANES), LANES), LANES)
    face_s[...] = jnp.zeros(face_s.shape, F32)

    for i in range(pitch):
        parts = []
        for f in range(planes):
            core = f_ref[f, i, :, tile] if f < nfield else k_ref[i, :, tile]
            parts += slab(core, halo_ref[f * pitch + i, :, tile])
        first, second = near(stator, parts)
        face_s[i : i + 1] = first
        face_s[pitch + i : pitch + i + 1] = second
    for n in range(2):
        speed = speed_ref[n, :, tile]
        first, second = near(stator, slab(speed[:radial], speed[radial:]) * planes)
        at = 2 * pitch + 2 * n
        face_s[at : at + 1] = first
        face_s[at + 1 : at + 2] = second
    face = face_s[...]
    face_ref[...] = face
    first = map_ref[...].astype(F32)
    face_ref[2 * pitch + 3 : 2 * pitch + 4] = jnp.broadcast_to(first[:, :1], (1, LANES))
    for d in range(npitch):
        buf_ref[d, 1 - q] = face

    def layers(indices, nearest):
        rows = []
        for f in range(planes):
            for i in indices:
                rows.append(f_ref[f, i] if f < nfield else k_ref[i])
        for f in range(planes):
            corner = halo_ref[f * pitch + nearest]
            rows += [corner[0:1], corner[7:8]]
        rows.append(jnp.zeros((8, axial), F32))
        return jnp.concatenate(rows, 0)

    top = layers((pitch - 2, pitch - 1), pitch - 1)
    bottom = layers((0, 1), 0)
    a_ref[...] = jnp.where(even, top, bottom).astype(BF16)
    b_ref[...] = jnp.where(even, bottom, top).astype(BF16)


class Faces:
    def __init__(self, nspan, speed_ref, radial):
        self.rows, self.lanes = speed_ref.shape[1:]
        shape = (self.rows, self.lanes)
        s = lax.axis_index("span")
        stator = lax.axis_index("row") == 0
        lane, radius = iota(shape, 1), iota(shape, 0)
        sa = TIME_STEP * speed_ref[0]
        sp = TIME_STEP * speed_ref[1]
        wa = 0.5 * (sa + pltpu.roll(sa, self.lanes - 1, 1))
        self.last = lane == self.lanes - 1
        self.wa_up, self.wa_dn = jnp.maximum(wa, 0.0), jnp.minimum(wa, 0.0)
        self.wp_up, self.wp_dn = jnp.maximum(sp, 0.0), jnp.minimum(sp, 0.0)
        self.wall = ((radius == radial - 1) & (s == nspan - 1)) | (
            (radius == self.rows - 1) & (s == 0)
        )
        inlet = jnp.where(stator & (lane == 0), sa, 0.0)
        self.keep = 1.0 + inlet - jnp.where(jnp.logical_not(stator) & self.last, sa, 0.0)
        self.half = 0.5 * TIME_STEP

    def plane(self, k):
        kappa = self.half * (k + pltpu.roll(k, self.lanes - 1, 1))
        aa = jnp.where(self.last, 0.0, self.wa_up + kappa)
        ab = jnp.where(self.last, 0.0, self.wa_dn - kappa)
        kr = jnp.where(self.wall, 0.0, self.half * (k + pltpu.roll(k, self.rows - 1, 0)))
        return aa, ab, kr

    def pitch(self, k, k_next):
        kappa = self.half * (k + k_next)
        return self.wp_up + kappa, self.wp_dn - kappa

    def step(self, v, coefficients, flux_up, flux_dn):
        aa, ab, kr = coefficients
        along = aa * v + ab * pltpu.roll(v, self.lanes - 1, 1)
        radial = kr * (v - pltpu.roll(v, self.rows - 1, 0))
        change = along - pltpu.roll(along, 1, 1) + radial - pltpu.roll(radial, 1, 0)
        return self.keep * v - (change + (flux_up - flux_dn))


def middle(nspan, f_ref, k_ref, speed_ref, halo_ref, o_ref, y4_ref, row_ref, y_s, c_s, p_s):
    nfield, pitch, radial, axial = f_ref.shape
    stator = lax.axis_index("row") == 0
    faces = Faces(nspan, speed_ref, radial)

    def state(f, i):
        return jnp.concatenate([f_ref[f, i], halo_ref[f * pitch + i]], 0)

    def kappa(i):
        return jnp.concatenate([k_ref[i], halo_ref[nfield * pitch + i]], 0)

    pa, pb = faces.pitch(kappa(0), kappa(1))
    for f in range(nfield):
        p_s[f] = pa * state(f, 0) + pb * state(f, 1)

    @pl.loop(1, pitch - 1)
    def _(i):
        k = kappa(i)
        plane = faces.plane(k)
        pa, pb = faces.pitch(k, kappa(i + 1))
        for n, value in enumerate((*plane, pa, pb)):
            c_s[n, i] = value
        for f in range(nfield):
            v = state(f, i)
            flux = pa * v + pb * state(f, i + 1)
            y_s[f, i] = faces.step(v, plane, flux, p_s[f])
            p_s[f] = flux

    for f in range(nfield):
        p_s[f] = c_s[3, 1] * y_s[f, 1] + c_s[4, 1] * y_s[f, 2]

    @pl.loop(2, pitch - 2)
    def _(i):
        aa, ab, kr, pa, pb = [c_s[n, i] for n in range(5)]
        for f in range(nfield):
            v = y_s[f, i]
            flux = pa * v + pb * y_s[f, i + 1]
            o_ref[f, i - 2] = faces.step(v, (aa, ab, kr), flux, p_s[f])[:radial]
            p_s[f] = flux

    for f in range(nfield):
        for n, i in enumerate((1, 2, pitch - 3, pitch - 2)):
            y4_ref[f, n] = y_s[f, i]
    row_ref[...] = jnp.zeros(row_ref.shape, F32)
    tile = pl.ds(pl.multiple_of(lax.axis_index("row") * (LANES - axial) + axial - LANES, LANES), LANES)
    blank = jnp.zeros((SLAB, LANES), F32)
    for i in range(1, pitch - 1):
        parts = []
        for f in range(nfield):
            parts += slab(y_s[f, i, :radial, tile], y_s[f, i, radial:, tile])
        row_ref[i : i + 1] = near(stator, parts + [blank])[0]


def edges(
    nspan, f_ref, k_ref, speed_ref, halo_ref, a_ref, b_ref, y4_ref, row_ref, o_ref, row_out, beyond_ref, y_s
):
    nfield, pitch, radial, axial = f_ref.shape
    planes = nfield + 1
    stator = lax.axis_index("row") == 0
    even = lax.rem(lax.axis_index("pitch"), 2) == 0
    faces = Faces(nspan, speed_ref, radial)
    ext = {
        -1: jnp.where(even, b_ref[...].astype(F32), a_ref[...].astype(F32)),
        1: jnp.where(even, a_ref[...].astype(F32), b_ref[...].astype(F32)),
    }
    sub = iota((EXTRA, axial), 0)
    corner_at = 2 * planes * radial

    def state(f, i):
        if 0 <= i < pitch:
            core = f_ref[f, i] if f < nfield else k_ref[i]
            return jnp.concatenate([core, halo_ref[f * pitch + i]], 0)
        side = ext[-1 if i < 0 else 1]
        at = (2 * f + (i + 2 if i < 0 else i - pitch)) * radial
        extra = jnp.zeros((EXTRA, axial), F32)
        if i in (-1, pitch):
            corner = corner_at + 2 * f
            extra = jnp.where(sub == 0, side[corner : corner + 1], 0.0)
            extra = jnp.where(sub == 7, side[corner + 1 : corner + 2], extra)
        return jnp.concatenate([side[at : at + radial], extra], 0)

    row_out[...] = row_ref[...]
    beyond_ref[...] = jnp.zeros(beyond_ref.shape, F32)
    tile = pl.ds(pl.multiple_of(lax.axis_index("row") * (LANES - axial) + axial - LANES, LANES), LANES)

    def edge_lanes(value):
        return jnp.where(stator, value[:, axial - LANES :], value[:, :LANES])

    blank = jnp.zeros((SLAB, LANES), F32)
    for side, new, done in ((0, (-1, 0), (0, 1)), (1, (pitch - 1, pitch), (pitch - 2, pitch - 1))):
        k = {i: state(nfield, i) for i in range(new[0] - 1, new[1] + 2)}
        low = min(new[0] - 1, done[0] - 1)
        top = max(new[1] + 1, done[1] + 1)
        k = {i: state(nfield, i) for i in range(low, top + 1)}
        along = {i: faces.pitch(k[i], k[i + 1]) for i in range(low, top)}
        plane = {i: faces.plane(k[i]) for i in sorted({*new, *done})}
        held = {}
        for n, i in enumerate((1, 2, pitch - 3, pitch - 2)):
            held[i] = n
        for f in range(nfield):
            x = {i: state(f, i) for i in range(new[0] - 1, new[1] + 2)}
            flux = {i: along[i][0] * x[i] + along[i][1] * x[i + 1] for i in range(new[0] - 1, new[1] + 1)}
            y = {i: y4_ref[f, held[i]] for i in held if done[0] - 1 <= i <= done[1] + 1}
            for i in new:
                y[i] = faces.step(x[i], plane[i], flux[i], flux[i - 1])
            flux = {i: along[i][0] * y[i] + along[i][1] * y[i + 1] for i in range(done[0] - 1, done[1] + 1)}
            for n, i in enumerate(done):
                o_ref[f, 2 * side + n] = faces.step(y[i], plane[i], flux[i], flux[i - 1])[:radial]
            y_s[f] = y[0 if side == 0 else pitch - 1]
        parts = []
        for f in range(nfield):
            parts += slab(y_s[f, :radial, tile], y_s[f, radial:, tile])
        i = 0 if side == 0 else pitch - 1
        row_out[i : i + 1] = near(stator, parts + [blank])[0]
        parts = []
        for f in range(planes):
            value = edge_lanes(state(f, -1 if side == 0 else pitch))
            parts += slab(value[:radial], value[radial:])
        beyond_ref[side : side + 1] = near(stator, parts)[0]


def interface(
    npitch,
    nspan,
    mid_ref,
    edge_ref,
    face_ref,
    row_ref,
    beyond_ref,
    buf_ref,
    o_ref,
    arr_ref,
    arr_s,
    tile_s,
    ring_s,
    sems,
):
    nfield, pitch, radial, axial = o_ref.shape
    planes = nfield + 1
    s = lax.axis_index("span")
    q = lax.axis_index("row")
    stator = q == 0
    near_tile = pl.ds(pl.multiple_of((1 - q) * (axial - LANES), LANES), LANES)
    copies = []
    if axial > LANES:
        rest = pl.ds(pl.multiple_of(q * LANES, LANES), axial - LANES)
        copies += [
            pltpu.make_async_copy(
                mid_ref.at[:, :, :, rest], o_ref.at[:, 2 : pitch - 2, :, rest], sems.at[0]
            ),
            pltpu.make_async_copy(
                edge_ref.at[:, :2, :, rest], o_ref.at[:, :2, :, rest], sems.at[1]
            ),
            pltpu.make_async_copy(
                edge_ref.at[:, 2:, :, rest], o_ref.at[:, pitch - 2 :, :, rest], sems.at[2]
            ),
        ]
    for copy in copies:
        copy.start()

    values = arr_ref.shape[0]
    capacity = arr_ref.shape[1] // npitch
    for p in range(npitch):
        for j in range(capacity // LANES):
            at = p * capacity + j * LANES
            arr_s[:, at : at + LANES] = buf_ref[p, q, j * values : (j + 1) * values, :]
    copies.append(pltpu.make_async_copy(arr_s, arr_ref, sems.at[3]))
    copies[-1].start()

    whole = npitch * pitch
    count = pitch + 8
    for p in range(npitch):
        ring_s[0, p * pitch : (p + 1) * pitch] = buf_ref[p, 1 - q, :pitch, :]
        ring_s[1, p * pitch : (p + 1) * pitch] = buf_ref[p, 1 - q, pitch : 2 * pitch, :]
    for n in range(2):
        ring_s[n, whole : whole + pitch] = ring_s[n, :pitch]
        ring_s[n, whole + pitch :] = ring_s[n, pitch : pitch + 8]
    begin = jnp.max(face_ref[2 * pitch + 3 : 2 * pitch + 4]).astype(jnp.int32) - 1
    begin = jnp.where(begin < 0, begin + whole, begin)
    ghost = ring_s[0, pl.ds(begin, count), :]
    farther = ring_s[1, pl.ds(begin, count), :]
    tail = jnp.zeros((count - pitch - 2, LANES), F32)
    own = jnp.concatenate(
        [beyond_ref[0:1], face_ref[:pitch], beyond_ref[1:2], tail], 0
    )
    top = jnp.zeros((1, LANES), F32)
    own_k1 = jnp.concatenate([top, face_ref[pitch : 2 * pitch], top, tail], 0)
    own_new = jnp.concatenate([top, row_ref[...], top, tail], 0)
    at = 2 * pitch
    sa0, sa1, sp0 = [TIME_STEP * face_ref[at + n : at + n + 1] for n in range(3)]
    ga0, ga1, gp0 = [TIME_STEP * buf_ref[0, 1 - q, at + n : at + n + 1, :] for n in range(3)]
    shape = (count, LANES)
    lane = iota(shape, 1)
    group = lax.shift_right_logical(lane, power(SLAB))
    radius = lane & (SLAB - 1)

    def spread(x):
        out = x
        for f in range(nfield):
            out = jnp.where(group == f, pltpu.roll(x, (f + 1) * SLAB, 1), out)
        return out

    half = 0.5 * TIME_STEP
    k0, k1, g0, g1 = spread(own), spread(own_k1), spread(ghost), spread(farther)
    wall = ((radius == 7 + radial) & (s == nspan - 1)) | ((radius == 7) & (s == 0))

    def ahead(x):
        return pltpu.roll(x, count - 1, 0)

    def outward(x):
        return pltpu.roll(x, LANES - 1, 1)

    def change(v, k, speed):
        kappa = half * (k + ahead(k))
        up, dn = jnp.maximum(speed, 0.0), jnp.minimum(speed, 0.0)
        along = (up + kappa) * v + (dn - kappa) * ahead(v)
        kappa = jnp.where(wall, 0.0, half * (k + outward(k)))
        across = kappa * (v - outward(v))
        return along - pltpu.roll(along, 1, 0) + across - pltpu.roll(across, 1, 1)

    def face(first, second, speed, kappa):
        lower = jnp.where(stator, first, second)
        upper = jnp.where(stator, second, first)
        return (jnp.maximum(speed, 0.0) + kappa) * lower + (jnp.minimum(speed, 0.0) - kappa) * upper

    sign = jnp.where(stator, 1.0, -1.0)
    speed = 0.5 * (sa0 + ga0)
    kappa = half * (k0 + g0)
    flux = sign * face(own, ghost, speed, kappa)
    shift = -flux
    ghost_new = (
        ghost
        + flux
        - sign * face(ghost, farther, 0.5 * (ga0 + ga1), half * (g0 + g1))
        - change(ghost, g0, gp0)
    )
    flux = sign * face(own_new + shift, ghost_new, speed, kappa)
    inner = 0.5 * (sa0 + sa1)
    kappa = half * (k0 + k1)
    inner = sign * jnp.where(
        stator, jnp.minimum(inner, 0.0) - kappa, jnp.maximum(inner, 0.0) + kappa
    ) * shift
    add0 = shift - change(shift, k0, sp0) + inner - flux
    add1 = -inner

    row = iota((LANES, LANES), 0)
    near_row = jnp.where(stator, LANES - 1, 0)
    far_row = jnp.where(stator, LANES - 2, 1)
    for i in range(pitch):
        block = jnp.where(
            row == near_row,
            add0[i + 1 : i + 2],
            jnp.where(row == far_row, add1[i + 1 : i + 2], 0.0),
        ).T
        for f in range(nfield):
            if 2 <= i < pitch - 2:
                old = mid_ref[f, i - 2, :, near_tile]
            else:
                old = edge_ref[f, i if i < 2 else i - pitch + 4, :, near_tile]
            tile_s[f, i] = old + block[f * SLAB + 8 : f * SLAB + 8 + radial]
    copies.append(pltpu.make_async_copy(tile_s, o_ref.at[:, :, :, near_tile], sems.at[4]))
    copies[-1].start()
    for copy in copies:
        copy.wait()


def local(
    fields,
    diffusivity,
    mean_flow,
    radial_kernel,
    tracer_values,
    tracer_cells,
    tracer_dest,
    interface_map,
):
    npitch = lax.axis_size("pitch")
    nspan = lax.axis_size("span")
    nfield, pitch, radial, axial = fields.shape
    planes = nfield + 1
    values, tracers = tracer_values.shape
    chunks = tracers // LANES
    capacity = 2 * tracers // npitch
    edge = planes * pitch
    cells = tracer_cells.reshape(chunks, LANES)
    dest = tracer_dest.reshape(chunks, LANES)

    mean_rows = 2 * radial
    sides = 1 if nspan == 2 else 2
    if nspan == 2:
        outs = [((2 * edge + mean_rows, axial), BF16)]
    else:
        outs = [((2 * edge, axial), BF16)] * 2 + [((mean_rows, axial), BF16)]
    packed = call(
        lambda *refs: pack_span(nspan, *refs),
        outs,
        [pltpu.with_memory_space_constraint(x, pltpu.HBM) for x in (fields, diffusivity, mean_flow)],
        [HBM] * 3,
        [
            pltpu.VMEM((sides, nfield, pitch, 8, axial), F32),
            pltpu.VMEM((sides, pitch, 8, axial), F32),
            pltpu.VMEM(mean_flow.shape, mean_flow.dtype),
            pltpu.SemaphoreType.DMA((1 + 2 * sides,)),
        ],
        nbytes=2**20,
    )
    if nspan == 2:
        span_got = (lax.ppermute(packed[0], "span", [(0, 1), (1, 0)]),)
    else:
        span_got = (
            lax.ppermute(packed[0], "span", [(n, n + 1) for n in range(nspan - 1)]),
            lax.ppermute(packed[1], "span", [(n + 1, n) for n in range(nspan - 1)]),
            lax.all_gather(packed[2], "span"),
        )

    samp, slot = call(
        lambda *refs: sample_fields(npitch, *refs),
        [((8, tracers), F32), ((1, tracers), jnp.int32)],
        (fields, cells, dest),
        [VMEM] * 3,
        flops=4 * nfield * pitch * radial * axial * tracers,
        nbytes=2**20,
    )

    rows = radial + EXTRA
    per_slot = max(values * capacity // LANES, 2 * pitch + 4)
    per_slot = -(-per_slot // 8) * 8
    halo_rows = 2 * planes * radial + 16
    pad = 16
    buf, a_send, b_send, speeds, halo, face = call(
        lambda *refs: dispatch(npitch, nspan, *refs),
        [
            ((npitch, 2, per_slot, LANES), F32),
            ((halo_rows, axial), BF16),
            ((halo_rows, axial), BF16),
            ((2, rows, axial), F32),
            ((edge, EXTRA, axial), F32),
            ((per_slot, LANES), F32),
        ],
        (
            fields,
            diffusivity,
            mean_flow,
            radial_kernel,
            tracer_values,
            cells,
            dest,
            samp,
            slot,
            interface_map,
        )
        + span_got,
        [VMEM] * (10 + len(span_got)),
        [
            pltpu.VMEM(radial_kernel.shape, F32),
            pltpu.VMEM((pad, tracers), F32),
            pltpu.VMEM((npitch * 2 * pad, tracers), BF16),
            pltpu.VMEM((per_slot, LANES), F32),
        ],
        flops=2 * npitch * 2 * pad * tracers * capacity,
        nbytes=2**21,
    )
    buf = lax.all_to_all(
        buf.reshape(npitch * 2, per_slot, LANES), ("pitch", "row"), 0, 0
    ).reshape(buf.shape)
    swap = [(n, n ^ 1) for n in range(npitch)]
    turn = [((n + 1) % npitch, ((n ^ 1) + 1) % npitch) for n in range(npitch)]
    a_got = lax.ppermute(a_send, "pitch", swap)
    b_got = lax.ppermute(b_send, "pitch", turn)

    mid, near_edge, new_rows = call(
        lambda *refs: middle(nspan, *refs),
        [
            ((nfield, pitch - 4, radial, axial), F32),
            ((nfield, 4, rows, axial), F32),
            ((pitch, LANES), F32),
        ],
        (fields, diffusivity, speeds, halo),
        [VMEM] * 4,
        [
            pltpu.VMEM((nfield, pitch, rows, axial), F32),
            pltpu.VMEM((5, pitch, rows, axial), F32),
            pltpu.VMEM((nfield, rows, axial), F32),
        ],
        flops=2**24,
        nbytes=2**22,
    )
    outer, new_rows, beyond = call(
        lambda *refs: edges(nspan, *refs),
        [
            ((nfield, 4, radial, axial), F32),
            ((pitch, LANES), F32),
            ((8, LANES), F32),
        ],
        (fields, diffusivity, speeds, halo, a_got, b_got, near_edge, new_rows),
        [VMEM] * 8,
        [pltpu.VMEM((nfield, rows, axial), F32)],
        flops=2**23,
        nbytes=2**21,
    )
    return call(
        lambda *refs: interface(npitch, nspan, *refs),
        [(fields.shape, F32), ((values, npitch * capacity), F32)],
        (mid, outer, face, new_rows, beyond, buf),
        [VMEM] * 6,
        [
            pltpu.VMEM((values, npitch * capacity), F32),
            pltpu.VMEM((nfield, pitch, radial, LANES), F32),
            pltpu.VMEM((2, npitch * pitch + pitch + 8, LANES), F32),
            pltpu.SemaphoreType.DMA((5,)),
        ],
        flops=2**22,
        nbytes=2**21,
        place=ANY,
    )


def solution(mesh):
    placed = (
        P(None, "pitch", "span", "row"),
        P("pitch", "span", "row"),
        P("span", None, "row"),
        P(),
        P(None, ("pitch", "span", "row")),
        P(("pitch", "span", "row")),
        P(("pitch", "span", "row"), None),
        P("row", "pitch"),
    )
    return jax.shard_map(
        local,
        mesh=mesh,
        in_specs=placed,
        out_specs=(P(None, "pitch", "span", "row"), P(None, ("pitch", "span", "row"))),
        check_vma=False,
    )
```

time: 40.3 us -> 32.3 us (0.80)
  waiting for transfers between devices: 7.82 us -> 2.86 us
  local copies, waits for them, and re-layouts: 3.47 us -> 0.67 us
    ppermute x1, waiting for transfers between devices: 5.78 us -> 2.55 us  [local(): b_got = lax.ppermute(b_send, 'pitch', turn)]
    unnamed x20 -> x16, local copies, waits for them, and re-layouts: 3.47 us -> 0.67 us
    ppermute x1, waiting for transfers between devices: 1.71 us -> 0.01 us  [local(): a_got = lax.ppermute(a_send, 'pitch', swap)]
    pallas_call x4 -> x6, Pallas kernels: 13.3 us -> 13.2 us  [call(): pl.pallas_call(body, out_shape=tuple((jax.ShapeDtypeStruct(s, d) for s, d...]
  transfers between devices with their start and end apart: 4 -> 4, of which waited for: 3 -> 2; matrix products, arithmetic and copies ran while one was open for 0% -> 0% of each run, Pallas kernels for 5% -> 25%
where the time goes in v2:
time: 32.3 us; the launch traced here: 32.1 us
  starting transfers between devices  14.6 us (45%)
  Pallas kernels  13.2 us (41%)
  waiting for transfers between devices  2.86 us (9%)
  between operations  0.76 us (2%)
  local copies, waits for them, and re-layouts  0.67 us (2%)
    pallas_call x6, Pallas kernels, call(): pl.pallas_call(body, out_shape=tuple((jax.ShapeDtypeStruct(s, d) for s, d...  13.2 us
    all_to_all x1, starting transfers between devices, local(): lax.all_to_all(buf.reshape(npitch * 2, per_slot, LANES), ('pitch', 'row')...  6.4 us
    ppermute x1, starting transfers between devices, local(): b_got = lax.ppermute(b_send, 'pitch', turn)  3.27 us
    ppermute x1, starting transfers between devices, local(): span_got = (lax.ppermute(packed[0], 'span', [(0, 1), (1, 0)]),)  3.03 us
    ppermute x1, waiting for transfers between devices, local(): b_got = lax.ppermute(b_send, 'pitch', turn)  2.55 us
    ppermute x1, starting transfers between devices, local(): a_got = lax.ppermute(a_send, 'pitch', swap)  1.93 us
    unnamed x16, local copies, waits for them, and re-layouts  0.67 us
  transfers between devices with their start and end apart: 4, of which 2 were waited for; matrix products, arithmetic and copies ran while one was open for 0% of the time, Pallas kernels for 25%

profile of v2, /device:TPU:0, one launch (start us, length us, event | category | flops | bytes accessed | tf_op | source)
XLA Modules:
  0.0 32.1 jit_solution(4363898700579235890)
XLA Ops:
  0.6 0.0 copy-start
  0.6 0.0 copy-start.6
  0.6 0.0 copy-start.5
  0.7 1.2 %shard_map.96 = bf16[160,256]{1,0:T(8,128)(2,1)S(1)} custom-call(f32[3,16,16,256]{3,2,1,0:T(8,128)} %refs_0_.9, f32[16,16,256]{2,1,0:T(8,128)} %refs_1_.7, bf16[16,2,256]{2,1,0:T(2,128)(2,1)} %refs_2_.3), custom_call_target="tpu_custom_call" | custom-call | bytes 1048576 | tf_op jit(solution)/shard_map/pallas_call | solution.py:38
  1.9 3.0 %collective-permute-start = (bf16[160,256]{1,0:T(8,128)(2,1)S(1)}, bf16[160,256]{1,0:T(8,128)(2,1)S(1)}, u32[]{:S(2)}, u32[]{:S(2)}) collective-permute-start(bf16[160,256]{1,0:T(8,128)(2,1)S(1)} %shard_map.96), channel_id=1, source_target_pairs={{0,2},{2,0},{1,3},{3,1},{4,6},{6,4},{5,7},{7,5},{8,10},{10,8},{9,1... | collective-permute-start | bytes 245768 | tf_op jit(solution)/shard_map/ppermute | solution.py:625
  4.9 0.0 copy-done
  4.9 0.0 copy-done.6
  4.9 0.0 copy-done.5
  5.0 0.0 copy-start.1
  5.0 0.0 copy-start.2
  5.0 0.0 copy-start.3
  5.0 0.0 copy-start.4
  5.0 2.1 %shard_map.95 = (f32[8,2048]{1,0:T(8,128)S(1)}, s32[1,2048]{1,0:T(1,128)S(1)}) custom-call(f32[3,16,16,256]{3,2,1,0:T(8,128)S(1)} %copy-done, s32[16,128]{1,0:T(8,128)S(1)} %bitcast.5, s32[16,128]{1,0:T(8,128)S(1)} %bitcast.7), custom_call_target="tpu_custom_call" | custom-call | flops 1610612736 | bytes 1048576 | tf_op jit(solution)/shard_map/pallas_call | solution.py:38
  7.1 0.3 collective-permute-done.refs_10_
  7.4 0.0 copy-start.7
  7.4 0.0 copy-done.1
  7.4 0.0 copy-done.2
  7.4 0.0 copy-done.3
  7.4 0.0 copy-done.4
  7.4 0.6 %copy-done.7 = s32[1,16]{1,0:T(1,128)S(1)} copy-done((s32[1,16]{1,0:T(1,128)S(1)}, s32[1,16]{1,0:T(1,128)}, u32[]{:S(2)}) %copy-start.7) | copy-done | bytes 88
  8.0 2.4 %shard_map.97 = (f32[8,2,40,128]{3,2,1,0:T(8,128)}, bf16[144,256]{1,0:T(8,128)(2,1)S(1)}, bf16[144,256]{1,0:T(8,128)(2,1)S(1)}, f32[2,24,256]{2,1,0:T(8,128)S(1)...) custom-call(f32[3,16,16,256]{3,2,1,0:T(8,128)S(1)} %copy-done, f32[16,16,256]{2,1,0:T(8,128)S(1)} %copy-done.1, ...), custom_call_target="tpu_custom_call" | custom-call | flops 536870912 | bytes 2097152 | tf_op jit(solution)/shard_map/pallas_call | solution.py:38
  10.5 6.4 %all-to-all-start = ((f32[16,40,128]{2,1,0:T(8,128)}), f32[16,40,128]{2,1,0:T(8,128)S(1)}, u32[]{:S(2)}, u32[]{:S(2)}) async-start(f32[16,40,128]{2,1,0:T(8,128)} %bitcast.2), calls=%async_computation | async-start | bytes 655360 | tf_op jit(solution)/shard_map/all_to_all | solution.py:680
  16.9 1.9 %collective-permute-start.1 = (bf16[144,256]{1,0:T(8,128)(2,1)S(1)}, bf16[144,256]{1,0:T(8,128)(2,1)S(1)}, u32[]{:S(2)}, u32[]{:S(2)}) collective-permute-start(bf16[144,256]{1,0:T(8,128)(2,1)S(1)} %get-tuple-element.21), channel_id=1, source_target_pairs={{0,4},{4,0},{8,12},{12,8},{16,20},{20,16},{24,28},{28,24},{1,5},{5... | collective-permute-start | bytes 221192 | tf_op jit(solution)/shard_map/ppermute | solution.py:685
  18.8 3.3 %collective-permute-start.2 = (bf16[144,256]{1,0:T(8,128)(2,1)S(1)}, bf16[144,256]{1,0:T(8,128)(2,1)S(1)}, u32[]{:S(2)}, u32[]{:S(2)}) collective-permute-start(bf16[144,256]{1,0:T(8,128)(2,1)S(1)} %get-tuple-element.22), channel_id=1, source_target_pairs={{4,8},{8,4},{12,16},{16,12},{20,24},{24,20},{28,0},{0,28},{5,9},{9... | collective-permute-start | bytes 221192 | tf_op jit(solution)/shard_map/ppermute | solution.py:686
  22.1 4.9 %shard_map.98 = (f32[3,12,16,256]{3,2,1,0:T(8,128)S(1)}, f32[3,4,24,256]{3,2,1,0:T(8,128)S(1)}, f32[16,128]{1,0:T(8,128)S(1)}) custom-call(f32[3,16,16,256]{3,2,1,0:T(8,128)S(1)} %copy-done, f32[16,16,256]{2,1,0:T(8,128)S(1)} %copy-done.1, f32[2,24,256]{2,1,0:T(8,128)S(1)} %get-tuple-element.18.refs_2_, f32[64,8,256]{2,1,0:T(8,128)S(1)} %get-tuple-element.19.refs_3_), custom_call_target="tpu_custom_call" | custom-call | flops 16777216 | bytes 4194304 | tf_op jit(solution)/shard_map/pallas_call | solution.py:38
  27.0 0.0 collective-permute-done.1.refs_4_
  27.0 2.5 %collective-permute-done.2.refs_5_ = bf16[144,256]{1,0:T(8,128)(2,1)S(1)} collective-permute-done((bf16[144,256]{1,0:T(8,128)(2,1)S(1)}, bf16[144,256]{1,0:T(8,128)(2,1)S(1)}, u32[]{:S(2)}, u32[]{:S(2)}) %collective-permute-start.2) | collective-permute-done | bytes 73760 | tf_op jit(solution)/shard_map/ppermute | solution.py:686
  29.5 0.9 %shard_map.99 = (f32[3,4,16,256]{3,2,1,0:T(8,128)S(1)}, f32[16,128]{1,0:T(8,128)S(1)}, f32[8,128]{1,0:T(8,128)S(1)}) custom-call(f32[3,16,16,256]{3,2,1,0:T(8,128)S(1)} %copy-done, f32[16,16,256]{2,1,0:T(8,128)S(1)} %copy-done.1, f32[2,24,256]{2,1,0:T(8,128)S(1)} %get-tuple-element.18.refs_2_, f32[64,8,256]{2,1,0:T(8,128)S(1)} %get-tuple-element.19.refs_3_, ...), custom_call_target="tpu_custom_call" | custom-call | flops 8388608 | bytes 2097152 | tf_op jit(solution)/shard_map/pallas_call | solution.py:38
  30.5 0.0 all-to-all-done
  30.5 1.6 %shard_map.100 = (f32[3,16,16,256]{3,2,1,0:T(8,128)}, f32[10,4096]{1,0:T(8,128)}) custom-call(f32[3,12,16,256]{3,2,1,0:T(8,128)S(1)} %get-tuple-element.20.refs_0_, f32[3,4,16,256]{3,2,1,0:T(8,128)S(1)} %get-tuple-element.25.refs_1_, f32[40,128]{1,0:T(8,128)S(1)} %get-tuple-element.26.refs_2_, f32[16,128]{1,0:T(8,128)S(1)} %get-tuple-element.27.refs_3_, ...), custom_call_target="tpu_custom_call" | custom-call | flops 4194304 | bytes 2097152 | tf_op jit(solution)/shard_map/pallas_call | solution.py:38
Async XLA Ops:
  0.6 4.3 %copy-start = (f32[3,16,16,256]{3,2,1,0:T(8,128)S(1)}, f32[3,16,16,256]{3,2,1,0:T(8,128)}, u32[]{:S(2)}) copy-start(f32[3,16,16,256]{3,2,1,0:T(8,128)} %refs_0_.9) | copy-start | bytes 2359300
  0.6 4.3 %copy-start.6 = (s32[2048,1]{0,1:T(1,128)S(1)}, s32[2048,1]{0,1:T(1,128)}, u32[]{:S(2)}) copy-start(s32[2048,1]{0,1:T(1,128)} %param.14) | copy-start | bytes 24580
  0.6 4.3 %copy-start.5 = (s32[2048]{0:T(1024)S(1)}, s32[2048]{0:T(1024)}, u32[]{:S(2)}) copy-start(s32[2048]{0:T(1024)} %param.13) | copy-start | bytes 24580
  1.9 5.5 %collective-permute-start = (bf16[160,256]{1,0:T(8,128)(2,1)S(1)}, bf16[160,256]{1,0:T(8,128)(2,1)S(1)}, u32[]{:S(2)}, u32[]{:S(2)}) collective-permute-start(bf16[160,256]{1,0:T(8,128)(2,1)S(1)} %shard_map.96), channel_id=1, source_target_pairs={{0,2},{2,0},{1,3},{3,1},{4,6},{6,4},{5,7},{7,5},{8,10},{10,8},{9,1... | collective-permute-start | bytes 245768 | tf_op jit(solution)/shard_map/ppermute | solution.py:625
  5.0 2.4 %copy-start.1 = (f32[16,16,256]{2,1,0:T(8,128)S(1)}, f32[16,16,256]{2,1,0:T(8,128)}, u32[]{:S(2)}) copy-start(f32[16,16,256]{2,1,0:T(8,128)} %refs_1_.7) | copy-start | bytes 786436
  5.0 2.4 %copy-start.2 = (bf16[16,2,256]{2,1,0:T(2,128)(2,1)S(1)}, bf16[16,2,256]{2,1,0:T(2,128)(2,1)}, u32[]{:S(2)}) copy-start(bf16[16,2,256]{2,1,0:T(2,128)(2,1)} %refs_2_.3) | copy-start | bytes 49156
  5.0 2.4 %copy-start.3 = (f32[10,2048]{1,0:T(8,128)S(1)}, f32[10,2048]{1,0:T(8,128)}, u32[]{:S(2)}) copy-start(f32[10,2048]{1,0:T(8,128)} %refs_4_.1) | copy-start | bytes 245764
  5.0 2.4 %copy-start.4 = (bf16[32,32]{1,0:T(8,128)(2,1)S(1)}, bf16[32,32]{1,0:T(8,128)(2,1)}, u32[]{:S(2)}) copy-start(bf16[32,32]{1,0:T(8,128)(2,1)} %refs_3_.1) | copy-start | bytes 6148
  7.4 0.7 %copy-start.7 = (s32[1,16]{1,0:T(1,128)S(1)}, s32[1,16]{1,0:T(1,128)}, u32[]{:S(2)}) copy-start(s32[1,16]{1,0:T(1,128)} %refs_9_.1) | copy-start | bytes 196
  10.5 20.0 %all-to-all-start = ((f32[16,40,128]{2,1,0:T(8,128)}), f32[16,40,128]{2,1,0:T(8,128)S(1)}, u32[]{:S(2)}, u32[]{:S(2)}) async-start(f32[16,40,128]{2,1,0:T(8,128)} %bitcast.2), calls=%async_computation | async-start | bytes 655360 | tf_op jit(solution)/shard_map/all_to_all | solution.py:680
  16.9 10.1 %collective-permute-start.1 = (bf16[144,256]{1,0:T(8,128)(2,1)S(1)}, bf16[144,256]{1,0:T(8,128)(2,1)S(1)}, u32[]{:S(2)}, u32[]{:S(2)}) collective-permute-start(bf16[144,256]{1,0:T(8,128)(2,1)S(1)} %get-tuple-element.21), channel_id=1, source_target_pairs={{0,4},{4,0},{8,12},{12,8},{16,20},{20,16},{24,28},{28,24},{1,5},{5... | collective-permute-start | bytes 221192 | tf_op jit(solution)/shard_map/ppermute | solution.py:685
  18.8 10.8 %collective-permute-start.2 = (bf16[144,256]{1,0:T(8,128)(2,1)S(1)}, bf16[144,256]{1,0:T(8,128)(2,1)S(1)}, u32[]{:S(2)}, u32[]{:S(2)}) collective-permute-start(bf16[144,256]{1,0:T(8,128)(2,1)S(1)} %get-tuple-element.22), channel_id=1, source_target_pairs={{4,8},{8,4},{12,16},{16,12},{20,24},{24,20},{28,0},{0,28},{5,9},{9... | collective-permute-start | bytes 221192 | tf_op jit(solution)/shard_map/ppermute | solution.py:686

commit v3 on v2

v3 whole, which is shorter than its diff:
```python
import jax
import jax.numpy as jnp
from jax import lax
from jax.experimental import pallas as pl
from jax.experimental.pallas import tpu as pltpu
from jax.sharding import PartitionSpec as P

SUB = 2
TIME_STEP = 0.9
AXIAL_SPEED = 0.15
PITCH_SPEED = 0.15
LANES = 128
EXTRA = 8
SLAB = 32
F32 = jnp.float32
BF16 = jnp.bfloat16
VMEM = pl.BlockSpec(memory_space=pltpu.VMEM)
ANY = pl.BlockSpec(memory_space=pl.ANY)
HBM = pl.BlockSpec(memory_space=pltpu.HBM)
CODE = 10.0
FINE = 18.0
VMEM_LIMIT = 48 * 1024 * 1024


def iota(shape, dim):
    return lax.broadcasted_iota(jnp.int32, shape, dim)


def split(x):
    high = x.astype(BF16)
    return high, (x - high.astype(F32)).astype(BF16)


def power(n):
    assert n & (n - 1) == 0
    return n.bit_length() - 1


def call(body, outs, args, specs, scratch=(), flops=0, nbytes=0, place=VMEM, fixed=False):
    shape = pltpu.VMEM if fixed else jax.ShapeDtypeStruct
    return pl.pallas_call(
        body,
        out_shape=tuple(shape(s, d) for s, d in outs),
        in_specs=list(specs),
        out_specs=tuple(place for _ in outs),
        scratch_shapes=list(scratch),
        compiler_params=pltpu.CompilerParams(vmem_limit_bytes=VMEM_LIMIT),
        cost_estimate=pl.CostEstimate(flops=flops, bytes_accessed=nbytes, transcendentals=0),
    )(*args)


def pack_span(nspan, n_in, *refs):
    ins, rest = refs[:n_in], refs[n_in:]
    outs, kept, (m_s, sems) = rest[: -n_in - 1], rest[-n_in - 1 : -2], rest[-2:]
    f_ref, k_ref = kept[:2]
    radial, axial = f_ref.shape[2:]
    s = lax.axis_index("span")
    half = radial - 8
    early = [pltpu.make_async_copy(ins[-1], m_s, sems.at[0])]
    late = []
    for n, first, size in ((0, (1 - s) * half, 8), (1, s * 8, half)):
        rows = pl.ds(pl.multiple_of(first, 8), size)
        copies = [
            pltpu.make_async_copy(
                ins[0].at[:, :, rows, :], f_ref.at[:, :, rows, :], sems.at[1 + 2 * n]
            ),
            pltpu.make_async_copy(ins[1].at[:, rows, :], k_ref.at[:, rows, :], sems.at[2 + 2 * n]),
        ]
        if n == 0 or nspan > 2:
            early += copies
        else:
            late += copies
    for n in range(2, n_in - 1):
        late.append(pltpu.make_async_copy(ins[n], kept[n], sems.at[n + 3]))
    for copy in early + late:
        copy.start()
    for copy in early:
        copy.wait()

    def edge(first):
        parts = []
        for r in range(2):
            row = pl.ds(first + r, 1)
            parts += [f_ref[:, :, row, :].reshape(-1, axial), k_ref[:, row, :].reshape(-1, axial)]
        return jnp.concatenate(parts, 0).astype(BF16)

    flow = m_s[...].astype(F32)
    flow = jnp.concatenate([flow[:, 0, :], flow[:, 1, :]], 0).astype(BF16)
    if nspan == 2:
        packed = edge((1 - s) * (radial - 2))
        outs[0][: packed.shape[0]] = packed
        outs[0][packed.shape[0] :] = flow
    else:
        outs[0][...] = edge(radial - 2)
        outs[1][...] = edge(0)
        outs[2][...] = flow
    for copy in late:
        copy.wait()


def tracer_chunk(ref, c):
    both = [ref[pl.ds(2 * c + n, 1), :] for n in range(2)]
    return jnp.concatenate(both, 1), pl.ds(pl.multiple_of(c * 2 * LANES, 2 * LANES), 2 * LANES)


def one_hot(rows, index):
    return (iota((rows, index.shape[1]), 0) == index).astype(F32).astype(BF16)


def sample_fields(npitch, f_ref, cell_ref, dest_ref, samp_ref, place_ref, key_ref, pick_ref, table_s):
    nfield, pitch, radial, axial = f_ref.shape
    lines = pitch * radial
    chunks = cell_ref.shape[0]

    @pl.loop(0, nfield, unroll=True)
    def _(f):
        table_s[f] = jnp.exp2(FINE * f_ref[f].reshape(lines, axial)).astype(BF16)

    table = table_s[...].reshape(nfield * lines, axial)
    samp_ref[...] = jnp.zeros(samp_ref.shape, F32)

    @pl.loop(0, chunks // 2, unroll=True)
    def _(c):
        cells, span = tracer_chunk(cell_ref, c)
        pick = one_hot(axial, cells & (axial - 1))
        pick_ref[:, span] = pick
        got = jnp.dot(table, pick, preferred_element_type=F32)
        mine = iota((lines, cells.shape[1]), 0) == lax.shift_right_logical(cells, power(axial))
        for f in range(nfield):
            part = jnp.where(mine, got[f * lines : (f + 1) * lines], 0.0)
            part = jnp.sum(part, 0, keepdims=True)
            samp_ref[f : f + 1, span] = jnp.log2(part) * (1.0 / FINE)

    ones = []
    for c in range(chunks):
        ones.append((iota((npitch, LANES), 0) == dest_ref[c : c + 1, :]).astype(F32))
    stacked = jnp.concatenate(ones, 0)
    before = (iota((LANES, LANES), 0) < iota((LANES, LANES), 1)).astype(F32).astype(BF16)
    prefix = jnp.dot(stacked.astype(BF16), before, preferred_element_type=F32)
    carry = jnp.zeros((npitch, 1), F32)
    for c in range(chunks):
        rank = prefix[c * npitch : (c + 1) * npitch] + carry
        slot = jnp.sum(rank * ones[c], 0, keepdims=True).astype(jnp.int32)
        span = slice(c * LANES, (c + 1) * LANES)
        width = place_ref.shape[0]
        place_ref[:, span] = one_hot(width, slot & (width - 1))
        groups = 2 * chunks * LANES // npitch // width
        key_ref[:, span] = dest_ref[c : c + 1, :] * groups + lax.shift_right_logical(slot, power(width))
        carry = carry + jnp.sum(ones[c], 1, keepdims=True)


def slab(core, extra):
    return [extra, core, extra]


def near(stator, parts):
    turned = jnp.concatenate(parts, 0).T
    return (
        jnp.where(stator, turned[LANES - 1 : LANES], turned[0:1]),
        jnp.where(stator, turned[LANES - 2 : LANES - 1], turned[1:2]),
    )


def dispatch(
    npitch,
    nspan,
    f_ref,
    k_ref,
    kern_ref,
    tv_ref,
    cell_ref,
    map_ref,
    samp_ref,
    place_ref,
    key_ref,
    pick_ref,
    *refs,
):
    nfield, pitch, radial, axial = f_ref.shape
    planes = nfield + 1
    edge = planes * pitch
    if nspan == 2:
        sent_ref, got_ref = refs[:2]
        refs = refs[2:]
        low_ref = high_ref = got_ref
    else:
        low_ref, high_ref, all_ref = refs[:3]
        refs = refs[3:]
    buf_ref, up_ref, down_ref, speed_ref, halo_ref, face_ref, kern_s, upd_s, lhs_s, acc_s, face_s, near_s = refs
    s = lax.axis_index("span")
    q = lax.axis_index("row")

    total = kern_ref.shape[0]
    kern_s[...] = kern_ref[...].astype(F32)
    main = kern_s[pl.ds(pl.multiple_of(s * radial, 8), radial), :]
    above = kern_s[pl.ds(pl.multiple_of(jnp.minimum((s + 1) * radial, total - 8), 8), 8), :]
    below = kern_s[pl.ds(pl.multiple_of(jnp.maximum(s * radial - 8, 0), 8), 8), :]
    wide = jnp.concatenate([main, jnp.where(iota((EXTRA, total), 0) < 4, above, below)], 0).astype(BF16)
    smoothed = []
    for c in range(2):
        if nspan == 2:
            at = slice(2 * edge + c * radial, 2 * edge + (c + 1) * radial)
            own, other = sent_ref[at, :].astype(F32), got_ref[at, :].astype(F32)
            rows = [jnp.where(s == 0, own, other), jnp.where(s == 0, other, own)]
        else:
            rows = [all_ref[n, c * radial : (c + 1) * radial, :].astype(F32) for n in range(nspan)]
        smoothed.append(
            jnp.dot(wide, jnp.concatenate(rows, 0).astype(BF16), preferred_element_type=F32)
        )
    sa = AXIAL_SPEED * (1.0 + 0.5 * jnp.tanh(smoothed[0]))
    sp = PITCH_SPEED * jnp.tanh(smoothed[1])
    speed_ref[0] = sa
    speed_ref[1] = sp

    chunks = cell_ref.shape[0]
    values, tracers = tv_ref.shape
    capacity = 2 * tracers // npitch
    count = nfield + 2
    table = jnp.concatenate(split(jnp.concatenate([sa[:radial], sp[:radial]], 0)), 0)

    @pl.loop(0, chunks // 2, unroll=True)
    def _(c):
        cells, span = tracer_chunk(cell_ref, c)
        line = lax.shift_right_logical(cells, power(axial)) & (radial - 1)
        got = jnp.dot(table, pick_ref[:, span], preferred_element_type=F32)
        got = got[: 2 * radial] + got[2 * radial :]
        mine = iota((radial, cells.shape[1]), 0) == line
        sampled = [samp_ref[f : f + 1, span] for f in range(nfield)]
        for n in range(2):
            part = jnp.where(mine, got[n * radial : (n + 1) * radial], 0.0)
            sampled.append(jnp.sum(part, 0, keepdims=True))
        for v, value in enumerate(sampled):
            head = tv_ref[v : v + 1, span]
            upd_s[v : v + 1, span] = head + 0.5 * (value - head)
            upd_s[count + v : count + v + 1, span] = tv_ref[count + v : count + v + 1, span] + 0.8 * value

    width = place_ref.shape[0]
    groups = capacity // width
    keys = npitch * groups
    coded = jnp.exp2(CODE * upd_s[:values])
    mine = iota((keys, tracers), 0) == key_ref[...]
    for v in range(values):
        lhs_s[v * keys : (v + 1) * keys, :] = jnp.where(mine, coded[v : v + 1], 0.0).astype(BF16)
    acc_s[...] = lax.dot_general(
        lhs_s[...], place_ref[...], (((1,), (1,)), ((), ())), preferred_element_type=F32
    ).reshape(acc_s.shape)
    room = buf_ref.shape[2] - values * capacity // LANES
    filler = [jnp.zeros((room, LANES), F32)] if room else []
    for d in range(npitch):
        pieces = []
        for g in range(groups):
            for n in range(width // LANES):
                pieces.append(acc_s[:, d * groups + g, n * LANES : (n + 1) * LANES])
        buf_ref[d, q] = jnp.concatenate(pieces + filler, 0).astype(BF16)

    sub = iota((EXTRA, axial), 0)
    near_s[0] = high_ref[: 2 * edge].astype(F32)
    near_s[1] = low_ref[: 2 * edge].astype(F32)

    @pl.loop(0, edge, unroll=True)
    def _(n):
        tile = jnp.where(sub == 0, near_s[0, pl.ds(n, 1), :], 0.0)
        tile = jnp.where(sub == 1, near_s[0, pl.ds(edge + n, 1), :], tile)
        tile = jnp.where(sub == 6, near_s[1, pl.ds(n, 1), :], tile)
        halo_ref[n] = jnp.where(sub == 7, near_s[1, pl.ds(edge + n, 1), :], tile)

    stator = q == 0
    tile = pl.ds(pl.multiple_of((1 - q) * (axial - LANES), LANES), LANES)
    face_s[...] = jnp.zeros(face_s.shape, F32)

    @pl.loop(0, pitch, unroll=True)
    def _(i):
        parts = []
        for f in range(planes):
            core = f_ref[f, i, :, tile] if f < nfield else k_ref[i, :, tile]
            parts += slab(core, halo_ref[f * pitch + i, :, tile])
        first, second = near(stator, parts)
        face_s[pl.ds(i, 1), :] = first
        face_s[pl.ds(pitch + i, 1), :] = second

    parts = []
    for n in range(2):
        speed = speed_ref[n, :, tile]
        parts += slab(speed[:radial], speed[radial:])
    first, second = near(stator, parts + [jnp.zeros((LANES - 2 * SLAB, LANES), F32)])
    face_s[2 * pitch : 2 * pitch + 1] = first
    face_s[2 * pitch + 1 : 2 * pitch + 2] = second
    face = face_s[...]
    face_ref[...] = face
    offset = map_ref[...].astype(F32)
    face_ref[2 * pitch + 2 : 2 * pitch + 3] = jnp.broadcast_to(offset[:, :1], (1, LANES))
    face = face.astype(BF16)

    @pl.loop(0, npitch, unroll=True)
    def _(d):
        buf_ref[d, 1 - q] = face

    def layers(ref, top):
        rows = []
        for f in range(planes):
            for n in range(2):
                i = top * (pitch - 2) + n
                rows.append(f_ref[f, i] if f < nfield else k_ref[i])
        for f in range(planes):
            corner = halo_ref[f * pitch + top * (pitch - 1)]
            rows += [corner[0:1], corner[7:8]]
        rows.append(jnp.zeros((8, axial), F32))
        ref[...] = jnp.concatenate(rows, 0).astype(BF16)

    layers(up_ref, 1)
    layers(down_ref, 0)


class Faces:
    def __init__(self, nspan, speed_ref, radial):
        self.rows, self.lanes = speed_ref.shape[1:]
        shape = (self.rows, self.lanes)
        s = lax.axis_index("span")
        stator = lax.axis_index("row") == 0
        lane, radius = iota(shape, 1), iota(shape, 0)
        sa = TIME_STEP * speed_ref[0]
        sp = TIME_STEP * speed_ref[1]
        wa = 0.5 * (sa + pltpu.roll(sa, self.lanes - 1, 1))
        self.first, self.last = lane == 0, lane == self.lanes - 1
        up, dn = jnp.maximum(wa, 0.0), jnp.minimum(wa, 0.0)
        self.axial = (
            jnp.where(self.last, 0.0, up),
            jnp.where(self.last, 0.0, dn),
            pltpu.roll(jnp.where(self.last, 0.0, up), 1, 1),
            pltpu.roll(jnp.where(self.last, 0.0, dn), 1, 1),
        )
        self.pitch_up, self.pitch_dn = jnp.maximum(sp, 0.0), jnp.minimum(sp, 0.0)
        top, bottom = s == nspan - 1, s == 0
        end = self.rows - 1
        self.wall_up = ((radius == radial - 1) & top) | ((radius == end) & bottom)
        self.wall_dn = ((radius == radial) & top) | ((radius == 0) & bottom)
        inlet = jnp.where(stator & self.first, sa, 0.0)
        keep = 1.0 + inlet - jnp.where(jnp.logical_not(stator) & self.last, sa, 0.0)
        self.keep = keep - self.axial[0] + self.axial[3] - self.pitch_up + self.pitch_dn

    def weights(self, k_before, k, k_after):
        half = 0.5 * TIME_STEP
        k = half * k
        k_up = jnp.where(self.last, 0.0, k + pltpu.roll(k, self.lanes - 1, 1))
        k_dn = jnp.where(self.first, 0.0, k + pltpu.roll(k, 1, 1))
        r_up = jnp.where(self.wall_up, 0.0, k + pltpu.roll(k, self.rows - 1, 0))
        r_dn = jnp.where(self.wall_dn, 0.0, k + pltpu.roll(k, 1, 0))
        p_up, p_dn = k + half * k_after, k + half * k_before
        return (
            self.keep - (k_up + k_dn) - (r_up + r_dn) - (p_up + p_dn),
            k_up - self.axial[1],
            k_dn + self.axial[2],
            r_up,
            r_dn,
            p_up - self.pitch_dn,
            p_dn + self.pitch_up,
        )

    def step(self, w, before, v, after):
        a = w[0] * v + w[1] * pltpu.roll(v, self.lanes - 1, 1)
        b = w[2] * pltpu.roll(v, 1, 1) + w[3] * pltpu.roll(v, self.rows - 1, 0)
        c = w[4] * pltpu.roll(v, 1, 0) + w[5] * after
        return (a + b) + (c + w[6] * before)


def middle(nspan, f_ref, k_ref, speed_ref, halo_ref, o_ref, y4_ref, row_ref, y_s, w_s):
    nfield, pitch, radial, axial = f_ref.shape
    stator = lax.axis_index("row") == 0
    faces = Faces(nspan, speed_ref, radial)

    def state(f, i):
        return jnp.concatenate([f_ref[f, i], halo_ref[f * pitch + i]], 0)

    def kappa(i):
        return jnp.concatenate([k_ref[i], halo_ref[nfield * pitch + i]], 0)

    @pl.loop(1, pitch - 1, unroll=True)
    def _(i):
        w = faces.weights(kappa(i - 1), kappa(i), kappa(i + 1))
        for n, value in enumerate(w):
            w_s[n, i] = value
        for f in range(nfield):
            y_s[f, i] = faces.step(w, state(f, i - 1), state(f, i), state(f, i + 1))

    @pl.loop(2, pitch - 2, unroll=True)
    def _(i):
        w = [w_s[n, i] for n in range(7)]
        for f in range(nfield):
            o_ref[f, i - 2] = faces.step(w, y_s[f, i - 1], y_s[f, i], y_s[f, i + 1])[:radial]

    for f in range(nfield):
        for n, i in enumerate((1, 2, pitch - 3, pitch - 2)):
            y4_ref[f, n] = y_s[f, i]
    row_ref[...] = jnp.zeros(row_ref.shape, F32)
    q = lax.axis_index("row")
    tile = pl.ds(pl.multiple_of((1 - q) * (axial - LANES), LANES), LANES)
    blank = jnp.zeros((SLAB, LANES), F32)

    @pl.loop(1, pitch - 1, unroll=True)
    def _(i):
        parts = []
        for f in range(nfield):
            parts += slab(y_s[f, i, :radial, tile], y_s[f, i, radial:, tile])
        row_ref[pl.ds(i, 1), :] = near(stator, parts + [blank])[0]


def edges(
    nspan, f_ref, k_ref, speed_ref, halo_ref, lower_ref, upper_ref, y4_ref, row_ref, o_ref, row_out, beyond_ref, y_s
):
    nfield, pitch, radial, axial = f_ref.shape
    planes = nfield + 1
    stator = lax.axis_index("row") == 0
    faces = Faces(nspan, speed_ref, radial)
    ext = {-1: lower_ref[...].astype(F32), 1: upper_ref[...].astype(F32)}
    sub = iota((EXTRA, axial), 0)
    corner_at = 2 * planes * radial

    def state(f, i):
        if 0 <= i < pitch:
            core = f_ref[f, i] if f < nfield else k_ref[i]
            return jnp.concatenate([core, halo_ref[f * pitch + i]], 0)
        side = ext[-1 if i < 0 else 1]
        at = (2 * f + (i + 2 if i < 0 else i - pitch)) * radial
        extra = jnp.zeros((EXTRA, axial), F32)
        if i in (-1, pitch):
            corner = corner_at + 2 * f
            extra = jnp.where(sub == 0, side[corner : corner + 1], 0.0)
            extra = jnp.where(sub == 7, side[corner + 1 : corner + 2], extra)
        return jnp.concatenate([side[at : at + radial], extra], 0)

    row_out[...] = row_ref[...]
    beyond_ref[...] = jnp.zeros(beyond_ref.shape, F32)
    tile = pl.ds(pl.multiple_of(lax.axis_index("row") * (LANES - axial) + axial - LANES, LANES), LANES)

    def edge_lanes(value):
        return jnp.where(stator, value[:, axial - LANES :], value[:, :LANES])

    blank = jnp.zeros((SLAB, LANES), F32)
    held = {i: n for n, i in enumerate((1, 2, pitch - 3, pitch - 2))}
    for side, new, done in ((0, (-1, 0), (0, 1)), (1, (pitch - 1, pitch), (pitch - 2, pitch - 1))):
        touched = sorted({*new, *done})
        k = {i: state(nfield, i) for i in range(touched[0] - 1, touched[-1] + 2)}
        w = {i: faces.weights(k[i - 1], k[i], k[i + 1]) for i in touched}
        for f in range(nfield):
            x = {i: state(f, i) for i in range(new[0] - 1, new[1] + 2)}
            y = {i: y4_ref[f, held[i]] for i in held if done[0] - 1 <= i <= done[1] + 1}
            for i in new:
                y[i] = faces.step(w[i], x[i - 1], x[i], x[i + 1])
            for n, i in enumerate(done):
                o_ref[f, 2 * side + n] = faces.step(w[i], y[i - 1], y[i], y[i + 1])[:radial]
            y_s[f] = y[0 if side == 0 else pitch - 1]
        parts = []
        for f in range(nfield):
            parts += slab(y_s[f, :radial, tile], y_s[f, radial:, tile])
        i = 0 if side == 0 else pitch - 1
        row_out[i : i + 1] = near(stator, parts + [blank])[0]
        parts = []
        for f in range(planes):
            value = edge_lanes(state(f, -1 if side == 0 else pitch))
            parts += slab(value[:radial], value[radial:])
        beyond_ref[side : side + 1] = near(stator, parts)[0]


def interface(
    npitch,
    nspan,
    mid_ref,
    edge_ref,
    face_ref,
    row_ref,
    beyond_ref,
    buf_ref,
    o_ref,
    arr_ref,
    arr_s,
    tile_s,
    ring_s,
    add_s,
    sems,
):
    nfield, pitch, radial, axial = o_ref.shape
    planes = nfield + 1
    s = lax.axis_index("span")
    q = lax.axis_index("row")
    stator = q == 0
    near_tile = pl.ds(pl.multiple_of((1 - q) * (axial - LANES), LANES), LANES)
    copies = []
    if axial > LANES:
        rest = pl.ds(pl.multiple_of(q * LANES, LANES), axial - LANES)
        copies += [
            pltpu.make_async_copy(
                mid_ref.at[:, :, :, rest], o_ref.at[:, 2 : pitch - 2, :, rest], sems.at[0]
            ),
            pltpu.make_async_copy(
                edge_ref.at[:, :2, :, rest], o_ref.at[:, :2, :, rest], sems.at[1]
            ),
            pltpu.make_async_copy(
                edge_ref.at[:, 2:, :, rest], o_ref.at[:, pitch - 2 :, :, rest], sems.at[2]
            ),
        ]
    for copy in copies:
        copy.start()

    values = arr_ref.shape[0]
    capacity = arr_ref.shape[1] // npitch

    @pl.loop(0, npitch, unroll=True)
    def _(p):
        coded = buf_ref[p, q].astype(F32)
        plain = jnp.where(coded > 0.0, jnp.log2(coded) * (1.0 / CODE), 0.0)
        for j in range(capacity // LANES):
            at = pl.ds(pl.multiple_of(p * capacity + j * LANES, LANES), LANES)
            arr_s[:, at] = plain[j * values : (j + 1) * values]

    copies.append(pltpu.make_async_copy(arr_s, arr_ref, sems.at[3]))
    copies[-1].start()

    whole = npitch * pitch
    count = pitch + 8

    @pl.loop(0, npitch, unroll=True)
    def _(p):
        at = pl.ds(pl.multiple_of(p * pitch, pitch), pitch)
        both = buf_ref[p, 1 - q].astype(F32)
        ring_s[0, at, :] = both[:pitch]
        ring_s[1, at, :] = both[pitch : 2 * pitch]

    for n in range(2):
        ring_s[n, whole : whole + pitch] = ring_s[n, :pitch]
        ring_s[n, whole + pitch :] = ring_s[n, pitch : pitch + 8]
    begin = jnp.max(face_ref[2 * pitch + 2 : 2 * pitch + 3]).astype(jnp.int32) - 1
    begin = jnp.where(begin < 0, begin + whole, begin)
    ghost = ring_s[0, pl.ds(begin, count), :]
    farther = ring_s[1, pl.ds(begin, count), :]
    tail = jnp.zeros((count - pitch - 2, LANES), F32)
    own = jnp.concatenate(
        [beyond_ref[0:1], face_ref[:pitch], beyond_ref[1:2], tail], 0
    )
    top = jnp.zeros((1, LANES), F32)
    own_k1 = jnp.concatenate([top, face_ref[pitch : 2 * pitch], top, tail], 0)
    own_new = jnp.concatenate([top, row_ref[...], top, tail], 0)
    at = 2 * pitch

    def groups(row, g):
        out = row
        for f in range(planes):
            if f != g:
                out = jnp.where(iota(row.shape, 1) // SLAB == f, pltpu.roll(row, (f - g) * SLAB % LANES, 1), out)
        return out

    def speeds(rows):
        rows = TIME_STEP * rows
        return groups(rows[0:1], 0), groups(rows[1:2], 0), groups(rows[0:1], 1)

    sa0, sa1, sp0 = speeds(face_ref[at : at + 2])
    ga0, ga1, gp0 = speeds(buf_ref[0, 1 - q].astype(F32)[at : at + 2])
    shape = (count, LANES)
    lane = iota(shape, 1)
    group = lax.shift_right_logical(lane, power(SLAB))
    radius = lane & (SLAB - 1)

    def spread(x):
        out = x
        for f in range(nfield):
            out = jnp.where(group == f, pltpu.roll(x, (f + 1) * SLAB, 1), out)
        return out

    half = 0.5 * TIME_STEP
    k0, k1, g0, g1 = spread(own), spread(own_k1), spread(ghost), spread(farther)
    wall = ((radius == 7 + radial) & (s == nspan - 1)) | ((radius == 7) & (s == 0))

    def ahead(x):
        return pltpu.roll(x, count - 1, 0)

    def outward(x):
        return pltpu.roll(x, LANES - 1, 1)

    def change(v, k, speed):
        kappa = half * (k + ahead(k))
        up, dn = jnp.maximum(speed, 0.0), jnp.minimum(speed, 0.0)
        along = (up + kappa) * v + (dn - kappa) * ahead(v)
        kappa = jnp.where(wall, 0.0, half * (k + outward(k)))
        across = kappa * (v - outward(v))
        return along - pltpu.roll(along, 1, 0) + across - pltpu.roll(across, 1, 1)

    def face(first, second, speed, kappa):
        lower = jnp.where(stator, first, second)
        upper = jnp.where(stator, second, first)
        return (jnp.maximum(speed, 0.0) + kappa) * lower + (jnp.minimum(speed, 0.0) - kappa) * upper

    sign = jnp.where(stator, 1.0, -1.0)
    speed = 0.5 * (sa0 + ga0)
    kappa = half * (k0 + g0)
    flux = sign * face(own, ghost, speed, kappa)
    shift = -flux
    ghost_new = (
        ghost
        + flux
        - sign * face(ghost, farther, 0.5 * (ga0 + ga1), half * (g0 + g1))
        - change(ghost, g0, gp0)
    )
    flux = sign * face(own_new + shift, ghost_new, speed, kappa)
    inner = 0.5 * (sa0 + sa1)
    kappa = half * (k0 + k1)
    inner = sign * jnp.where(
        stator, jnp.minimum(inner, 0.0) - kappa, jnp.maximum(inner, 0.0) + kappa
    ) * shift
    add0 = shift - change(shift, k0, sp0) + inner - flux
    add1 = -inner

    row = iota((LANES, LANES), 0)
    near_row = jnp.where(stator, LANES - 1, 0)
    far_row = jnp.where(stator, LANES - 2, 1)
    add_s[0], add_s[1] = add0, add1

    def column(i, old):
        block = jnp.where(
            row == near_row,
            add_s[0, pl.ds(i + 1, 1), :],
            jnp.where(row == far_row, add_s[1, pl.ds(i + 1, 1), :], 0.0),
        ).T
        for f in range(nfield):
            tile_s[f, i] = old(f) + block[f * SLAB + 8 : f * SLAB + 8 + radial]

    @pl.loop(2, pitch - 2, unroll=True)
    def _(i):
        column(i, lambda f: mid_ref[f, i - 2, :, near_tile])

    @pl.loop(0, 4, unroll=True)
    def _(n):
        column(jnp.where(n < 2, n, n + pitch - 4), lambda f: edge_ref[f, n, :, near_tile])

    copies.append(pltpu.make_async_copy(tile_s, o_ref.at[:, :, :, near_tile], sems.at[4]))
    copies[-1].start()
    for copy in copies:
        copy.wait()


def local(
    fields,
    diffusivity,
    mean_flow,
    radial_kernel,
    tracer_values,
    tracer_cells,
    tracer_dest,
    interface_map,
):
    npitch = lax.axis_size("pitch")
    nspan = lax.axis_size("span")
    nfield, pitch, radial, axial = fields.shape
    planes = nfield + 1
    values, tracers = tracer_values.shape
    chunks = tracers // LANES
    capacity = 2 * tracers // npitch
    edge = planes * pitch
    cells = tracer_cells.reshape(chunks, LANES)
    dest = tracer_dest.reshape(chunks, LANES)

    mean_rows = 2 * radial
    if nspan == 2:
        outs = [((2 * edge + mean_rows, axial), BF16)]
    else:
        outs = [((2 * edge, axial), BF16)] * 2 + [((mean_rows, axial), BF16)]
    inputs = [fields, diffusivity, radial_kernel, tracer_values, cells, dest, interface_map, mean_flow]
    *packed, fields, diffusivity, radial_kernel, tracer_values, cells, dest, interface_map = call(
        lambda *refs: pack_span(nspan, len(inputs), *refs),
        outs + [(x.shape, x.dtype) for x in inputs[:-1]],
        [pltpu.with_memory_space_constraint(x, pltpu.HBM) for x in inputs],
        [HBM] * len(inputs),
        [
            pltpu.VMEM(mean_flow.shape, mean_flow.dtype),
            pltpu.SemaphoreType.DMA((len(inputs) + 2,)),
        ],
        nbytes=2**20,
        fixed=True,
    )
    if nspan == 2:
        span_got = (packed[0], lax.ppermute(packed[0], "span", [(0, 1), (1, 0)]))
    else:
        span_got = (
            lax.ppermute(packed[0], "span", [(n, n + 1) for n in range(nspan - 1)]),
            lax.ppermute(packed[1], "span", [(n + 1, n) for n in range(nspan - 1)]),
            lax.all_gather(packed[2], "span"),
        )

    width = min(2 * LANES, capacity)
    sampled = call(
        lambda *refs: sample_fields(npitch, *refs),
        [
            ((8, tracers), F32),
            ((width, tracers), BF16),
            ((1, tracers), jnp.int32),
            ((axial, tracers), BF16),
        ],
        (fields, cells, dest),
        [VMEM] * 3,
        [pltpu.VMEM((nfield, pitch * radial, axial), BF16)],
        flops=4 * nfield * pitch * radial * axial * tracers,
        nbytes=2**20,
    )

    rows = radial + EXTRA
    per_slot = max(values * capacity // LANES, 2 * pitch + 3)
    per_slot = -(-per_slot // 8) * 8
    halo_rows = 2 * planes * radial + 16
    buf, up, down, speeds, halo, face = call(
        lambda *refs: dispatch(npitch, nspan, *refs),
        [
            ((npitch, 2, per_slot, LANES), BF16),
            ((halo_rows, axial), BF16),
            ((halo_rows, axial), BF16),
            ((2, rows, axial), F32),
            ((edge, EXTRA, axial), F32),
            ((per_slot, LANES), F32),
        ],
        (
            fields,
            diffusivity,
            radial_kernel,
            tracer_values,
            cells,
            interface_map,
        )
        + tuple(sampled)
        + span_got,
        [VMEM] * (10 + len(span_got)),
        [
            pltpu.VMEM(radial_kernel.shape, F32),
            pltpu.VMEM((16, tracers), F32),
            pltpu.VMEM((values * npitch * capacity // width, tracers), BF16),
            pltpu.VMEM((values, npitch * capacity // width, width), F32),
            pltpu.VMEM((per_slot, LANES), F32),
            pltpu.VMEM((2, 2 * edge, axial), F32),
        ],
        flops=2 * npitch * values * tracers * capacity,
        nbytes=2**21,
    )
    buf = lax.all_to_all(
        buf.reshape(npitch * 2, per_slot, LANES), ("pitch", "row"), 0, 0
    ).reshape(buf.shape)
    ring = [(n, (n + 1) % npitch) for n in range(npitch)]
    lower = lax.ppermute(up, "pitch", ring)
    upper = lax.ppermute(down, "pitch", [(b, a) for a, b in ring])

    mid, near_edge, new_rows = call(
        lambda *refs: middle(nspan, *refs),
        [
            ((nfield, pitch - 4, radial, axial), F32),
            ((nfield, 4, rows, axial), F32),
            ((pitch, LANES), F32),
        ],
        (fields, diffusivity, speeds, halo),
        [VMEM] * 4,
        [
            pltpu.VMEM((nfield, pitch, rows, axial), F32),
            pltpu.VMEM((7, pitch, rows, axial), F32),
        ],
        flops=2**24,
        nbytes=2**22,
    )
    outer, new_rows, beyond = call(
        lambda *refs: edges(nspan, *refs),
        [
            ((nfield, 4, radial, axial), F32),
            ((pitch, LANES), F32),
            ((8, LANES), F32),
        ],
        (fields, diffusivity, speeds, halo, lower, upper, near_edge, new_rows),
        [VMEM] * 8,
        [pltpu.VMEM((nfield, rows, axial), F32)],
        flops=2**23,
        nbytes=2**21,
    )
    return call(
        lambda *refs: interface(npitch, nspan, *refs),
        [(fields.shape, F32), ((values, npitch * capacity), F32)],
        (mid, outer, face, new_rows, beyond, buf),
        [VMEM] * 6,
        [
            pltpu.VMEM((values, npitch * capacity), F32),
            pltpu.VMEM((nfield, pitch, radial, LANES), F32),
            pltpu.VMEM((2, npitch * pitch + pitch + 8, LANES), F32),
            pltpu.VMEM((2, pitch + 8, LANES), F32),
            pltpu.SemaphoreType.DMA((5,)),
        ],
        flops=2**22,
        nbytes=2**21,
        place=ANY,
    )


def solution(mesh):
    placed = (
        P(None, "pitch", "span", "row"),
        P("pitch", "span", "row"),
        P("span", None, "row"),
        P(),
        P(None, ("pitch", "span", "row")),
        P(("pitch", "span", "row")),
        P(("pitch", "span", "row"), None),
        P("row", "pitch"),
    )
    return jax.shard_map(
        local,
        mesh=mesh,
        in_specs=placed,
        out_specs=(P(None, "pitch", "span", "row"), P(None, ("pitch", "span", "row"))),
        check_vma=False,
    )
```

time: 32.3 us -> 28.2 us (0.87)
  Pallas kernels: 13.2 us -> 8.96 us
  waiting for transfers between devices: 2.86 us -> 3.95 us
  local copies, waits for them, and re-layouts: 0.67 us -> 0 us
  starting transfers between devices: 14.6 us -> 14.2 us
    pallas_call x6, Pallas kernels: 13.2 us -> 8.96 us  [call(): pl.pallas_call(body, out_shape=tuple((shape(s, d) for s, d in outs)), in_...]
    ppermute x3, waiting for transfers between devices: 2.86 us -> 3.95 us  [the longest x1 3.41 us: local(): lower = lax.ppermute(up, 'pitch', ring)]
    unnamed x16 -> x0, local copies, waits for them, and re-layouts: 0.67 us -> none
    ppermute x3, starting transfers between devices: 8.22 us -> 7.82 us  [the longest x1 3.03 us: local(): span_got = (packed[0], lax.ppermute(packed[0], 'span', [(0, 1), (1, 0)]))]
  transfers between devices with their start and end apart: 4 -> 4, of which waited for: 2 -> 2; matrix products, arithmetic and copies ran while one was open for 0% -> 0% of each run, Pallas kernels for 25% -> 16%
where the time goes in v3:
time: 28.2 us; the launch traced here: 27.8 us
  starting transfers between devices  14.2 us (50%)
  Pallas kernels  8.96 us (32%)
  waiting for transfers between devices  3.95 us (14%)
  between operations  0.68 us (2%)
    pallas_call x6, Pallas kernels, call(): pl.pallas_call(body, out_shape=tuple((shape(s, d) for s, d in outs)), in_...  8.96 us
    all_to_all x1, starting transfers between devices, local(): lax.all_to_all(buf.reshape(npitch * 2, per_slot, LANES), ('pitch', 'row')...  6.39 us
    ppermute x1, waiting for transfers between devices, local(): lower = lax.ppermute(up, 'pitch', ring)  3.41 us
    ppermute x1, starting transfers between devices, local(): span_got = (packed[0], lax.ppermute(packed[0], 'span', [(0, 1), (1, 0)]))  3.03 us
    ppermute x1, starting transfers between devices, local(): upper = lax.ppermute(down, 'pitch', [(b, a) for a, b in ring])  2.86 us
    ppermute x1, starting transfers between devices, local(): lower = lax.ppermute(up, 'pitch', ring)  1.93 us
  transfers between devices with their start and end apart: 4, of which 2 were waited for; matrix products, arithmetic and copies ran while one was open for 0% of the time, Pallas kernels for 16%

profile of v3, /device:TPU:0, one launch (start us, length us, event | category | flops | bytes accessed | tf_op | source)
XLA Modules:
  0.0 27.8 jit_solution(9691771789493522451)
XLA Ops:
  0.6 1.4 %shard_map.95 = (bf16[160,256]{1,0:T(8,128)(2,1)S(1)}, f32[3,16,16,256]{3,2,1,0:T(8,128)S(1)}, f32[16,16,256]{2,1,0:T(8,128)S(1)}, bf16[32,32]{1,0:T(8,128)(2,1)...) custom-call(f32[3,16,16,256]{3,2,1,0:T(8,128)} %refs_0_.1, ...), custom_call_target="tpu_custom_call" | custom-call | bytes 1048576 | tf_op jit(solution)/shard_map/pallas_call | solution.py:41
  2.0 3.0 %collective-permute-start = (bf16[160,256]{1,0:T(8,128)(2,1)S(1)}, bf16[160,256]{1,0:T(8,128)(2,1)S(1)}, u32[]{:S(2)}, u32[]{:S(2)}) collective-permute-start(bf16[160,256]{1,0:T(8,128)(2,1)S(1)} %get-tuple-element.37.refs_10_), channel_id=1, source_target_pairs={{0,2},{2,0},{1,3},{3,1},{4,6},{6,4},{5,7},{7,5},{8,10},{10,8},{9,1... | collective-permute-start | bytes 245768 | tf_op jit(solution)/shard_map/ppermute | solution.py:679
  5.0 1.9 %shard_map.96 = (f32[8,2048]{1,0:T(8,128)S(1)}, bf16[256,2048]{1,0:T(8,128)(2,1)S(1)}, s32[1,2048]{1,0:T(1,128)S(1)}, bf16[256,2048]{1,0:T(8,128)(2,1)S(1)}) custom-call(f32[3,16,16,256]{3,2,1,0:T(8,128)S(1)} %get-tuple-element.26.refs_0_, s32[16,128]{1,0:T(8,128)S(1)} %get-tuple-element.30.refs_1_.refs_4_, s32[16,128]{1,0:T(8,128)S(1)} %get-tuple-element.32.refs_2_), custom_call_target="tpu_custom_call" | custom-call | flops 1610612736 | bytes 1048576 | tf_op jit(solution)/shard_map/pallas_call | solution.py:41
  6.9 0.5 %collective-permute-done.refs_11_ = bf16[160,256]{1,0:T(8,128)(2,1)S(1)} collective-permute-done((bf16[160,256]{1,0:T(8,128)(2,1)S(1)}, bf16[160,256]{1,0:T(8,128)(2,1)S(1)}, u32[]{:S(2)}, u32[]{:S(2)}) %collective-permute-start) | collective-permute-done | bytes 81952 | tf_op jit(solution)/shard_map/ppermute | solution.py:679
  7.5 1.6 %shard_map.97 = (bf16[8,2,40,128]{3,2,1,0:T(8,128)(2,1)}, bf16[144,256]{1,0:T(8,128)(2,1)S(1)}, bf16[144,256]{1,0:T(8,128)(2,1)S(1)}, f32[2,24,256]{2,1,0:T(8,12...) custom-call(f32[3,16,16,256]{3,2,1,0:T(8,128)S(1)} %get-tuple-element.26.refs_0_, ...), custom_call_target="tpu_custom_call" | custom-call | flops 167772160 | bytes 2097152 | tf_op jit(solution)/shard_map/pallas_call | solution.py:41
  9.1 6.4 %all-to-all-start = ((bf16[16,40,128]{2,1,0:T(8,128)(2,1)}), bf16[16,40,128]{2,1,0:T(8,128)(2,1)S(1)}, u32[]{:S(2)}, u32[]{:S(2)}) async-start(bf16[16,40,128]{2,1,0:T(8,128)(2,1)} %bitcast.2), calls=%async_computation | async-start | bytes 327680 | tf_op jit(solution)/shard_map/all_to_all | solution.py:739
  15.5 1.9 %collective-permute-start.1 = (bf16[144,256]{1,0:T(8,128)(2,1)S(1)}, bf16[144,256]{1,0:T(8,128)(2,1)S(1)}, u32[]{:S(2)}, u32[]{:S(2)}) collective-permute-start(bf16[144,256]{1,0:T(8,128)(2,1)S(1)} %get-tuple-element.41), channel_id=1, source_target_pairs={{0,4},{4,8},{8,12},{12,16},{16,20},{20,24},{24,28},{28,0},{1,5},{5... | collective-permute-start | bytes 221192 | tf_op jit(solution)/shard_map/ppermute | solution.py:743
  17.4 2.9 %collective-permute-start.2 = (bf16[144,256]{1,0:T(8,128)(2,1)S(1)}, bf16[144,256]{1,0:T(8,128)(2,1)S(1)}, u32[]{:S(2)}, u32[]{:S(2)}) collective-permute-start(bf16[144,256]{1,0:T(8,128)(2,1)S(1)} %get-tuple-element.42), channel_id=1, source_target_pairs={{4,0},{8,4},{12,8},{16,12},{20,16},{24,20},{28,24},{0,28},{5,1},{9... | collective-permute-start | bytes 221192 | tf_op jit(solution)/shard_map/ppermute | solution.py:744
  20.3 1.8 %shard_map.98 = (f32[3,12,16,256]{3,2,1,0:T(8,128)S(1)}, f32[3,4,24,256]{3,2,1,0:T(8,128)S(1)}, f32[16,128]{1,0:T(8,128)S(1)}) custom-call(f32[3,16,16,256]{3,2,1,0:T(8,128)S(1)} %get-tuple-element.26.refs_0_, f32[16,16,256]{2,1,0:T(8,128)S(1)} %get-tuple-element.27.refs_1_, f32[2,24,256]{2,1,0:T(8,128)S(1)} %get-tuple-element.38.refs_2_, ...), custom_call_target="tpu_custom_call" | custom-call | flops 16777216 | bytes 4194304 | tf_op jit(solution)/shard_map/pallas_call | solution.py:41
  22.1 3.4 %collective-permute-done.1.refs_4_ = bf16[144,256]{1,0:T(8,128)(2,1)S(1)} collective-permute-done((bf16[144,256]{1,0:T(8,128)(2,1)S(1)}, bf16[144,256]{1,0:T(8,128)(2,1)S(1)}, u32[]{:S(2)}, u32[]{:S(2)}) %collective-permute-start.1) | collective-permute-done | bytes 73760 | tf_op jit(solution)/shard_map/ppermute | solution.py:743
  25.6 0.0 collective-permute-done.2.refs_5_
  25.6 0.7 %shard_map.99 = (f32[3,4,16,256]{3,2,1,0:T(8,128)S(1)}, f32[16,128]{1,0:T(8,128)S(1)}, f32[8,128]{1,0:T(8,128)S(1)}) custom-call(f32[3,16,16,256]{3,2,1,0:T(8,128)S(1)} %get-tuple-element.26.refs_0_, f32[16,16,256]{2,1,0:T(8,128)S(1)} %get-tuple-element.27.refs_1_, f32[2,24,256]{2,1,0:T(8,128)S(1)} %get-tuple-element.38.refs_2_, ...), custom_call_target="tpu_custom_call" | custom-call | flops 8388608 | bytes 2097152 | tf_op jit(solution)/shard_map/pallas_call | solution.py:41
  26.3 0.0 all-to-all-done
  26.3 1.5 %shard_map.100 = (f32[3,16,16,256]{3,2,1,0:T(8,128)}, f32[10,4096]{1,0:T(8,128)}) custom-call(f32[3,12,16,256]{3,2,1,0:T(8,128)S(1)} %get-tuple-element.40.refs_0_, f32[3,4,16,256]{3,2,1,0:T(8,128)S(1)} %get-tuple-element.45.refs_1_, f32[40,128]{1,0:T(8,128)S(1)} %get-tuple-element.46.refs_2_, f32[16,128]{1,0:T(8,128)S(1)} %get-tuple-element.47.refs_3_, ...), custom_call_target="tpu_custom_call" | custom-call | flops 4194304 | bytes 2097152 | tf_op jit(solution)/shard_map/pallas_call | solution.py:41
Async XLA Ops:
  2.0 5.5 %collective-permute-start = (bf16[160,256]{1,0:T(8,128)(2,1)S(1)}, bf16[160,256]{1,0:T(8,128)(2,1)S(1)}, u32[]{:S(2)}, u32[]{:S(2)}) collective-permute-start(bf16[160,256]{1,0:T(8,128)(2,1)S(1)} %get-tuple-element.37.refs_10_), channel_id=1, source_target_pairs={{0,2},{2,0},{1,3},{3,1},{4,6},{6,4},{5,7},{7,5},{8,10},{10,8},{9,1... | collective-permute-start | bytes 245768 | tf_op jit(solution)/shard_map/ppermute | solution.py:679
  9.1 17.2 %all-to-all-start = ((bf16[16,40,128]{2,1,0:T(8,128)(2,1)}), bf16[16,40,128]{2,1,0:T(8,128)(2,1)S(1)}, u32[]{:S(2)}, u32[]{:S(2)}) async-start(bf16[16,40,128]{2,1,0:T(8,128)(2,1)} %bitcast.2), calls=%async_computation | async-start | bytes 327680 | tf_op jit(solution)/shard_map/all_to_all | solution.py:739
  15.5 10.0 %collective-permute-start.1 = (bf16[144,256]{1,0:T(8,128)(2,1)S(1)}, bf16[144,256]{1,0:T(8,128)(2,1)S(1)}, u32[]{:S(2)}, u32[]{:S(2)}) collective-permute-start(bf16[144,256]{1,0:T(8,128)(2,1)S(1)} %get-tuple-element.41), channel_id=1, source_target_pairs={{0,4},{4,8},{8,12},{12,16},{16,20},{20,24},{24,28},{28,0},{1,5},{5... | collective-permute-start | bytes 221192 | tf_op jit(solution)/shard_map/ppermute | solution.py:743
  17.4 8.1 %collective-permute-start.2 = (bf16[144,256]{1,0:T(8,128)(2,1)S(1)}, bf16[144,256]{1,0:T(8,128)(2,1)S(1)}, u32[]{:S(2)}, u32[]{:S(2)}) collective-permute-start(bf16[144,256]{1,0:T(8,128)(2,1)S(1)} %get-tuple-element.42), channel_id=1, source_target_pairs={{4,0},{8,4},{12,8},{16,12},{20,16},{24,20},{28,24},{0,28},{5,1},{9... | collective-permute-start | bytes 221192 | tf_op jit(solution)/shard_map/ppermute | solution.py:744

commit v4 on v3

--- a/solution.py
+++ b/solution.py
@@ -36,13 +36,14 @@
     return n.bit_length() - 1
 
 
-def call(body, outs, args, specs, scratch=(), flops=0, nbytes=0, place=VMEM, fixed=False):
+def call(body, outs, args, specs, scratch=(), flops=0, nbytes=0, place=VMEM, fixed=False, passed=()):
     shape = pltpu.VMEM if fixed else jax.ShapeDtypeStruct
     return pl.pallas_call(
         body,
         out_shape=tuple(shape(s, d) for s, d in outs),
         in_specs=list(specs),
-        out_specs=tuple(place for _ in outs),
+        out_specs=place if isinstance(place, tuple) else tuple(ANY if n in passed else place for n in range(len(outs))),
+        input_output_aliases={n: n for n in passed},
         scratch_shapes=list(scratch),
         compiler_params=pltpu.CompilerParams(vmem_limit_bytes=VMEM_LIMIT),
         cost_estimate=pl.CostEstimate(flops=flops, bytes_accessed=nbytes, transcendentals=0),
@@ -86,14 +87,28 @@
 
     flow = m_s[...].astype(F32)
     flow = jnp.concatenate([flow[:, 0, :], flow[:, 1, :]], 0).astype(BF16)
+    def corner(layer):
+        stator = lax.axis_index("row") == 0
+        return jnp.where(stator, layer[:, axial - LANES :], layer[:, :LANES]).astype(BF16)
+
     if nspan == 2:
         packed = edge((1 - s) * (radial - 2))
-        outs[0][: packed.shape[0]] = packed
-        outs[0][packed.shape[0] :] = flow
+        outs[1][...] = packed
+        both = packed.astype(F32)
+        half = both.shape[0] // 2
+        near = corner(jnp.where(s == 0, both[half:], both[:half]))
+        half = near.shape[0] // 2
+        outs[0][: 2 * radial] = flow
+        outs[0][2 * radial :, :LANES] = near[:half]
+        outs[0][2 * radial :, LANES : 2 * LANES] = near[half:]
     else:
-        outs[0][...] = edge(radial - 2)
-        outs[1][...] = edge(0)
-        outs[2][...] = flow
+        top, bottom = edge(radial - 2), edge(0)
+        half = top.shape[0] // 2
+        outs[0][...] = top
+        outs[1][...] = bottom
+        outs[2][...] = corner(top[half:].astype(F32))
+        outs[3][...] = corner(bottom[:half].astype(F32))
+        outs[4][...] = flow
     for copy in late:
         copy.wait()
 
@@ -182,11 +197,10 @@
     if nspan == 2:
         sent_ref, got_ref = refs[:2]
         refs = refs[2:]
-        low_ref = high_ref = got_ref
     else:
         low_ref, high_ref, all_ref = refs[:3]
         refs = refs[3:]
-    buf_ref, up_ref, down_ref, speed_ref, halo_ref, face_ref, kern_s, upd_s, lhs_s, acc_s, face_s, near_s = refs
+    buf_ref, speed_ref, face_ref, kern_s, upd_s, lhs_s, acc_s, face_s, near_s = refs
     s = lax.axis_index("span")
     q = lax.axis_index("row")
 
@@ -199,7 +213,7 @@
     smoothed = []
     for c in range(2):
         if nspan == 2:
-            at = slice(2 * edge + c * radial, 2 * edge + (c + 1) * radial)
+            at = slice(c * radial, (c + 1) * radial)
             own, other = sent_ref[at, :].astype(F32), got_ref[at, :].astype(F32)
             rows = [jnp.where(s == 0, own, other), jnp.where(s == 0, other, own)]
         else:
@@ -253,30 +267,32 @@
                 pieces.append(acc_s[:, d * groups + g, n * LANES : (n + 1) * LANES])
         buf_ref[d, q] = jnp.concatenate(pieces + filler, 0).astype(BF16)
 
-    sub = iota((EXTRA, axial), 0)
-    near_s[0] = high_ref[: 2 * edge].astype(F32)
-    near_s[1] = low_ref[: 2 * edge].astype(F32)
-
-    @pl.loop(0, edge, unroll=True)
-    def _(n):
-        tile = jnp.where(sub == 0, near_s[0, pl.ds(n, 1), :], 0.0)
-        tile = jnp.where(sub == 1, near_s[0, pl.ds(edge + n, 1), :], tile)
-        tile = jnp.where(sub == 6, near_s[1, pl.ds(n, 1), :], tile)
-        halo_ref[n] = jnp.where(sub == 7, near_s[1, pl.ds(edge + n, 1), :], tile)
+    if nspan == 2:
+        near_s[0, : edge // 2] = got_ref[2 * radial :, :LANES].astype(F32)
+        near_s[0, edge // 2 :] = got_ref[2 * radial :, LANES : 2 * LANES].astype(F32)
+        near_s[1] = near_s[0]
+    else:
+        near_s[0] = high_ref[...].astype(F32)
+        near_s[1] = low_ref[...].astype(F32)
+    sub = iota((EXTRA, LANES), 0)
+
+    def beside(n):
+        return jnp.where(
+            sub == 0, near_s[0, n : n + 1], jnp.where(sub == 7, near_s[1, n : n + 1], 0.0)
+        )
 
     stator = q == 0
     tile = pl.ds(pl.multiple_of((1 - q) * (axial - LANES), LANES), LANES)
     face_s[...] = jnp.zeros(face_s.shape, F32)
 
-    @pl.loop(0, pitch, unroll=True)
-    def _(i):
+    for i in range(pitch):
         parts = []
         for f in range(planes):
             core = f_ref[f, i, :, tile] if f < nfield else k_ref[i, :, tile]
-            parts += slab(core, halo_ref[f * pitch + i, :, tile])
+            parts += slab(core, beside(f * pitch + i))
         first, second = near(stator, parts)
-        face_s[pl.ds(i, 1), :] = first
-        face_s[pl.ds(pitch + i, 1), :] = second
+        face_s[i : i + 1] = first
+        face_s[pitch + i : pitch + i + 1] = second
 
     parts = []
     for n in range(2):
@@ -294,6 +310,22 @@
     @pl.loop(0, npitch, unroll=True)
     def _(d):
         buf_ref[d, 1 - q] = face
+
+
+def halos(low_ref, high_ref, f_ref, k_ref, halo_ref, up_ref, down_ref, near_s):
+    nfield, pitch, radial, axial = f_ref.shape
+    planes = nfield + 1
+    edge = planes * pitch
+    sub = iota((EXTRA, axial), 0)
+    near_s[0] = high_ref[: 2 * edge].astype(F32)
+    near_s[1] = low_ref[: 2 * edge].astype(F32)
+
+    @pl.loop(0, edge, unroll=True)
+    def _(n):
+        tile = jnp.where(sub == 0, near_s[0, pl.ds(n, 1), :], 0.0)
+        tile = jnp.where(sub == 1, near_s[0, pl.ds(edge + n, 1), :], tile)
+        tile = jnp.where(sub == 6, near_s[1, pl.ds(n, 1), :], tile)
+        halo_ref[n] = jnp.where(sub == 7, near_s[1, pl.ds(edge + n, 1), :], tile)
 
     def layers(ref, top):
         rows = []
@@ -404,12 +436,181 @@
         row_ref[pl.ds(i, 1), :] = near(stator, parts + [blank])[0]
 
 
-def edges(
-    nspan, f_ref, k_ref, speed_ref, halo_ref, lower_ref, upper_ref, y4_ref, row_ref, o_ref, row_out, beyond_ref, y_s
+def contribution(nspan, pitch, radial, face_ref, beyond, new_rows, window_ref):
+    planes = LANES // SLAB
+    nfield = planes - 1
+    s = lax.axis_index("span")
+    stator = lax.axis_index("row") == 0
+    count = window_ref.shape[1]
+    ghost, farther = window_ref[0], window_ref[1]
+    tail = jnp.zeros((count - pitch - 2, LANES), F32)
+    own = jnp.concatenate([beyond[0], face_ref[:pitch], beyond[1], tail], 0)
+    top = jnp.zeros((1, LANES), F32)
+    own_k1 = jnp.concatenate([top, face_ref[pitch : 2 * pitch], top, tail], 0)
+    own_new = jnp.concatenate([top, new_rows, top, tail], 0)
+    at = 2 * pitch
+
+    def groups(row, g):
+        out = row
+        for f in range(planes):
+            if f != g:
+                out = jnp.where(iota(row.shape, 1) // SLAB == f, pltpu.roll(row, (f - g) * SLAB % LANES, 1), out)
+        return out
+
+    def speeds(rows):
+        rows = TIME_STEP * rows
+        return groups(rows[0:1], 0), groups(rows[1:2], 0), groups(rows[0:1], 1)
+
+    sa0, sa1, sp0 = speeds(face_ref[at : at + 2])
+    ga0, ga1, gp0 = speeds(window_ref[2, :2])
+    shape = (count, LANES)
+    lane = iota(shape, 1)
+    group = lax.shift_right_logical(lane, power(SLAB))
+    radius = lane & (SLAB - 1)
+
+    def spread(x):
+        out = x
+        for f in range(nfield):
+            out = jnp.where(group == f, pltpu.roll(x, (f + 1) * SLAB, 1), out)
+        return out
+
+    half = 0.5 * TIME_STEP
+    k0, k1, g0, g1 = spread(own), spread(own_k1), spread(ghost), spread(farther)
+    wall = ((radius == 7 + radial) & (s == nspan - 1)) | ((radius == 7) & (s == 0))
+
+    def ahead(x):
+        return pltpu.roll(x, count - 1, 0)
+
+    def outward(x):
+        return pltpu.roll(x, LANES - 1, 1)
+
+    def change(v, k, speed):
+        kappa = half * (k + ahead(k))
+        up, dn = jnp.maximum(speed, 0.0), jnp.minimum(speed, 0.0)
+        along = (up + kappa) * v + (dn - kappa) * ahead(v)
+        kappa = jnp.where(wall, 0.0, half * (k + outward(k)))
+        across = kappa * (v - outward(v))
+        return along - pltpu.roll(along, 1, 0) + across - pltpu.roll(across, 1, 1)
+
+    def face(first, second, speed, kappa):
+        lower = jnp.where(stator, first, second)
+        upper = jnp.where(stator, second, first)
+        return (jnp.maximum(speed, 0.0) + kappa) * lower + (jnp.minimum(speed, 0.0) - kappa) * upper
+
+    sign = jnp.where(stator, 1.0, -1.0)
+    speed = 0.5 * (sa0 + ga0)
+    kappa = half * (k0 + g0)
+    flux = sign * face(own, ghost, speed, kappa)
+    shift = -flux
+    ghost_new = (
+        ghost
+        + flux
+        - sign * face(ghost, farther, 0.5 * (ga0 + ga1), half * (g0 + g1))
+        - change(ghost, g0, gp0)
+    )
+    flux = sign * face(own_new + shift, ghost_new, speed, kappa)
+    inner = 0.5 * (sa0 + sa1)
+    kappa = half * (k0 + k1)
+    inner = sign * jnp.where(
+        stator, jnp.minimum(inner, 0.0) - kappa, jnp.maximum(inner, 0.0) + kappa
+    ) * shift
+    add0 = shift - change(shift, k0, sp0) + inner - flux
+    add1 = -inner
+    return add0, add1
+
+
+def column(stator, adds, i):
+    row = iota((LANES, LANES), 0)
+    near_row = jnp.where(stator, LANES - 1, 0)
+    far_row = jnp.where(stator, LANES - 2, 1)
+    far = jnp.where(row == far_row, adds[1][i + 1 : i + 2], 0.0)
+    return jnp.where(row == near_row, adds[0][i + 1 : i + 2], far).T
+
+
+def centre(npitch, nspan, mid_ref, face_ref, row_ref, buf_ref, tile_ref, arr_ref, window_ref, ring_s):
+    nfield, inner, radial, axial = mid_ref.shape
+    pitch = inner + 4
+    q = lax.axis_index("row")
+    stator = q == 0
+    near_tile = pl.ds(pl.multiple_of((1 - q) * (axial - LANES), LANES), LANES)
+
+    values = arr_ref.shape[0]
+    capacity = arr_ref.shape[1] // npitch
+    for p in range(npitch):
+        coded = buf_ref[p, q].astype(F32)
+        plain = jnp.where(coded > 0.0, jnp.log2(coded) * (1.0 / CODE), 0.0)
+        for j in range(capacity // LANES):
+            at = p * capacity + j * LANES
+            arr_ref[:, at : at + LANES] = plain[j * values : (j + 1) * values]
+
+    whole = npitch * pitch
+    count = window_ref.shape[1]
+    for p in range(npitch):
+        both = buf_ref[p, 1 - q].astype(F32)
+        ring_s[0, p * pitch : (p + 1) * pitch] = both[:pitch]
+        ring_s[1, p * pitch : (p + 1) * pitch] = both[pitch : 2 * pitch]
+        if p == 0:
+            window_ref[2, :8] = both[2 * pitch : 2 * pitch + 8]
+    for n in range(2):
+        ring_s[n, whole : whole + pitch] = ring_s[n, :pitch]
+        ring_s[n, whole + pitch :] = ring_s[n, pitch : count]
+    begin = jnp.max(face_ref[2 * pitch + 2 : 2 * pitch + 3]).astype(jnp.int32) - 1
+    begin = jnp.where(begin < 0, begin + whole, begin)
+    window_ref[0] = ring_s[0, pl.ds(begin, count), :]
+    window_ref[1] = ring_s[1, pl.ds(begin, count), :]
+    blank = jnp.zeros((1, LANES), F32)
+    adds = contribution(
+        nspan, pitch, radial, face_ref, (blank, blank), row_ref[...], window_ref
+    )
+    for i in range(inner):
+        block = column(stator, adds, i + 2)
+        for f in range(nfield):
+            at = f * SLAB + 8
+            tile_ref[f, i] = mid_ref[f, i, :, near_tile] + block[at : at + radial]
+
+
+def finish(
+    nspan,
+    mid_ref,
+    tile_ref,
+    arr_ref,
+    f_ref,
+    k_ref,
+    speed_ref,
+    halo_ref,
+    lower_ref,
+    upper_ref,
+    y4_ref,
+    row_ref,
+    face_ref,
+    window_ref,
+    out_ref,
+    arr_out,
+    y_s,
+    o_s,
+    row_s,
+    sems,
 ):
     nfield, pitch, radial, axial = f_ref.shape
     planes = nfield + 1
     stator = lax.axis_index("row") == 0
+    q = lax.axis_index("row")
+    near_tile = pl.ds(pl.multiple_of((1 - q) * (axial - LANES), LANES), LANES)
+    copies = [
+        pltpu.make_async_copy(arr_ref, arr_out, sems.at[2]),
+        pltpu.make_async_copy(
+            tile_ref, out_ref.at[:, 2 : pitch - 2, :, near_tile], sems.at[3]
+        ),
+    ]
+    if axial > LANES:
+        rest = pl.ds(pl.multiple_of(q * LANES, LANES), axial - LANES)
+        copies.append(
+            pltpu.make_async_copy(
+                mid_ref.at[:, :, :, rest], out_ref.at[:, 2 : pitch - 2, :, rest], sems.at[4]
+            )
+        )
+    for copy in copies:
+        copy.start()
     faces = Faces(nspan, speed_ref, radial)
     ext = {-1: lower_ref[...].astype(F32), 1: upper_ref[...].astype(F32)}
     sub = iota((EXTRA, axial), 0)
@@ -428,8 +629,8 @@
             extra = jnp.where(sub == 7, side[corner + 1 : corner + 2], extra)
         return jnp.concatenate([side[at : at + radial], extra], 0)
 
-    row_out[...] = row_ref[...]
-    beyond_ref[...] = jnp.zeros(beyond_ref.shape, F32)
+    row_s[...] = row_ref[...]
+    beyond = []
     tile = pl.ds(pl.multiple_of(lax.axis_index("row") * (LANES - axial) + axial - LANES, LANES), LANES)
 
     def edge_lanes(value):
@@ -447,191 +648,32 @@
             for i in new:
                 y[i] = faces.step(w[i], x[i - 1], x[i], x[i + 1])
             for n, i in enumerate(done):
-                o_ref[f, 2 * side + n] = faces.step(w[i], y[i - 1], y[i], y[i + 1])[:radial]
+                o_s[f, 2 * side + n] = faces.step(w[i], y[i - 1], y[i], y[i + 1])[:radial]
             y_s[f] = y[0 if side == 0 else pitch - 1]
         parts = []
         for f in range(nfield):
             parts += slab(y_s[f, :radial, tile], y_s[f, radial:, tile])
         i = 0 if side == 0 else pitch - 1
-        row_out[i : i + 1] = near(stator, parts + [blank])[0]
+        row_s[i : i + 1] = near(stator, parts + [blank])[0]
         parts = []
         for f in range(planes):
             value = edge_lanes(state(f, -1 if side == 0 else pitch))
             parts += slab(value[:radial], value[radial:])
-        beyond_ref[side : side + 1] = near(stator, parts)[0]
-
-
-def interface(
-    npitch,
-    nspan,
-    mid_ref,
-    edge_ref,
-    face_ref,
-    row_ref,
-    beyond_ref,
-    buf_ref,
-    o_ref,
-    arr_ref,
-    arr_s,
-    tile_s,
-    ring_s,
-    add_s,
-    sems,
-):
-    nfield, pitch, radial, axial = o_ref.shape
-    planes = nfield + 1
-    s = lax.axis_index("span")
-    q = lax.axis_index("row")
-    stator = q == 0
-    near_tile = pl.ds(pl.multiple_of((1 - q) * (axial - LANES), LANES), LANES)
-    copies = []
-    if axial > LANES:
-        rest = pl.ds(pl.multiple_of(q * LANES, LANES), axial - LANES)
-        copies += [
+        beyond.append(near(stator, parts)[0])
+    adds = contribution(nspan, pitch, radial, face_ref, beyond, row_s[...], window_ref)
+    for side in range(2):
+        first = side * (pitch - 2)
+        for n in range(2):
+            block = column(stator, adds, first + n)
+            for f in range(nfield):
+                at = f * SLAB + 8
+                o_s[f, 2 * side + n, :, tile] += block[at : at + radial]
+        copies.append(
             pltpu.make_async_copy(
-                mid_ref.at[:, :, :, rest], o_ref.at[:, 2 : pitch - 2, :, rest], sems.at[0]
-            ),
-            pltpu.make_async_copy(
-                edge_ref.at[:, :2, :, rest], o_ref.at[:, :2, :, rest], sems.at[1]
-            ),
-            pltpu.make_async_copy(
-                edge_ref.at[:, 2:, :, rest], o_ref.at[:, pitch - 2 :, :, rest], sems.at[2]
-            ),
-        ]
-    for copy in copies:
-        copy.start()
-
-    values = arr_ref.shape[0]
-    capacity = arr_ref.shape[1] // npitch
-
-    @pl.loop(0, npitch, unroll=True)
-    def _(p):
-        coded = buf_ref[p, q].astype(F32)
-        plain = jnp.where(coded > 0.0, jnp.log2(coded) * (1.0 / CODE), 0.0)
-        for j in range(capacity // LANES):
-            at = pl.ds(pl.multiple_of(p * capacity + j * LANES, LANES), LANES)
-            arr_s[:, at] = plain[j * values : (j + 1) * values]
-
-    copies.append(pltpu.make_async_copy(arr_s, arr_ref, sems.at[3]))
-    copies[-1].start()
-
-    whole = npitch * pitch
-    count = pitch + 8
-
-    @pl.loop(0, npitch, unroll=True)
-    def _(p):
-        at = pl.ds(pl.multiple_of(p * pitch, pitch), pitch)
-        both = buf_ref[p, 1 - q].astype(F32)
-        ring_s[0, at, :] = both[:pitch]
-        ring_s[1, at, :] = both[pitch : 2 * pitch]
-
-    for n in range(2):
-        ring_s[n, whole : whole + pitch] = ring_s[n, :pitch]
-        ring_s[n, whole + pitch :] = ring_s[n, pitch : pitch + 8]
-    begin = jnp.max(face_ref[2 * pitch + 2 : 2 * pitch + 3]).astype(jnp.int32) - 1
-    begin = jnp.where(begin < 0, begin + whole, begin)
-    ghost = ring_s[0, pl.ds(begin, count), :]
-    farther = ring_s[1, pl.ds(begin, count), :]
-    tail = jnp.zeros((count - pitch - 2, LANES), F32)
-    own = jnp.concatenate(
-        [beyond_ref[0:1], face_ref[:pitch], beyond_ref[1:2], tail], 0
-    )
-    top = jnp.zeros((1, LANES), F32)
-    own_k1 = jnp.concatenate([top, face_ref[pitch : 2 * pitch], top, tail], 0)
-    own_new = jnp.concatenate([top, row_ref[...], top, tail], 0)
-    at = 2 * pitch
-
-    def groups(row, g):
-        out = row
-        for f in range(planes):
-            if f != g:
-                out = jnp.where(iota(row.shape, 1) // SLAB == f, pltpu.roll(row, (f - g) * SLAB % LANES, 1), out)
-        return out
-
-    def speeds(rows):
-        rows = TIME_STEP * rows
-        return groups(rows[0:1], 0), groups(rows[1:2], 0), groups(rows[0:1], 1)
-
-    sa0, sa1, sp0 = speeds(face_ref[at : at + 2])
-    ga0, ga1, gp0 = speeds(buf_ref[0, 1 - q].astype(F32)[at : at + 2])
-    shape = (count, LANES)
-    lane = iota(shape, 1)
-    group = lax.shift_right_logical(lane, power(SLAB))
-    radius = lane & (SLAB - 1)
-
-    def spread(x):
-        out = x
-        for f in range(nfield):
-            out = jnp.where(group == f, pltpu.roll(x, (f + 1) * SLAB, 1), out)
-        return out
-
-    half = 0.5 * TIME_STEP
-    k0, k1, g0, g1 = spread(own), spread(own_k1), spread(ghost), spread(farther)
-    wall = ((radius == 7 + radial) & (s == nspan - 1)) | ((radius == 7) & (s == 0))
-
-    def ahead(x):
-        return pltpu.roll(x, count - 1, 0)
-
-    def outward(x):
-        return pltpu.roll(x, LANES - 1, 1)
-
-    def change(v, k, speed):
-        kappa = half * (k + ahead(k))
-        up, dn = jnp.maximum(speed, 0.0), jnp.minimum(speed, 0.0)
-        along = (up + kappa) * v + (dn - kappa) * ahead(v)
-        kappa = jnp.where(wall, 0.0, half * (k + outward(k)))
-        across = kappa * (v - outward(v))
-        return along - pltpu.roll(along, 1, 0) + across - pltpu.roll(across, 1, 1)
-
-    def face(first, second, speed, kappa):
-        lower = jnp.where(stator, first, second)
-        upper = jnp.where(stator, second, first)
-        return (jnp.maximum(speed, 0.0) + kappa) * lower + (jnp.minimum(speed, 0.0) - kappa) * upper
-
-    sign = jnp.where(stator, 1.0, -1.0)
-    speed = 0.5 * (sa0 + ga0)
-    kappa = half * (k0 + g0)
-    flux = sign * face(own, ghost, speed, kappa)
-    shift = -flux
-    ghost_new = (
-        ghost
-        + flux
-        - sign * face(ghost, farther, 0.5 * (ga0 + ga1), half * (g0 + g1))
-        - change(ghost, g0, gp0)
-    )
-    flux = sign * face(own_new + shift, ghost_new, speed, kappa)
-    inner = 0.5 * (sa0 + sa1)
-    kappa = half * (k0 + k1)
-    inner = sign * jnp.where(
-        stator, jnp.minimum(inner, 0.0) - kappa, jnp.maximum(inner, 0.0) + kappa
-    ) * shift
-    add0 = shift - change(shift, k0, sp0) + inner - flux
-    add1 = -inner
-
-    row = iota((LANES, LANES), 0)
-    near_row = jnp.where(stator, LANES - 1, 0)
-    far_row = jnp.where(stator, LANES - 2, 1)
-    add_s[0], add_s[1] = add0, add1
-
-    def column(i, old):
-        block = jnp.where(
-            row == near_row,
-            add_s[0, pl.ds(i + 1, 1), :],
-            jnp.where(row == far_row, add_s[1, pl.ds(i + 1, 1), :], 0.0),
-        ).T
-        for f in range(nfield):
-            tile_s[f, i] = old(f) + block[f * SLAB + 8 : f * SLAB + 8 + radial]
-
-    @pl.loop(2, pitch - 2, unroll=True)
-    def _(i):
-        column(i, lambda f: mid_ref[f, i - 2, :, near_tile])
-
-    @pl.loop(0, 4, unroll=True)
-    def _(n):
-        column(jnp.where(n < 2, n, n + pitch - 4), lambda f: edge_ref[f, n, :, near_tile])
-
-    copies.append(pltpu.make_async_copy(tile_s, o_ref.at[:, :, :, near_tile], sems.at[4]))
-    copies[-1].start()
+                o_s.at[:, 2 * side : 2 * side + 2], out_ref.at[:, first : first + 2], sems.at[side]
+            )
+        )
+        copies[-1].start()
     for copy in copies:
         copy.wait()
 
@@ -659,9 +701,10 @@
 
     mean_rows = 2 * radial
     if nspan == 2:
-        outs = [((2 * edge + mean_rows, axial), BF16)]
+        outs = [((mean_rows + edge // 2, axial), BF16), ((2 * edge, axial), BF16)]
     else:
-        outs = [((2 * edge, axial), BF16)] * 2 + [((mean_rows, axial), BF16)]
+        outs = [((2 * edge, axial), BF16)] * 2 + [((edge, LANES), BF16)] * 2
+        outs += [((mean_rows, axial), BF16)]
     inputs = [fields, diffusivity, radial_kernel, tracer_values, cells, dest, interface_map, mean_flow]
     *packed, fields, diffusivity, radial_kernel, tracer_values, cells, dest, interface_map = call(
         lambda *refs: pack_span(nspan, len(inputs), *refs),
@@ -676,12 +719,17 @@
         fixed=True,
     )
     if nspan == 2:
-        span_got = (packed[0], lax.ppermute(packed[0], "span", [(0, 1), (1, 0)]))
+        swap = [(0, 1), (1, 0)]
+        span_got = (packed[0], lax.ppermute(packed[0], "span", swap))
+        low = high = lax.ppermute(packed[1], "span", swap)
     else:
+        upward = [(n, n + 1) for n in range(nspan - 1)]
+        downward = [(n + 1, n) for n in range(nspan - 1)]
+        low, high = lax.ppermute(packed[0], "span", upward), lax.ppermute(packed[1], "span", downward)
         span_got = (
-            lax.ppermute(packed[0], "span", [(n, n + 1) for n in range(nspan - 1)]),
-            lax.ppermute(packed[1], "span", [(n + 1, n) for n in range(nspan - 1)]),
-            lax.all_gather(packed[2], "span"),
+            lax.ppermute(packed[2], "span", upward),
+            lax.ppermute(packed[3], "span", downward),
+            lax.all_gather(packed[4], "span"),
         )
 
     width = min(2 * LANES, capacity)
@@ -704,14 +752,11 @@
     per_slot = max(values * capacity // LANES, 2 * pitch + 3)
     per_slot = -(-per_slot // 8) * 8
     halo_rows = 2 * planes * radial + 16
-    buf, up, down, speeds, halo, face = call(
+    buf, speeds, face = call(
         lambda *refs: dispatch(npitch, nspan, *refs),
         [
             ((npitch, 2, per_slot, LANES), BF16),
-            ((halo_rows, axial), BF16),
-            ((halo_rows, axial), BF16),
             ((2, rows, axial), F32),
-            ((edge, EXTRA, axial), F32),
             ((per_slot, LANES), F32),
         ],
         (
@@ -731,10 +776,20 @@
             pltpu.VMEM((values * npitch * capacity // width, tracers), BF16),
             pltpu.VMEM((values, npitch * capacity // width, width), F32),
             pltpu.VMEM((per_slot, LANES), F32),
-            pltpu.VMEM((2, 2 * edge, axial), F32),
+            pltpu.VMEM((2, edge, LANES), F32),
         ],
         flops=2 * npitch * values * tracers * capacity,
         nbytes=2**21,
+    )
+    buf, halo, up, down = call(
+        lambda *refs: halos(*refs[1:5], *refs[6:]),
+        [((npitch, 2, per_slot, LANES), BF16), ((edge, EXTRA, axial), F32)]
+        + [((halo_rows, axial), BF16)] * 2,
+        (buf, low, high, fields, diffusivity),
+        [ANY] + [VMEM] * 4,
+        [pltpu.VMEM((2, 2 * edge, axial), F32)],
+        nbytes=2**18,
+        passed=(0,),
     )
     buf = lax.all_to_all(
         buf.reshape(npitch * 2, per_slot, LANES), ("pitch", "row"), 0, 0
@@ -759,32 +814,46 @@
         flops=2**24,
         nbytes=2**22,
     )
-    outer, new_rows, beyond = call(
-        lambda *refs: edges(nspan, *refs),
+    near_mid, arrived, window = call(
+        lambda *refs: centre(npitch, nspan, *refs),
         [
-            ((nfield, 4, radial, axial), F32),
-            ((pitch, LANES), F32),
-            ((8, LANES), F32),
+            ((nfield, pitch - 4, radial, LANES), F32),
+            ((values, npitch * capacity), F32),
+            ((3, pitch + 8, LANES), F32),
         ],
-        (fields, diffusivity, speeds, halo, lower, upper, near_edge, new_rows),
-        [VMEM] * 8,
-        [pltpu.VMEM((nfield, rows, axial), F32)],
-        flops=2**23,
+        (mid, face, new_rows, buf),
+        [VMEM] * 4,
+        [pltpu.VMEM((2, npitch * pitch + pitch + 8, LANES), F32)],
+        flops=2**22,
         nbytes=2**21,
+        fixed=True,
     )
     return call(
-        lambda *refs: interface(npitch, nspan, *refs),
-        [(fields.shape, F32), ((values, npitch * capacity), F32)],
-        (mid, outer, face, new_rows, beyond, buf),
-        [VMEM] * 6,
+        lambda *refs: finish(nspan, *refs),
+        [(fields.shape, F32), (arrived.shape, F32)],
+        (
+            mid,
+            near_mid,
+            arrived,
+            fields,
+            diffusivity,
+            speeds,
+            halo,
+            lower,
+            upper,
+            near_edge,
+            new_rows,
+            face,
+            window,
+        ),
+        [VMEM] * 13,
         [
-            pltpu.VMEM((values, npitch * capacity), F32),
-            pltpu.VMEM((nfield, pitch, radial, LANES), F32),
-            pltpu.VMEM((2, npitch * pitch + pitch + 8, LANES), F32),
-            pltpu.VMEM((2, pitch + 8, LANES), F32),
+            pltpu.VMEM((nfield, rows, axial), F32),
+            pltpu.VMEM((nfield, 4, radial, axial), F32),
+            pltpu.VMEM((pitch, LANES), F32),
             pltpu.SemaphoreType.DMA((5,)),
         ],
-        flops=2**22,
+        flops=2**23,
         nbytes=2**21,
         place=ANY,
     )

time: 28.2 us -> 27.5 us (0.975)
  waiting for transfers between devices: 3.95 us -> 3.46 us
  starting transfers between devices: 14.2 us -> 13.8 us
    ppermute x1, waiting for transfers between devices: 3.41 us -> 0.46 us  [local(): lower = lax.ppermute(up, 'pitch', ring)]
    all_to_all x1, waiting for transfers between devices: 0.01 us -> 2.3 us  [local(): lax.all_to_all(buf.reshape(npitch * 2, per_slot, LANES), ('pitch', 'row')...]
    all_to_all x1, starting transfers between devices: 6.39 us -> 5.92 us  [local(): lax.all_to_all(buf.reshape(npitch * 2, per_slot, LANES), ('pitch', 'row')...]
    pallas_call x6 -> x7, Pallas kernels: 8.96 us -> 9.16 us  [call(): pl.pallas_call(body, out_shape=tuple((shape(s, d) for s, d in outs)), in_...]
    ppermute x1 -> x2, waiting for transfers between devices: 0.54 us -> 0.7 us  [the longest x1 0.7 us: local(): low = high = lax.ppermute(packed[1], 'span', swap)]
    ppermute x1 -> x2, starting transfers between devices: 3.03 us -> 3.11 us  [the longest x1 3.03 us: local(): span_got = (packed[0], lax.ppermute(packed[0], 'span', swap))]
  transfers between devices with their start and end apart: 4 -> 5, of which waited for: 2 -> 3; matrix products, arithmetic and copies ran while one was open for 0% -> 0% of each run, Pallas kernels for 16% -> 22%
where the time goes in v4:
time: 27.5 us; the launch traced here: 27.1 us
  starting transfers between devices  13.8 us (50%)
  Pallas kernels  9.16 us (33%)
  waiting for transfers between devices  3.46 us (13%)
  between operations  0.69 us (3%)
    pallas_call x7, Pallas kernels, call(): pl.pallas_call(body, out_shape=tuple((shape(s, d) for s, d in outs)), in_...  9.16 us
    all_to_all x1, starting transfers between devices, local(): lax.all_to_all(buf.reshape(npitch * 2, per_slot, LANES), ('pitch', 'row')...  5.92 us
    ppermute x1, starting transfers between devices, local(): span_got = (packed[0], lax.ppermute(packed[0], 'span', swap))  3.03 us
    ppermute x1, starting transfers between devices, local(): upper = lax.ppermute(down, 'pitch', [(b, a) for a, b in ring])  2.86 us
    all_to_all x1, waiting for transfers between devices, local(): lax.all_to_all(buf.reshape(npitch * 2, per_slot, LANES), ('pitch', 'row')...  2.3 us
    ppermute x1, starting transfers between devices, local(): lower = lax.ppermute(up, 'pitch', ring)  1.93 us
    ppermute x1, waiting for transfers between devices, local(): low = high = lax.ppermute(packed[1], 'span', swap)  0.7 us
  transfers between devices with their start and end apart: 5, of which 3 were waited for; matrix products, arithmetic and copies ran while one was open for 0% of the time, Pallas kernels for 22%

profile of v4, /device:TPU:0, one launch (start us, length us, event | category | flops | bytes accessed | tf_op | source)
XLA Modules:
  0.0 27.1 jit_solution(447183531647363932)
XLA Ops:
  0.6 1.4 %shard_map.95 = (bf16[64,256]{1,0:T(8,128)(2,1)S(1)}, bf16[128,256]{1,0:T(8,128)(2,1)S(1)}, f32[3,16,16,256]{3,2,1,0:T(8,128)S(1)}, f32[16,16,256]{2,1,0:T(8,128...) custom-call(f32[3,16,16,256]{3,2,1,0:T(8,128)} %refs_0_.1, ...), custom_call_target="tpu_custom_call" | custom-call | bytes 1048576 | tf_op jit(solution)/shard_map/pallas_call | solution.py:41
  2.0 3.0 %collective-permute-start = (bf16[64,256]{1,0:T(8,128)(2,1)S(1)}, bf16[64,256]{1,0:T(8,128)(2,1)S(1)}, u32[]{:S(2)}, u32[]{:S(2)}) collective-permute-start(bf16[64,256]{1,0:T(8,128)(2,1)S(1)} %get-tuple-element.39.refs_10_), channel_id=1, source_target_pairs={{0,2},{2,0},{1,3},{3,1},{4,6},{6,4},{5,7},{7,5},{8,10},{10,8},{9,1... | collective-permute-start | bytes 98312 | tf_op jit(solution)/shard_map/ppermute | solution.py:723
  5.0 0.1 collective-permute-start.1
  5.1 1.9 %shard_map.96 = (f32[8,2048]{1,0:T(8,128)S(1)}, bf16[256,2048]{1,0:T(8,128)(2,1)S(1)}, s32[1,2048]{1,0:T(1,128)S(1)}, bf16[256,2048]{1,0:T(8,128)(2,1)S(1)}) custom-call(f32[3,16,16,256]{3,2,1,0:T(8,128)S(1)} %get-tuple-element.28.refs_0_.refs_3_, s32[16,128]{1,0:T(8,128)S(1)} %get-tuple-element.32.refs_1_.refs_4_, s32[16,128]{1,0:T(8,128)S(1)} %get-tuple-element.34.refs_2_), custom_call_target="tpu_custom_call" | custom-call | flops 1610612736 | bytes 1048576 | tf_op jit(solution)/shard_map/pallas_call | solution.py:41
  7.0 0.0 collective-permute-done.refs_11_
  7.0 1.6 %shard_map.97 = (bf16[8,2,40,128]{3,2,1,0:T(8,128)(2,1)}, f32[2,24,256]{2,1,0:T(8,128)S(1)}, f32[40,128]{1,0:T(8,128)S(1)}) custom-call(f32[3,16,16,256]{3,2,1,0:T(8,128)S(1)} %get-tuple-element.28.refs_0_.refs_3_, f32[16,16,256]{2,1,0:T(8,128)S(1)} %get-tuple-element.29.refs_1_.refs_4_, bf16[32,32]{1,0:T(8,128)(2,1)S(1)} %get-tuple-element.30.refs_2_, ...), custom_call_target="tpu_custom_call" | custom-call | flops 167772160 | bytes 2097152 | tf_op jit(solution)/shard_map/pallas_call | solution.py:41
  8.6 0.7 %collective-permute-done.1.refs_1_.refs_2_ = bf16[128,256]{1,0:T(8,128)(2,1)S(1)} collective-permute-done((bf16[128,256]{1,0:T(8,128)(2,1)S(1)}, bf16[128,256]{1,0:T(8,128)(2,1)S(1)}, u32[]{:S(2)}, u32[]{:S(2)}) %collective-permute-start.1) | collective-permute-done | bytes 65568 | tf_op jit(solution)/shard_map/ppermute | solution.py:724
  9.3 0.2 shard_map.98
  9.5 5.9 %all-to-all-start = ((bf16[16,40,128]{2,1,0:T(8,128)(2,1)}), bf16[16,40,128]{2,1,0:T(8,128)(2,1)S(1)}, u32[]{:S(2)}, u32[]{:S(2)}) async-start(bf16[16,40,128]{2,1,0:T(8,128)(2,1)} %bitcast.2), calls=%async_computation | async-start | bytes 327680 | tf_op jit(solution)/shard_map/all_to_all | solution.py:794
  15.4 1.9 %collective-permute-start.2 = (bf16[144,256]{1,0:T(8,128)(2,1)S(1)}, bf16[144,256]{1,0:T(8,128)(2,1)S(1)}, u32[]{:S(2)}, u32[]{:S(2)}) collective-permute-start(bf16[144,256]{1,0:T(8,128)(2,1)S(1)} %get-tuple-element.50), channel_id=1, source_target_pairs={{0,4},{4,8},{8,12},{12,16},{16,20},{20,24},{24,28},{28,0},{1,5},{5... | collective-permute-start | bytes 221192 | tf_op jit(solution)/shard_map/ppermute | solution.py:798
  17.3 2.9 %collective-permute-start.3 = (bf16[144,256]{1,0:T(8,128)(2,1)S(1)}, bf16[144,256]{1,0:T(8,128)(2,1)S(1)}, u32[]{:S(2)}, u32[]{:S(2)}) collective-permute-start(bf16[144,256]{1,0:T(8,128)(2,1)S(1)} %get-tuple-element.51), channel_id=1, source_target_pairs={{4,0},{8,4},{12,8},{16,12},{20,16},{24,20},{28,24},{0,28},{5,1},{9... | collective-permute-start | bytes 221192 | tf_op jit(solution)/shard_map/ppermute | solution.py:799
  20.2 1.8 %shard_map.99 = (f32[3,12,16,256]{3,2,1,0:T(8,128)S(1)}, f32[3,4,24,256]{3,2,1,0:T(8,128)S(1)}, f32[16,128]{1,0:T(8,128)S(1)}) custom-call(f32[3,16,16,256]{3,2,1,0:T(8,128)S(1)} %get-tuple-element.28.refs_0_.refs_3_, f32[16,16,256]{2,1,0:T(8,128)S(1)} %get-tuple-element.29.refs_1_.refs_4_, f32[2,24,256]{2,1,0:T(8,128)S(1)} %get-tuple-element.40.refs_2_.refs_5_, ...), custom_call_target="tpu_custom_call" | custom-call | flops 16777216 | bytes 4194304 | tf_op jit(solution)/shard_map/pallas_call | solution.py:41
  22.0 2.3 %all-to-all-done = bf16[16,40,128]{2,1,0:T(8,128)(2,1)S(1)} async-done(((bf16[16,40,128]{2,1,0:T(8,128)(2,1)}), bf16[16,40,128]{2,1,0:T(8,128)(2,1)S(1)}, u32[]{:S(2)}, u32[]{:S(2)}) %all-to-all-start) | async-done | bytes 163872 | tf_op jit(solution)/shard_map/all_to_all | solution.py:794
  24.3 0.6 %shard_map.100 = (f32[3,12,16,128]{3,2,1,0:T(8,128)S(1)}, f32[10,4096]{1,0:T(8,128)S(1)}, f32[3,24,128]{2,1,0:T(8,128)S(1)}) custom-call(f32[3,12,16,256]{3,2,1,0:T(8,128)S(1)} %get-tuple-element.44.refs_0_, f32[40,128]{1,0:T(8,128)S(1)} %get-tuple-element.45.refs_1_.refs_11_, f32[16,128]{1,0:T(8,128)S(1)} %get-tuple-element.46.refs_2_.refs_10_, ...), custom_call_target="tpu_custom_call" | custom-call | flops 4194304 | bytes 2097152 | tf_op jit(solution)/shard_map/pallas_call | solution.py:41
  25.0 0.5 %collective-permute-done.2.refs_7_ = bf16[144,256]{1,0:T(8,128)(2,1)S(1)} collective-permute-done((bf16[144,256]{1,0:T(8,128)(2,1)S(1)}, bf16[144,256]{1,0:T(8,128)(2,1)S(1)}, u32[]{:S(2)}, u32[]{:S(2)}) %collective-permute-start.2) | collective-permute-done | bytes 73760 | tf_op jit(solution)/shard_map/ppermute | solution.py:798
  25.4 0.0 collective-permute-done.3.refs_8_
  25.4 1.7 %shard_map.101 = (f32[3,16,16,256]{3,2,1,0:T(8,128)}, f32[10,4096]{1,0:T(8,128)}) custom-call(f32[3,12,16,256]{3,2,1,0:T(8,128)S(1)} %get-tuple-element.44.refs_0_, f32[3,12,16,128]{3,2,1,0:T(8,128)S(1)} %get-tuple-element.48.refs_1_, f32[10,4096]{1,0:T(8,128)S(1)} %get-tuple-element.49.refs_2_, f32[3,16,16,256]{3,2,1,0:T(8,128)S(1)} %get-tuple-element.28.refs_0_.refs_3_, ...), custom_call_target="tpu_custom_call" | custom-call | flops 8388608 | bytes 2097152 | tf_op jit(solution)/shard_map/pallas_call | solution.py:41
Async XLA Ops:
  2.0 5.0 %collective-permute-start = (bf16[64,256]{1,0:T(8,128)(2,1)S(1)}, bf16[64,256]{1,0:T(8,128)(2,1)S(1)}, u32[]{:S(2)}, u32[]{:S(2)}) collective-permute-start(bf16[64,256]{1,0:T(8,128)(2,1)S(1)} %get-tuple-element.39.refs_10_), channel_id=1, source_target_pairs={{0,2},{2,0},{1,3},{3,1},{4,6},{6,4},{5,7},{7,5},{8,10},{10,8},{9,1... | collective-permute-start | bytes 98312 | tf_op jit(solution)/shard_map/ppermute | solution.py:723
  5.0 4.3 %collective-permute-start.1 = (bf16[128,256]{1,0:T(8,128)(2,1)S(1)}, bf16[128,256]{1,0:T(8,128)(2,1)S(1)}, u32[]{:S(2)}, u32[]{:S(2)}) collective-permute-start(bf16[128,256]{1,0:T(8,128)(2,1)S(1)} %get-tuple-element.42), channel_id=1, source_target_pairs={{0,2},{2,0},{1,3},{3,1},{4,6},{6,4},{5,7},{7,5},{8,10},{10,8},{9,1... | collective-permute-start | bytes 196616 | tf_op jit(solution)/shard_map/ppermute | solution.py:724
  9.5 14.9 %all-to-all-start = ((bf16[16,40,128]{2,1,0:T(8,128)(2,1)}), bf16[16,40,128]{2,1,0:T(8,128)(2,1)S(1)}, u32[]{:S(2)}, u32[]{:S(2)}) async-start(bf16[16,40,128]{2,1,0:T(8,128)(2,1)} %bitcast.2), calls=%async_computation | async-start | bytes 327680 | tf_op jit(solution)/shard_map/all_to_all | solution.py:794
  15.4 10.0 %collective-permute-start.2 = (bf16[144,256]{1,0:T(8,128)(2,1)S(1)}, bf16[144,256]{1,0:T(8,128)(2,1)S(1)}, u32[]{:S(2)}, u32[]{:S(2)}) collective-permute-start(bf16[144,256]{1,0:T(8,128)(2,1)S(1)} %get-tuple-element.50), channel_id=1, source_target_pairs={{0,4},{4,8},{8,12},{12,16},{16,20},{20,24},{24,28},{28,0},{1,5},{5... | collective-permute-start | bytes 221192 | tf_op jit(solution)/shard_map/ppermute | solution.py:798
  17.3 8.1 %collective-permute-start.3 = (bf16[144,256]{1,0:T(8,128)(2,1)S(1)}, bf16[144,256]{1,0:T(8,128)(2,1)S(1)}, u32[]{:S(2)}, u32[]{:S(2)}) collective-permute-start(bf16[144,256]{1,0:T(8,128)(2,1)S(1)} %get-tuple-element.51), channel_id=1, source_target_pairs={{4,0},{8,4},{12,8},{16,12},{20,16},{24,20},{28,24},{0,28},{5,1},{9... | collective-permute-start | bytes 221192 | tf_op jit(solution)/shard_map/ppermute | solution.py:799

commit v5 on v4

--- a/solution.py
+++ b/solution.py
@@ -38,12 +38,13 @@
 
 def call(body, outs, args, specs, scratch=(), flops=0, nbytes=0, place=VMEM, fixed=False, passed=()):
     shape = pltpu.VMEM if fixed else jax.ShapeDtypeStruct
+    passed = dict(passed)
     return pl.pallas_call(
         body,
         out_shape=tuple(shape(s, d) for s, d in outs),
         in_specs=list(specs),
-        out_specs=place if isinstance(place, tuple) else tuple(ANY if n in passed else place for n in range(len(outs))),
-        input_output_aliases={n: n for n in passed},
+        out_specs=place if isinstance(place, tuple) else (place,) * len(outs),
+        input_output_aliases=passed,
         scratch_shapes=list(scratch),
         compiler_params=pltpu.CompilerParams(vmem_limit_bytes=VMEM_LIMIT),
         cost_estimate=pl.CostEstimate(flops=flops, bytes_accessed=nbytes, transcendentals=0),
@@ -395,7 +396,7 @@
         return (a + b) + (c + w[6] * before)
 
 
-def middle(nspan, f_ref, k_ref, speed_ref, halo_ref, o_ref, y4_ref, row_ref, y_s, w_s):
+def middle(nspan, f_ref, k_ref, speed_ref, halo_ref, out_ref, o_ref, y2_ref, part_ref, outer_ref, row_ref, y_s, w_s, sem):
     nfield, pitch, radial, axial = f_ref.shape
     stator = lax.axis_index("row") == 0
     faces = Faces(nspan, speed_ref, radial)
@@ -420,9 +421,31 @@
         for f in range(nfield):
             o_ref[f, i - 2] = faces.step(w, y_s[f, i - 1], y_s[f, i], y_s[f, i + 1])[:radial]
 
+    copies = []
+    if axial > LANES:
+        rest = pl.ds(pl.multiple_of(lax.axis_index("row") * LANES, LANES), axial - LANES)
+        copies.append(
+            pltpu.make_async_copy(
+                o_ref.at[:, :, :, rest], out_ref.at[:, 2 : pitch - 2, :, rest], sem.at[0]
+            )
+        )
+        copies[-1].start()
+    k = [kappa(i) for i in (0, 1, pitch - 2, pitch - 1)]
+    ends = faces.weights(-k[0], k[0], k[1]), faces.weights(k[2], k[3], -k[3])
+    for n, value in enumerate(ends[0]):
+        outer_ref[0, n] = value
+    for n, value in enumerate(ends[1]):
+        outer_ref[1, n] = value
+    outer_ref[0, 7] = w_s[6, 1]
+    outer_ref[1, 7] = w_s[5, pitch - 2]
+    none = jnp.zeros((faces.rows, axial), F32)
+    inner = [[w_s[n, i] for n in range(7)] for i in (1, pitch - 2)]
     for f in range(nfield):
-        for n, i in enumerate((1, 2, pitch - 3, pitch - 2)):
-            y4_ref[f, n] = y_s[f, i]
+        y2_ref[f, 0], y2_ref[f, 1] = y_s[f, 1], y_s[f, pitch - 2]
+        part_ref[f, 0] = faces.step(ends[0], none, state(f, 0), state(f, 1))
+        part_ref[f, 1] = faces.step(ends[1], state(f, pitch - 2), state(f, pitch - 1), none)
+        part_ref[f, 2, :radial] = faces.step(inner[0], none, y_s[f, 1], y_s[f, 2])[:radial]
+        part_ref[f, 3, :radial] = faces.step(inner[1], y_s[f, pitch - 3], y_s[f, pitch - 2], none)[:radial]
     row_ref[...] = jnp.zeros(row_ref.shape, F32)
     q = lax.axis_index("row")
     tile = pl.ds(pl.multiple_of((1 - q) * (axial - LANES), LANES), LANES)
@@ -434,6 +457,9 @@
         for f in range(nfield):
             parts += slab(y_s[f, i, :radial, tile], y_s[f, i, radial:, tile])
         row_ref[pl.ds(i, 1), :] = near(stator, parts + [blank])[0]
+
+    for copy in copies:
+        copy.wait()
 
 
 def contribution(nspan, pitch, radial, face_ref, beyond, new_rows, window_ref):
@@ -527,7 +553,7 @@
     return jnp.where(row == near_row, adds[0][i + 1 : i + 2], far).T
 
 
-def centre(npitch, nspan, mid_ref, face_ref, row_ref, buf_ref, tile_ref, arr_ref, window_ref, ring_s):
+def centre(npitch, nspan, mid_ref, face_ref, row_ref, buf_ref, tile_ref, arr_out, window_ref, ring_s, arr_ref, sem):
     nfield, inner, radial, axial = mid_ref.shape
     pitch = inner + 4
     q = lax.axis_index("row")
@@ -542,6 +568,9 @@
         for j in range(capacity // LANES):
             at = p * capacity + j * LANES
             arr_ref[:, at : at + LANES] = plain[j * values : (j + 1) * values]
+
+    copy = pltpu.make_async_copy(arr_ref, arr_out, sem.at[0])
+    copy.start()
 
     whole = npitch * pitch
     count = window_ref.shape[1]
@@ -567,28 +596,27 @@
         for f in range(nfield):
             at = f * SLAB + 8
             tile_ref[f, i] = mid_ref[f, i, :, near_tile] + block[at : at + radial]
+    copy.wait()
 
 
 def finish(
     nspan,
-    mid_ref,
+    _,
     tile_ref,
-    arr_ref,
     f_ref,
     k_ref,
     speed_ref,
     halo_ref,
     lower_ref,
     upper_ref,
-    y4_ref,
+    y2_ref,
+    part_ref,
+    outer_ref,
     row_ref,
     face_ref,
     window_ref,
     out_ref,
-    arr_out,
-    y_s,
     o_s,
-    row_s,
     sems,
 ):
     nfield, pitch, radial, axial = f_ref.shape
@@ -597,18 +625,10 @@
     q = lax.axis_index("row")
     near_tile = pl.ds(pl.multiple_of((1 - q) * (axial - LANES), LANES), LANES)
     copies = [
-        pltpu.make_async_copy(arr_ref, arr_out, sems.at[2]),
         pltpu.make_async_copy(
-            tile_ref, out_ref.at[:, 2 : pitch - 2, :, near_tile], sems.at[3]
-        ),
+            tile_ref, out_ref.at[:, 2 : pitch - 2, :, near_tile], sems.at[2]
+        )
     ]
-    if axial > LANES:
-        rest = pl.ds(pl.multiple_of(q * LANES, LANES), axial - LANES)
-        copies.append(
-            pltpu.make_async_copy(
-                mid_ref.at[:, :, :, rest], out_ref.at[:, 2 : pitch - 2, :, rest], sems.at[4]
-            )
-        )
     for copy in copies:
         copy.start()
     faces = Faces(nspan, speed_ref, radial)
@@ -629,45 +649,57 @@
             extra = jnp.where(sub == 7, side[corner + 1 : corner + 2], extra)
         return jnp.concatenate([side[at : at + radial], extra], 0)
 
-    row_s[...] = row_ref[...]
-    beyond = []
-    tile = pl.ds(pl.multiple_of(lax.axis_index("row") * (LANES - axial) + axial - LANES, LANES), LANES)
+    beyond, ends, results = [], [], {}
 
     def edge_lanes(value):
         return jnp.where(stator, value[:, axial - LANES :], value[:, :LANES])
 
     blank = jnp.zeros((SLAB, LANES), F32)
-    held = {i: n for n, i in enumerate((1, 2, pitch - 3, pitch - 2))}
-    for side, new, done in ((0, (-1, 0), (0, 1)), (1, (pitch - 1, pitch), (pitch - 2, pitch - 1))):
-        touched = sorted({*new, *done})
-        k = {i: state(nfield, i) for i in range(touched[0] - 1, touched[-1] + 2)}
-        w = {i: faces.weights(k[i - 1], k[i], k[i + 1]) for i in touched}
+    for side in range(2):
+        inside, outside, beyond_it = ((0, -1, -2), (pitch - 1, pitch, pitch + 1))[side]
+
+        def ordered(far, centre, near):
+            return (far, centre, near) if side == 0 else (near, centre, far)
+
+        k_in, k_out = state(nfield, inside), state(nfield, outside)
+        w_out = faces.weights(*ordered(state(nfield, beyond_it), k_out, k_in))
+        kappa = 0.5 * TIME_STEP * (k_in + k_out)
+        w_in = [outer_ref[side, n] for n in range(7)]
+        w_in[0] = w_in[0] - kappa
+        w_in[6 - side] = w_in[6 - side] + kappa
+        wind = faces.pitch_up if side == 0 else -faces.pitch_dn
+        updated = []
         for f in range(nfield):
-            x = {i: state(f, i) for i in range(new[0] - 1, new[1] + 2)}
-            y = {i: y4_ref[f, held[i]] for i in held if done[0] - 1 <= i <= done[1] + 1}
-            for i in new:
-                y[i] = faces.step(w[i], x[i - 1], x[i], x[i + 1])
-            for n, i in enumerate(done):
-                o_s[f, 2 * side + n] = faces.step(w[i], y[i - 1], y[i], y[i + 1])[:radial]
-            y_s[f] = y[0 if side == 0 else pitch - 1]
-        parts = []
-        for f in range(nfield):
-            parts += slab(y_s[f, :radial, tile], y_s[f, radial:, tile])
-        i = 0 if side == 0 else pitch - 1
-        row_s[i : i + 1] = near(stator, parts + [blank])[0]
+            x_in, x_out = state(f, inside), state(f, outside)
+            y_out = faces.step(w_out, *ordered(state(f, beyond_it), x_out, x_in))
+            y_in = part_ref[f, side] + kappa * (x_out - x_in) + wind * x_out
+            new_in = faces.step(w_in, *ordered(y_out, y_in, y2_ref[f, side]))[:radial]
+            new_next = part_ref[f, 2 + side, :radial] + (outer_ref[side, 7] * y_in)[:radial]
+            results[f, 3 * side] = new_in
+            results[f, 1 + side] = new_next
+            value = edge_lanes(y_in)
+            updated += slab(value[:radial], value[radial:])
+        ends.append(near(stator, updated + [blank])[0])
         parts = []
         for f in range(planes):
             value = edge_lanes(state(f, -1 if side == 0 else pitch))
             parts += slab(value[:radial], value[radial:])
         beyond.append(near(stator, parts)[0])
-    adds = contribution(nspan, pitch, radial, face_ref, beyond, row_s[...], window_ref)
+    rows = row_ref[...]
+    index = iota(rows.shape, 0)
+    rows = jnp.where(index == 0, ends[0], jnp.where(index == pitch - 1, ends[1], rows))
+    adds = contribution(nspan, pitch, radial, face_ref, beyond, rows, window_ref)
+    none = jnp.zeros((radial, axial - LANES), F32)
     for side in range(2):
         first = side * (pitch - 2)
         for n in range(2):
             block = column(stator, adds, first + n)
             for f in range(nfield):
-                at = f * SLAB + 8
-                o_s[f, 2 * side + n, :, tile] += block[at : at + radial]
+                add = block[f * SLAB + 8 : f * SLAB + 8 + radial]
+                add = jnp.where(
+                    stator, jnp.concatenate([none, add], 1), jnp.concatenate([add, none], 1)
+                )
+                o_s[f, 2 * side + n] = results[f, 2 * side + n] + add
         copies.append(
             pltpu.make_async_copy(
                 o_s.at[:, 2 * side : 2 * side + 2], out_ref.at[:, first : first + 2], sems.at[side]
@@ -789,7 +821,8 @@
         [ANY] + [VMEM] * 4,
         [pltpu.VMEM((2, 2 * edge, axial), F32)],
         nbytes=2**18,
-        passed=(0,),
+        place=(ANY, VMEM, VMEM, VMEM),
+        passed={0: 0},
     )
     buf = lax.all_to_all(
         buf.reshape(npitch * 2, per_slot, LANES), ("pitch", "row"), 0, 0
@@ -798,11 +831,14 @@
     lower = lax.ppermute(up, "pitch", ring)
     upper = lax.ppermute(down, "pitch", [(b, a) for a, b in ring])
 
-    mid, near_edge, new_rows = call(
+    moved, mid, near_edge, part, outer, new_rows = call(
         lambda *refs: middle(nspan, *refs),
         [
+            (fields.shape, F32),
             ((nfield, pitch - 4, radial, axial), F32),
+            ((nfield, 2, rows, axial), F32),
             ((nfield, 4, rows, axial), F32),
+            ((2, 8, rows, axial), F32),
             ((pitch, LANES), F32),
         ],
         (fields, diffusivity, speeds, halo),
@@ -810,9 +846,11 @@
         [
             pltpu.VMEM((nfield, pitch, rows, axial), F32),
             pltpu.VMEM((7, pitch, rows, axial), F32),
+            pltpu.SemaphoreType.DMA((1,)),
         ],
         flops=2**24,
         nbytes=2**22,
+        place=(ANY,) + (VMEM,) * 5,
     )
     near_mid, arrived, window = call(
         lambda *refs: centre(npitch, nspan, *refs),
@@ -823,18 +861,21 @@
         ],
         (mid, face, new_rows, buf),
         [VMEM] * 4,
-        [pltpu.VMEM((2, npitch * pitch + pitch + 8, LANES), F32)],
+        [
+            pltpu.VMEM((2, npitch * pitch + pitch + 8, LANES), F32),
+            pltpu.VMEM((values, npitch * capacity), F32),
+            pltpu.SemaphoreType.DMA((1,)),
+        ],
         flops=2**22,
         nbytes=2**21,
-        fixed=True,
-    )
-    return call(
+        place=(VMEM, ANY, VMEM),
+    )
+    (moved,) = call(
         lambda *refs: finish(nspan, *refs),
-        [(fields.shape, F32), (arrived.shape, F32)],
+        [(fields.shape, F32)],
         (
-            mid,
+            moved,
             near_mid,
-            arrived,
             fields,
             diffusivity,
             speeds,
@@ -842,21 +883,23 @@
             lower,
             upper,
             near_edge,
+            part,
+            outer,
             new_rows,
             face,
             window,
         ),
-        [VMEM] * 13,
+        [ANY] + [VMEM] * 13,
         [
-            pltpu.VMEM((nfield, rows, axial), F32),
             pltpu.VMEM((nfield, 4, radial, axial), F32),
-            pltpu.VMEM((pitch, LANES), F32),
-            pltpu.SemaphoreType.DMA((5,)),
+            pltpu.SemaphoreType.DMA((3,)),
         ],
         flops=2**23,
         nbytes=2**21,
         place=ANY,
-    )
+        passed={0: 0},
+    )
+    return moved, arrived
 
 
 def solution(mesh):

time: 27.5 us -> 27.1 us (0.985)
  waiting for transfers between devices: 3.46 us -> 2.79 us
  Pallas kernels: 9.16 us -> 9.48 us
    all_to_all x1, waiting for transfers between devices: 2.3 us -> 1.84 us  [local(): lax.all_to_all(buf.reshape(npitch * 2, per_slot, LANES), ('pitch', 'row')...]
    pallas_call x7, Pallas kernels: 9.16 us -> 9.48 us  [call(): pl.pallas_call(body, out_shape=tuple((shape(s, d) for s, d in outs)), in_...]
  transfers between devices with their start and end apart: 5 -> 5, of which waited for: 3 -> 3; matrix products, arithmetic and copies ran while one was open for 0% -> 0% of each run, Pallas kernels for 22% -> 25%
where the time goes in v5:
time: 27.1 us; the launch traced here: 26.8 us
  starting transfers between devices  13.8 us (51%)
  Pallas kernels  9.48 us (35%)
  waiting for transfers between devices  2.79 us (10%)
  between operations  0.69 us (3%)
    pallas_call x7, Pallas kernels, call(): pl.pallas_call(body, out_shape=tuple((shape(s, d) for s, d in outs)), in_...  9.48 us
    all_to_all x1, starting transfers between devices, local(): lax.all_to_all(buf.reshape(npitch * 2, per_slot, LANES), ('pitch', 'row')...  5.92 us
    ppermute x1, starting transfers between devices, local(): span_got = (packed[0], lax.ppermute(packed[0], 'span', swap))  3.03 us
    ppermute x1, starting transfers between devices, local(): upper = lax.ppermute(down, 'pitch', [(b, a) for a, b in ring])  2.86 us
    ppermute x1, starting transfers between devices, local(): lower = lax.ppermute(up, 'pitch', ring)  1.93 us
    all_to_all x1, waiting for transfers between devices, local(): lax.all_to_all(buf.reshape(npitch * 2, per_slot, LANES), ('pitch', 'row')...  1.84 us
    ppermute x1, waiting for transfers between devices, local(): low = high = lax.ppermute(packed[1], 'span', swap)  0.7 us
  transfers between devices with their start and end apart: 5, of which 3 were waited for; matrix products, arithmetic and copies ran while one was open for 0% of the time, Pallas kernels for 25%

profile of v5, /device:TPU:0, one launch (start us, length us, event | category | flops | bytes accessed | tf_op | source)
XLA Modules:
  0.0 26.8 jit_solution(12166207633356858122)
XLA Ops:
  0.6 1.4 %shard_map.95 = (bf16[64,256]{1,0:T(8,128)(2,1)S(1)}, bf16[128,256]{1,0:T(8,128)(2,1)S(1)}, f32[3,16,16,256]{3,2,1,0:T(8,128)S(1)}, f32[16,16,256]{2,1,0:T(8,128...) custom-call(f32[3,16,16,256]{3,2,1,0:T(8,128)} %refs_0_.1, ...), custom_call_target="tpu_custom_call" | custom-call | bytes 1048576 | tf_op jit(solution)/shard_map/pallas_call | solution.py:42
  2.0 3.0 %collective-permute-start = (bf16[64,256]{1,0:T(8,128)(2,1)S(1)}, bf16[64,256]{1,0:T(8,128)(2,1)S(1)}, u32[]{:S(2)}, u32[]{:S(2)}) collective-permute-start(bf16[64,256]{1,0:T(8,128)(2,1)S(1)} %get-tuple-element.42.refs_10_), channel_id=1, source_target_pairs={{0,2},{2,0},{1,3},{3,1},{4,6},{6,4},{5,7},{7,5},{8,10},{10,8},{9,1... | collective-permute-start | bytes 98312 | tf_op jit(solution)/shard_map/ppermute | solution.py:755
  5.0 0.1 collective-permute-start.1
  5.1 1.9 %shard_map.96 = (f32[8,2048]{1,0:T(8,128)S(1)}, bf16[256,2048]{1,0:T(8,128)(2,1)S(1)}, s32[1,2048]{1,0:T(1,128)S(1)}, bf16[256,2048]{1,0:T(8,128)(2,1)S(1)}) custom-call(f32[3,16,16,256]{3,2,1,0:T(8,128)S(1)} %get-tuple-element.31.refs_0_.refs_3_.refs_2_, s32[16,128]{1,0:T(8,128)S(1)} %get-tuple-element.35.refs_1_.refs_4_, ...), custom_call_target="tpu_custom_call" | custom-call | flops 1610612736 | bytes 1048576 | tf_op jit(solution)/shard_map/pallas_call | solution.py:42
  7.0 0.0 collective-permute-done.refs_11_
  7.0 1.6 %shard_map.97 = (bf16[8,2,40,128]{3,2,1,0:T(8,128)(2,1)}, f32[2,24,256]{2,1,0:T(8,128)S(1)}, f32[40,128]{1,0:T(8,128)S(1)}) custom-call(f32[3,16,16,256]{3,2,1,0:T(8,128)S(1)} %get-tuple-element.31.refs_0_.refs_3_.refs_2_, f32[16,16,256]{2,1,0:T(8,128)S(1)} %get-tuple-element.32.refs_1_.refs_4_.refs_3_, bf16[32,32]{1,0:T(8,128)(2,1)S(1)} %get-tuple-element.33.refs_2_, ...), custom_call_target="tpu_custom_call" | custom-call | flops 167772160 | bytes 2097152 | tf_op jit(solution)/shard_map/pallas_call | solution.py:42
  8.6 0.7 %collective-permute-done.1.refs_1_.refs_2_ = bf16[128,256]{1,0:T(8,128)(2,1)S(1)} collective-permute-done((bf16[128,256]{1,0:T(8,128)(2,1)S(1)}, bf16[128,256]{1,0:T(8,128)(2,1)S(1)}, u32[]{:S(2)}, u32[]{:S(2)}) %collective-permute-start.1) | collective-permute-done | bytes 65568 | tf_op jit(solution)/shard_map/ppermute | solution.py:756
  9.3 0.2 shard_map.98
  9.5 5.9 %all-to-all-start = ((bf16[16,40,128]{2,1,0:T(8,128)(2,1)}), bf16[16,40,128]{2,1,0:T(8,128)(2,1)S(1)}, u32[]{:S(2)}, u32[]{:S(2)}) async-start(bf16[16,40,128]{2,1,0:T(8,128)(2,1)} %bitcast.2), calls=%async_computation | async-start | bytes 327680 | tf_op jit(solution)/shard_map/all_to_all | solution.py:827
  15.4 1.9 %collective-permute-start.2 = (bf16[144,256]{1,0:T(8,128)(2,1)S(1)}, bf16[144,256]{1,0:T(8,128)(2,1)S(1)}, u32[]{:S(2)}, u32[]{:S(2)}) collective-permute-start(bf16[144,256]{1,0:T(8,128)(2,1)S(1)} %get-tuple-element.53), channel_id=1, source_target_pairs={{0,4},{4,8},{8,12},{12,16},{16,20},{20,24},{24,28},{28,0},{1,5},{5... | collective-permute-start | bytes 221192 | tf_op jit(solution)/shard_map/ppermute | solution.py:831
  17.3 2.9 %collective-permute-start.3 = (bf16[144,256]{1,0:T(8,128)(2,1)S(1)}, bf16[144,256]{1,0:T(8,128)(2,1)S(1)}, u32[]{:S(2)}, u32[]{:S(2)}) collective-permute-start(bf16[144,256]{1,0:T(8,128)(2,1)S(1)} %get-tuple-element.54), channel_id=1, source_target_pairs={{4,0},{8,4},{12,8},{16,12},{20,16},{24,20},{28,24},{0,28},{5,1},{9... | collective-permute-start | bytes 221192 | tf_op jit(solution)/shard_map/ppermute | solution.py:832
  20.2 2.3 %shard_map.99 = (f32[3,16,16,256]{3,2,1,0:T(8,128)}, f32[3,12,16,256]{3,2,1,0:T(8,128)S(1)}, f32[3,2,24,256]{3,2,1,0:T(8,128)S(1)}, f32[3,4,24,256]{3,2,1,0:T(8,...) custom-call(f32[3,16,16,256]{3,2,1,0:T(8,128)S(1)} %get-tuple-element.31.refs_0_.refs_3_.refs_2_, ...), custom_call_target="tpu_custom_call" | custom-call | flops 16777216 | bytes 4194304 | tf_op jit(solution)/shard_map/pallas_call | solution.py:42
  22.5 1.8 %all-to-all-done = bf16[16,40,128]{2,1,0:T(8,128)(2,1)S(1)} async-done(((bf16[16,40,128]{2,1,0:T(8,128)(2,1)}), bf16[16,40,128]{2,1,0:T(8,128)(2,1)S(1)}, u32[]{:S(2)}, u32[]{:S(2)}) %all-to-all-start) | async-done | bytes 163872 | tf_op jit(solution)/shard_map/all_to_all | solution.py:827
  24.3 0.9 %shard_map.100 = (f32[3,12,16,128]{3,2,1,0:T(8,128)S(1)}, f32[10,4096]{1,0:T(8,128)}, f32[3,24,128]{2,1,0:T(8,128)S(1)}) custom-call(f32[3,12,16,256]{3,2,1,0:T(8,128)S(1)} %get-tuple-element.48.refs_0_, f32[40,128]{1,0:T(8,128)S(1)} %get-tuple-element.49.refs_1_.refs_12_, f32[16,128]{1,0:T(8,128)S(1)} %get-tuple-element.50.refs_2_.refs_11_, ...), custom_call_target="tpu_custom_call" | custom-call | flops 4194304 | bytes 2097152 | tf_op jit(solution)/shard_map/pallas_call | solution.py:42
  25.2 0.2 collective-permute-done.2.refs_6_
  25.4 0.0 collective-permute-done.3.refs_7_
  25.4 1.3 %shard_map.101 = f32[3,16,16,256]{3,2,1,0:T(8,128)} custom-call(f32[3,16,16,256]{3,2,1,0:T(8,128)} %get-tuple-element.47.refs_0_, f32[3,12,16,128]{3,2,1,0:T(8,128)S(1)} %get-tuple-element.52.refs_1_, f32[3,16,16,256]{3,2,1,0:T(8,128)S(1)} %get-tuple-element.31.refs_0_.refs_3_.refs_2_, ...), custom_call_target="tpu_custom_call", output_to_operand_aliasing={{}: (0, {})} | custom-call | flops 8388608 | bytes 2097152 | tf_op jit(solution)/shard_map/pallas_call | solution.py:42
Async XLA Ops:
  2.0 5.0 %collective-permute-start = (bf16[64,256]{1,0:T(8,128)(2,1)S(1)}, bf16[64,256]{1,0:T(8,128)(2,1)S(1)}, u32[]{:S(2)}, u32[]{:S(2)}) collective-permute-start(bf16[64,256]{1,0:T(8,128)(2,1)S(1)} %get-tuple-element.42.refs_10_), channel_id=1, source_target_pairs={{0,2},{2,0},{1,3},{3,1},{4,6},{6,4},{5,7},{7,5},{8,10},{10,8},{9,1... | collective-permute-start | bytes 98312 | tf_op jit(solution)/shard_map/ppermute | solution.py:755
  5.0 4.3 %collective-permute-start.1 = (bf16[128,256]{1,0:T(8,128)(2,1)S(1)}, bf16[128,256]{1,0:T(8,128)(2,1)S(1)}, u32[]{:S(2)}, u32[]{:S(2)}) collective-permute-start(bf16[128,256]{1,0:T(8,128)(2,1)S(1)} %get-tuple-element.45), channel_id=1, source_target_pairs={{0,2},{2,0},{1,3},{3,1},{4,6},{6,4},{5,7},{7,5},{8,10},{10,8},{9,1... | collective-permute-start | bytes 196616 | tf_op jit(solution)/shard_map/ppermute | solution.py:756
  9.5 14.9 %all-to-all-start = ((bf16[16,40,128]{2,1,0:T(8,128)(2,1)}), bf16[16,40,128]{2,1,0:T(8,128)(2,1)S(1)}, u32[]{:S(2)}, u32[]{:S(2)}) async-start(bf16[16,40,128]{2,1,0:T(8,128)(2,1)} %bitcast.2), calls=%async_computation | async-start | bytes 327680 | tf_op jit(solution)/shard_map/all_to_all | solution.py:827
  15.4 10.0 %collective-permute-start.2 = (bf16[144,256]{1,0:T(8,128)(2,1)S(1)}, bf16[144,256]{1,0:T(8,128)(2,1)S(1)}, u32[]{:S(2)}, u32[]{:S(2)}) collective-permute-start(bf16[144,256]{1,0:T(8,128)(2,1)S(1)} %get-tuple-element.53), channel_id=1, source_target_pairs={{0,4},{4,8},{8,12},{12,16},{16,20},{20,24},{24,28},{28,0},{1,5},{5... | collective-permute-start | bytes 221192 | tf_op jit(solution)/shard_map/ppermute | solution.py:831
  17.3 8.1 %collective-permute-start.3 = (bf16[144,256]{1,0:T(8,128)(2,1)S(1)}, bf16[144,256]{1,0:T(8,128)(2,1)S(1)}, u32[]{:S(2)}, u32[]{:S(2)}) collective-permute-start(bf16[144,256]{1,0:T(8,128)(2,1)S(1)} %get-tuple-element.54), channel_id=1, source_target_pairs={{4,0},{8,4},{12,8},{16,12},{20,16},{24,20},{28,24},{0,28},{5,1},{9... | collective-permute-start | bytes 221192 | tf_op jit(solution)/shard_map/ppermute | solution.py:832

commit v6 on v5

--- a/solution.py
+++ b/solution.py
@@ -266,7 +266,7 @@
         for g in range(groups):
             for n in range(width // LANES):
                 pieces.append(acc_s[:, d * groups + g, n * LANES : (n + 1) * LANES])
-        buf_ref[d, q] = jnp.concatenate(pieces + filler, 0).astype(BF16)
+        buf_ref[d, 0] = jnp.concatenate(pieces + filler, 0).astype(BF16)
 
     if nspan == 2:
         near_s[0, : edge // 2] = got_ref[2 * radial :, :LANES].astype(F32)
@@ -310,7 +310,7 @@
 
     @pl.loop(0, npitch, unroll=True)
     def _(d):
-        buf_ref[d, 1 - q] = face
+        buf_ref[d, 1] = face
 
 
 def halos(low_ref, high_ref, f_ref, k_ref, halo_ref, up_ref, down_ref, near_s):
@@ -553,40 +553,45 @@
     return jnp.where(row == near_row, adds[0][i + 1 : i + 2], far).T
 
 
-def centre(npitch, nspan, mid_ref, face_ref, row_ref, buf_ref, tile_ref, arr_out, window_ref, ring_s, arr_ref, sem):
-    nfield, inner, radial, axial = mid_ref.shape
-    pitch = inner + 4
-    q = lax.axis_index("row")
-    stator = q == 0
-    near_tile = pl.ds(pl.multiple_of((1 - q) * (axial - LANES), LANES), LANES)
-
+def unpack(npitch, buf_ref, arr_out, arr_ref, sem):
     values = arr_ref.shape[0]
     capacity = arr_ref.shape[1] // npitch
     for p in range(npitch):
-        coded = buf_ref[p, q].astype(F32)
+        coded = buf_ref[p, 0].astype(F32)
         plain = jnp.where(coded > 0.0, jnp.log2(coded) * (1.0 / CODE), 0.0)
         for j in range(capacity // LANES):
             at = p * capacity + j * LANES
             arr_ref[:, at : at + LANES] = plain[j * values : (j + 1) * values]
-
     copy = pltpu.make_async_copy(arr_ref, arr_out, sem.at[0])
     copy.start()
-
+    copy.wait()
+
+
+def extract(npitch, pitch, buf_ref, face_ref, window_ref, ring_s):
     whole = npitch * pitch
     count = window_ref.shape[1]
     for p in range(npitch):
-        both = buf_ref[p, 1 - q].astype(F32)
+        both = buf_ref[p, 1].astype(F32)
         ring_s[0, p * pitch : (p + 1) * pitch] = both[:pitch]
         ring_s[1, p * pitch : (p + 1) * pitch] = both[pitch : 2 * pitch]
         if p == 0:
             window_ref[2, :8] = both[2 * pitch : 2 * pitch + 8]
     for n in range(2):
         ring_s[n, whole : whole + pitch] = ring_s[n, :pitch]
-        ring_s[n, whole + pitch :] = ring_s[n, pitch : count]
-    begin = jnp.max(face_ref[2 * pitch + 2 : 2 * pitch + 3]).astype(jnp.int32) - 1
-    begin = jnp.where(begin < 0, begin + whole, begin)
+        ring_s[n, whole + pitch :] = ring_s[n, pitch:count]
+    facing = jnp.max(face_ref[2 * pitch + 2 : 2 * pitch + 3]).astype(jnp.int32)
+    begin = 2 * pitch * lax.axis_index("pitch") - facing - 1 + 2 * whole
+    begin = begin & (whole - 1)
     window_ref[0] = ring_s[0, pl.ds(begin, count), :]
     window_ref[1] = ring_s[1, pl.ds(begin, count), :]
+
+
+def centre(nspan, mid_ref, face_ref, row_ref, window_ref, tile_ref):
+    nfield, inner, radial, axial = mid_ref.shape
+    pitch = inner + 4
+    q = lax.axis_index("row")
+    stator = q == 0
+    near_tile = pl.ds(pl.multiple_of((1 - q) * (axial - LANES), LANES), LANES)
     blank = jnp.zeros((1, LANES), F32)
     adds = contribution(
         nspan, pitch, radial, face_ref, (blank, blank), row_ref[...], window_ref
@@ -596,7 +601,6 @@
         for f in range(nfield):
             at = f * SLAB + 8
             tile_ref[f, i] = mid_ref[f, i, :, near_tile] + block[at : at + radial]
-    copy.wait()
 
 
 def finish(
@@ -824,9 +828,7 @@
         place=(ANY, VMEM, VMEM, VMEM),
         passed={0: 0},
     )
-    buf = lax.all_to_all(
-        buf.reshape(npitch * 2, per_slot, LANES), ("pitch", "row"), 0, 0
-    ).reshape(buf.shape)
+    buf = lax.all_to_all(buf, "pitch", 0, 0)
     ring = [(n, (n + 1) % npitch) for n in range(npitch)]
     lower = lax.ppermute(up, "pitch", ring)
     upper = lax.ppermute(down, "pitch", [(b, a) for a, b in ring])
@@ -852,23 +854,31 @@
         nbytes=2**22,
         place=(ANY,) + (VMEM,) * 5,
     )
-    near_mid, arrived, window = call(
-        lambda *refs: centre(npitch, nspan, *refs),
-        [
-            ((nfield, pitch - 4, radial, LANES), F32),
-            ((values, npitch * capacity), F32),
-            ((3, pitch + 8, LANES), F32),
-        ],
-        (mid, face, new_rows, buf),
+    (window,) = call(
+        lambda *refs: extract(npitch, pitch, *refs[1:]),
+        [((3, pitch + 8, LANES), F32)],
+        (new_rows, buf, face),
+        [VMEM] * 3,
+        [pltpu.VMEM((2, npitch * pitch + pitch + 8, LANES), F32)],
+        nbytes=2**18,
+    )
+    (arrived,) = call(
+        lambda *refs: unpack(npitch, *refs[1:]),
+        [((values, npitch * capacity), F32)],
+        (window, buf),
+        [VMEM] * 2,
+        [pltpu.VMEM((values, npitch * capacity), F32), pltpu.SemaphoreType.DMA((1,))],
+        nbytes=2**20,
+        place=ANY,
+    )
+    window = lax.ppermute(window, "row", [(0, 1), (1, 0)])
+    (near_mid,) = call(
+        lambda *refs: centre(nspan, *refs),
+        [((nfield, pitch - 4, radial, LANES), F32)],
+        (mid, face, new_rows, window),
         [VMEM] * 4,
-        [
-            pltpu.VMEM((2, npitch * pitch + pitch + 8, LANES), F32),
-            pltpu.VMEM((values, npitch * capacity), F32),
-            pltpu.SemaphoreType.DMA((1,)),
-        ],
         flops=2**22,
-        nbytes=2**21,
-        place=(VMEM, ANY, VMEM),
+        nbytes=2**20,
     )
     (moved,) = call(
         lambda *refs: finish(nspan, *refs),

time: 27.1 us -> 26.5 us (0.978)
  waiting for transfers between devices: 2.79 us -> 1.66 us
  Pallas kernels: 9.48 us -> 10.1 us
    all_to_all x1, waiting for transfers between devices: 1.84 us -> 0.51 us  [local(): buf = lax.all_to_all(buf, 'pitch', 0, 0)]
    pallas_call x7 -> x9, Pallas kernels: 9.48 us -> 10.1 us  [call(): pl.pallas_call(body, out_shape=tuple((shape(s, d) for s, d in outs)), in_...]
    ppermute x0 -> x1, waiting for transfers between devices: none -> 0.44 us  [local(): window = lax.ppermute(window, 'row', [(0, 1), (1, 0)])]
  transfers between devices with their start and end apart: 5 -> 6, of which waited for: 3 -> 3; matrix products, arithmetic and copies ran while one was open for 0% -> 0% of each run, Pallas kernels for 25% -> 27%
where the time goes in v6:
time: 26.5 us; the launch traced here: 26.2 us
  starting transfers between devices  13.8 us (52%)
  Pallas kernels  10.1 us (38%)
  waiting for transfers between devices  1.66 us (6%)
  between operations  0.72 us (3%)
    pallas_call x9, Pallas kernels, call(): pl.pallas_call(body, out_shape=tuple((shape(s, d) for s, d in outs)), in_...  10.1 us
    all_to_all x1, starting transfers between devices, local(): buf = lax.all_to_all(buf, 'pitch', 0, 0)  5.82 us
    ppermute x1, starting transfers between devices, local(): span_got = (packed[0], lax.ppermute(packed[0], 'span', swap))  3.03 us
    ppermute x1, starting transfers between devices, local(): upper = lax.ppermute(down, 'pitch', [(b, a) for a, b in ring])  2.73 us
    ppermute x1, starting transfers between devices, local(): lower = lax.ppermute(up, 'pitch', ring)  2.02 us
    ppermute x1, waiting for transfers between devices, local(): low = high = lax.ppermute(packed[1], 'span', swap)  0.71 us
  transfers between devices with their start and end apart: 6, of which 3 were waited for; matrix products, arithmetic and copies ran while one was open for 0% of the time, Pallas kernels for 27%

profile of v6, /device:TPU:0, one launch (start us, length us, event | category | flops | bytes accessed | tf_op | source)
XLA Modules:
  0.0 26.2 jit_solution(5709457281222203983)
XLA Ops:
  0.6 1.4 %shard_map.95 = (bf16[64,256]{1,0:T(8,128)(2,1)S(1)}, bf16[128,256]{1,0:T(8,128)(2,1)S(1)}, f32[3,16,16,256]{3,2,1,0:T(8,128)S(1)}, f32[16,16,256]{2,1,0:T(8,128...) custom-call(f32[3,16,16,256]{3,2,1,0:T(8,128)} %refs_0_.1, ...), custom_call_target="tpu_custom_call" | custom-call | bytes 1048576 | tf_op jit(solution)/shard_map/pallas_call | solution.py:42
  2.0 3.0 %collective-permute-start = (bf16[64,256]{1,0:T(8,128)(2,1)S(1)}, bf16[64,256]{1,0:T(8,128)(2,1)S(1)}, u32[]{:S(2)}, u32[]{:S(2)}) collective-permute-start(bf16[64,256]{1,0:T(8,128)(2,1)S(1)} %get-tuple-element.39.refs_10_), channel_id=1, source_target_pairs={{0,2},{2,0},{1,3},{3,1},{4,6},{6,4},{5,7},{7,5},{8,10},{10,8},{9,1... | collective-permute-start | bytes 98312 | tf_op jit(solution)/shard_map/ppermute | solution.py:759
  5.0 0.1 collective-permute-start.1
  5.1 1.9 %shard_map.96 = (f32[8,2048]{1,0:T(8,128)S(1)}, bf16[256,2048]{1,0:T(8,128)(2,1)S(1)}, s32[1,2048]{1,0:T(1,128)S(1)}, bf16[256,2048]{1,0:T(8,128)(2,1)S(1)}) custom-call(f32[3,16,16,256]{3,2,1,0:T(8,128)S(1)} %get-tuple-element.28.refs_0_.refs_3_.refs_2_, s32[16,128]{1,0:T(8,128)S(1)} %get-tuple-element.32.refs_1_.refs_4_, ...), custom_call_target="tpu_custom_call" | custom-call | flops 1610612736 | bytes 1048576 | tf_op jit(solution)/shard_map/pallas_call | solution.py:42
  7.0 0.0 collective-permute-done.refs_11_
  7.0 1.6 %shard_map.97 = (bf16[8,2,40,128]{3,2,1,0:T(8,128)(2,1)}, f32[2,24,256]{2,1,0:T(8,128)S(1)}, f32[40,128]{1,0:T(8,128)S(1)}) custom-call(f32[3,16,16,256]{3,2,1,0:T(8,128)S(1)} %get-tuple-element.28.refs_0_.refs_3_.refs_2_, f32[16,16,256]{2,1,0:T(8,128)S(1)} %get-tuple-element.29.refs_1_.refs_4_.refs_3_, bf16[32,32]{1,0:T(8,128)(2,1)S(1)} %get-tuple-element.30.refs_2_, ...), custom_call_target="tpu_custom_call" | custom-call | flops 167772160 | bytes 2097152 | tf_op jit(solution)/shard_map/pallas_call | solution.py:42
  8.6 0.7 %collective-permute-done.1.refs_1_.refs_2_ = bf16[128,256]{1,0:T(8,128)(2,1)S(1)} collective-permute-done((bf16[128,256]{1,0:T(8,128)(2,1)S(1)}, bf16[128,256]{1,0:T(8,128)(2,1)S(1)}, u32[]{:S(2)}, u32[]{:S(2)}) %collective-permute-start.1) | collective-permute-done | bytes 65568 | tf_op jit(solution)/shard_map/ppermute | solution.py:760
  9.3 0.2 shard_map.98
  9.5 5.8 %all-to-all-start = ((bf16[8,2,40,128]{3,2,1,0:T(8,128)(2,1)}), bf16[8,2,40,128]{3,2,1,0:T(8,128)(2,1)S(1)}, u32[]{:S(2)}, u32[]{:S(2)}) async-start(bf16[8,2,40,128]{3,2,1,0:T(8,128)(2,1)} %get-tuple-element.48), calls=%async_computation | async-start | bytes 327680 | tf_op jit(solution)/shard_map/all_to_all | solution.py:831
  15.3 2.0 %collective-permute-start.3 = (bf16[144,256]{1,0:T(8,128)(2,1)S(1)}, bf16[144,256]{1,0:T(8,128)(2,1)S(1)}, u32[]{:S(2)}, u32[]{:S(2)}) collective-permute-start(bf16[144,256]{1,0:T(8,128)(2,1)S(1)} %get-tuple-element.49), channel_id=1, source_target_pairs={{0,4},{4,8},{8,12},{12,16},{16,20},{20,24},{24,28},{28,0},{1,5},{5... | collective-permute-start | bytes 221192 | tf_op jit(solution)/shard_map/ppermute | solution.py:833
  17.3 2.7 %collective-permute-start.4 = (bf16[144,256]{1,0:T(8,128)(2,1)S(1)}, bf16[144,256]{1,0:T(8,128)(2,1)S(1)}, u32[]{:S(2)}, u32[]{:S(2)}) collective-permute-start(bf16[144,256]{1,0:T(8,128)(2,1)S(1)} %get-tuple-element.50), channel_id=1, source_target_pairs={{4,0},{8,4},{12,8},{16,12},{20,16},{24,20},{28,24},{0,28},{5,1},{9... | collective-permute-start | bytes 221192 | tf_op jit(solution)/shard_map/ppermute | solution.py:834
  20.0 2.3 %shard_map.99 = (f32[3,16,16,256]{3,2,1,0:T(8,128)}, f32[3,12,16,256]{3,2,1,0:T(8,128)S(1)}, f32[3,2,24,256]{3,2,1,0:T(8,128)S(1)}, f32[3,4,24,256]{3,2,1,0:T(8,...) custom-call(f32[3,16,16,256]{3,2,1,0:T(8,128)S(1)} %get-tuple-element.28.refs_0_.refs_3_.refs_2_, ...), custom_call_target="tpu_custom_call" | custom-call | flops 16777216 | bytes 4194304 | tf_op jit(solution)/shard_map/pallas_call | solution.py:42
  22.3 0.5 %all-to-all-done.refs_1_ = bf16[8,2,40,128]{3,2,1,0:T(8,128)(2,1)S(1)} async-done(((bf16[8,2,40,128]{3,2,1,0:T(8,128)(2,1)}), bf16[8,2,40,128]{3,2,1,0:T(8,128)(2,1)S(1)}, u32[]{:S(2)}, u32[]{:S(2)}) %all-to-all-start) | async-done | bytes 163872 | tf_op jit(solution)/shard_map/all_to_all | solution.py:831
  22.9 0.1 shard_map.100.refs_0_
  23.0 0.1 collective-permute-start.2
  23.1 0.8 %shard_map.103 = f32[10,4096]{1,0:T(8,128)} custom-call(f32[3,24,128]{2,1,0:T(8,128)S(1)} %shard_map.100.refs_0_, bf16[8,2,40,128]{3,2,1,0:T(8,128)(2,1)S(1)} %all-to-all-done.refs_1_), custom_call_target="tpu_custom_call" | custom-call | bytes 1048576 | tf_op jit(solution)/shard_map/pallas_call | solution.py:42
  23.8 0.4 %collective-permute-done.2.refs_3_.refs_13_ = f32[3,24,128]{2,1,0:T(8,128)S(1)} collective-permute-done((f32[3,24,128]{2,1,0:T(8,128)S(1)}, f32[3,24,128]{2,1,0:T(8,128)S(1)}, u32[]{:S(2)}, u32[]{:S(2)}) %collective-permute-start.2) | collective-permute-done | bytes 36896 | tf_op jit(solution)/shard_map/ppermute | solution.py:874
  24.3 0.5 %shard_map.101.refs_1_ = f32[3,12,16,128]{3,2,1,0:T(8,128)S(1)} custom-call(f32[3,12,16,256]{3,2,1,0:T(8,128)S(1)} %get-tuple-element.45.refs_0_, f32[40,128]{1,0:T(8,128)S(1)} %get-tuple-element.46.refs_2_.refs_1_.refs_12_, f32[16,128]{1,0:T(8,128)S(1)} %get-tuple-element.47.refs_0_.refs_2_.refs_11_, f32[3,24,128]{2,1,0:T(8,128)S(1)} %collective-permute-done.2.refs_3_.refs_13_), custom_call_target="tpu_custom_call" | custom-call | flops 4194304 | bytes 1048576 | tf_op jit(solution)/shard_map/pallas_call | solution.py:42
  24.8 0.0 collective-permute-done.3.refs_6_
  24.8 0.0 collective-permute-done.4.refs_7_
  24.8 1.4 %shard_map.102 = f32[3,16,16,256]{3,2,1,0:T(8,128)} custom-call(f32[3,16,16,256]{3,2,1,0:T(8,128)} %get-tuple-element.44.refs_0_, f32[3,12,16,128]{3,2,1,0:T(8,128)S(1)} %shard_map.101.refs_1_, f32[3,16,16,256]{3,2,1,0:T(8,128)S(1)} %get-tuple-element.28.refs_0_.refs_3_.refs_2_, ...), custom_call_target="tpu_custom_call", output_to_operand_aliasing={{}: (0, {})} | custom-call | flops 8388608 | bytes 2097152 | tf_op jit(solution)/shard_map/pallas_call | solution.py:42
Async XLA Ops:
  2.0 5.0 %collective-permute-start = (bf16[64,256]{1,0:T(8,128)(2,1)S(1)}, bf16[64,256]{1,0:T(8,128)(2,1)S(1)}, u32[]{:S(2)}, u32[]{:S(2)}) collective-permute-start(bf16[64,256]{1,0:T(8,128)(2,1)S(1)} %get-tuple-element.39.refs_10_), channel_id=1, source_target_pairs={{0,2},{2,0},{1,3},{3,1},{4,6},{6,4},{5,7},{7,5},{8,10},{10,8},{9,1... | collective-permute-start | bytes 98312 | tf_op jit(solution)/shard_map/ppermute | solution.py:759
  5.0 4.3 %collective-permute-start.1 = (bf16[128,256]{1,0:T(8,128)(2,1)S(1)}, bf16[128,256]{1,0:T(8,128)(2,1)S(1)}, u32[]{:S(2)}, u32[]{:S(2)}) collective-permute-start(bf16[128,256]{1,0:T(8,128)(2,1)S(1)} %get-tuple-element.42), channel_id=1, source_target_pairs={{0,2},{2,0},{1,3},{3,1},{4,6},{6,4},{5,7},{7,5},{8,10},{10,8},{9,1... | collective-permute-start | bytes 196616 | tf_op jit(solution)/shard_map/ppermute | solution.py:760
  9.5 13.4 %all-to-all-start = ((bf16[8,2,40,128]{3,2,1,0:T(8,128)(2,1)}), bf16[8,2,40,128]{3,2,1,0:T(8,128)(2,1)S(1)}, u32[]{:S(2)}, u32[]{:S(2)}) async-start(bf16[8,2,40,128]{3,2,1,0:T(8,128)(2,1)} %get-tuple-element.48), calls=%async_computation | async-start | bytes 327680 | tf_op jit(solution)/shard_map/all_to_all | solution.py:831
  15.3 9.5 %collective-permute-start.3 = (bf16[144,256]{1,0:T(8,128)(2,1)S(1)}, bf16[144,256]{1,0:T(8,128)(2,1)S(1)}, u32[]{:S(2)}, u32[]{:S(2)}) collective-permute-start(bf16[144,256]{1,0:T(8,128)(2,1)S(1)} %get-tuple-element.49), channel_id=1, source_target_pairs={{0,4},{4,8},{8,12},{12,16},{16,20},{20,24},{24,28},{28,0},{1,5},{5... | collective-permute-start | bytes 221192 | tf_op jit(solution)/shard_map/ppermute | solution.py:833
  17.3 7.5 %collective-permute-start.4 = (bf16[144,256]{1,0:T(8,128)(2,1)S(1)}, bf16[144,256]{1,0:T(8,128)(2,1)S(1)}, u32[]{:S(2)}, u32[]{:S(2)}) collective-permute-start(bf16[144,256]{1,0:T(8,128)(2,1)S(1)} %get-tuple-element.50), channel_id=1, source_target_pairs={{4,0},{8,4},{12,8},{16,12},{20,16},{24,20},{28,24},{0,28},{5,1},{9... | collective-permute-start | bytes 221192 | tf_op jit(solution)/shard_map/ppermute | solution.py:834
  23.0 1.3 %collective-permute-start.2 = (f32[3,24,128]{2,1,0:T(8,128)S(1)}, f32[3,24,128]{2,1,0:T(8,128)S(1)}, u32[]{:S(2)}, u32[]{:S(2)}) collective-permute-start(f32[3,24,128]{2,1,0:T(8,128)S(1)} %shard_map.100.refs_0_), channel_id=1, source_target_pairs={{0,1},{1,0},{2,3},{3,2},{4,5},{5,4},{6,7},{7,6},{8,9},{9,8},{10,11... | collective-permute-start | bytes 110600 | tf_op jit(solution)/shard_map/ppermute | solution.py:874

commit v7 on v6

--- a/solution.py
+++ b/solution.py
@@ -586,27 +586,9 @@
     window_ref[1] = ring_s[1, pl.ds(begin, count), :]
 
 
-def centre(nspan, mid_ref, face_ref, row_ref, window_ref, tile_ref):
-    nfield, inner, radial, axial = mid_ref.shape
-    pitch = inner + 4
-    q = lax.axis_index("row")
-    stator = q == 0
-    near_tile = pl.ds(pl.multiple_of((1 - q) * (axial - LANES), LANES), LANES)
-    blank = jnp.zeros((1, LANES), F32)
-    adds = contribution(
-        nspan, pitch, radial, face_ref, (blank, blank), row_ref[...], window_ref
-    )
-    for i in range(inner):
-        block = column(stator, adds, i + 2)
-        for f in range(nfield):
-            at = f * SLAB + 8
-            tile_ref[f, i] = mid_ref[f, i, :, near_tile] + block[at : at + radial]
-
-
-def finish(
+def edges(
     nspan,
     _,
-    tile_ref,
     f_ref,
     k_ref,
     speed_ref,
@@ -617,24 +599,13 @@
     part_ref,
     outer_ref,
     row_ref,
-    face_ref,
-    window_ref,
-    out_ref,
-    o_s,
-    sems,
+    o_ref,
+    rows_ref,
+    beyond_ref,
 ):
     nfield, pitch, radial, axial = f_ref.shape
     planes = nfield + 1
     stator = lax.axis_index("row") == 0
-    q = lax.axis_index("row")
-    near_tile = pl.ds(pl.multiple_of((1 - q) * (axial - LANES), LANES), LANES)
-    copies = [
-        pltpu.make_async_copy(
-            tile_ref, out_ref.at[:, 2 : pitch - 2, :, near_tile], sems.at[2]
-        )
-    ]
-    for copy in copies:
-        copy.start()
     faces = Faces(nspan, speed_ref, radial)
     ext = {-1: lower_ref[...].astype(F32), 1: upper_ref[...].astype(F32)}
     sub = iota((EXTRA, axial), 0)
@@ -653,7 +624,7 @@
             extra = jnp.where(sub == 7, side[corner + 1 : corner + 2], extra)
         return jnp.concatenate([side[at : at + radial], extra], 0)
 
-    beyond, ends, results = [], [], {}
+    beyond, ends = [], []
 
     def edge_lanes(value):
         return jnp.where(stator, value[:, axial - LANES :], value[:, :LANES])
@@ -679,8 +650,8 @@
             y_in = part_ref[f, side] + kappa * (x_out - x_in) + wind * x_out
             new_in = faces.step(w_in, *ordered(y_out, y_in, y2_ref[f, side]))[:radial]
             new_next = part_ref[f, 2 + side, :radial] + (outer_ref[side, 7] * y_in)[:radial]
-            results[f, 3 * side] = new_in
-            results[f, 1 + side] = new_next
+            o_ref[f, 3 * side] = new_in
+            o_ref[f, 1 + side] = new_next
             value = edge_lanes(y_in)
             updated += slab(value[:radial], value[radial:])
         ends.append(near(stator, updated + [blank])[0])
@@ -691,22 +662,44 @@
         beyond.append(near(stator, parts)[0])
     rows = row_ref[...]
     index = iota(rows.shape, 0)
-    rows = jnp.where(index == 0, ends[0], jnp.where(index == pitch - 1, ends[1], rows))
-    adds = contribution(nspan, pitch, radial, face_ref, beyond, rows, window_ref)
-    none = jnp.zeros((radial, axial - LANES), F32)
-    for side in range(2):
-        first = side * (pitch - 2)
-        for n in range(2):
-            block = column(stator, adds, first + n)
+    rows_ref[...] = jnp.where(index == 0, ends[0], jnp.where(index == pitch - 1, ends[1], rows))
+    beyond_ref[...] = jnp.zeros(beyond_ref.shape, F32)
+    beyond_ref[0:1] = beyond[0]
+    beyond_ref[1:2] = beyond[1]
+
+
+def finish(nspan, _, mid_ref, edge_ref, face_ref, rows_ref, beyond_ref, window_ref, out_ref, tile_s, sems):
+    nfield, pitch, radial, axial = out_ref.shape
+    q = lax.axis_index("row")
+    near_tile = pl.ds(pl.multiple_of((1 - q) * (axial - LANES), LANES), LANES)
+    copies = []
+    if axial > LANES:
+        rest = pl.ds(pl.multiple_of(q * LANES, LANES), axial - LANES)
+        for side in range(2):
+            copies.append(
+                pltpu.make_async_copy(
+                    edge_ref.at[:, 2 * side : 2 * side + 2, :, rest],
+                    out_ref.at[:, side * (pitch - 2) : side * (pitch - 2) + 2, :, rest],
+                    sems.at[side],
+                )
+            )
+            copies[-1].start()
+    beyond = beyond_ref[0:1], beyond_ref[1:2]
+    adds = contribution(nspan, pitch, radial, face_ref, beyond, rows_ref[...], window_ref)
+    part = pitch // 4
+    for n in range(4):
+        for i in range(n * part, (n + 1) * part):
+            block = column(q == 0, adds, i)
             for f in range(nfield):
-                add = block[f * SLAB + 8 : f * SLAB + 8 + radial]
-                add = jnp.where(
-                    stator, jnp.concatenate([none, add], 1), jnp.concatenate([add, none], 1)
-                )
-                o_s[f, 2 * side + n] = results[f, 2 * side + n] + add
+                if 2 <= i < pitch - 2:
+                    old = mid_ref[f, i - 2, :, near_tile]
+                else:
+                    old = edge_ref[f, i if i < 2 else i - pitch + 4, :, near_tile]
+                tile_s[f, i] = old + block[f * SLAB + 8 : f * SLAB + 8 + radial]
+        done = slice(n * part, (n + 1) * part)
         copies.append(
             pltpu.make_async_copy(
-                o_s.at[:, 2 * side : 2 * side + 2], out_ref.at[:, first : first + 2], sems.at[side]
+                tile_s.at[:, done], out_ref.at[:, done, :, near_tile], sems.at[2 + n]
             )
         )
         copies[-1].start()
@@ -871,21 +864,15 @@
         nbytes=2**20,
         place=ANY,
     )
-    window = lax.ppermute(window, "row", [(0, 1), (1, 0)])
-    (near_mid,) = call(
-        lambda *refs: centre(nspan, *refs),
-        [((nfield, pitch - 4, radial, LANES), F32)],
-        (mid, face, new_rows, window),
-        [VMEM] * 4,
-        flops=2**22,
-        nbytes=2**20,
-    )
-    (moved,) = call(
-        lambda *refs: finish(nspan, *refs),
-        [(fields.shape, F32)],
+    near_edge, new_rows, beyond = call(
+        lambda *refs: edges(nspan, *refs),
+        [
+            ((nfield, 4, radial, axial), F32),
+            ((pitch, LANES), F32),
+            ((8, LANES), F32),
+        ],
         (
-            moved,
-            near_mid,
+            window,
             fields,
             diffusivity,
             speeds,
@@ -896,15 +883,22 @@
             part,
             outer,
             new_rows,
-            face,
-            window,
         ),
-        [ANY] + [VMEM] * 13,
+        [VMEM] * 11,
+        flops=2**23,
+        nbytes=2**21,
+    )
+    window = lax.ppermute(window, "row", [(0, 1), (1, 0)])
+    (moved,) = call(
+        lambda *refs: finish(nspan, *refs),
+        [(fields.shape, F32)],
+        (moved, mid, near_edge, face, new_rows, beyond, window),
+        [ANY] + [VMEM] * 6,
         [
-            pltpu.VMEM((nfield, 4, radial, axial), F32),
-            pltpu.SemaphoreType.DMA((3,)),
+            pltpu.VMEM((nfield, pitch, radial, LANES), F32),
+            pltpu.SemaphoreType.DMA((6,)),
         ],
-        flops=2**23,
+        flops=2**22,
         nbytes=2**21,
         place=ANY,
         passed={0: 0},

time: 26.5 us -> 25.9 us (0.977)
  waiting for transfers between devices: 1.66 us -> 1.3 us
    ppermute x1, waiting for transfers between devices: 0.44 us -> 0.04 us  [local(): window = lax.ppermute(window, 'row', [(0, 1), (1, 0)])]
  transfers between devices with their start and end apart: 6 -> 6, of which waited for: 3 -> 2; matrix products, arithmetic and copies ran while one was open for 0% -> 0% of each run, Pallas kernels for 27% -> 27%
where the time goes in v7:
time: 25.9 us; the launch traced here: 25.6 us
  starting transfers between devices  13.8 us (53%)
  Pallas kernels  9.85 us (38%)
  waiting for transfers between devices  1.3 us (5%)
  between operations  0.7 us (3%)
    pallas_call x9, Pallas kernels, call(): pl.pallas_call(body, out_shape=tuple((shape(s, d) for s, d in outs)), in_...  9.85 us
    all_to_all x1, starting transfers between devices, local(): buf = lax.all_to_all(buf, 'pitch', 0, 0)  5.82 us
    ppermute x1, starting transfers between devices, local(): span_got = (packed[0], lax.ppermute(packed[0], 'span', swap))  3.03 us
    ppermute x1, starting transfers between devices, local(): upper = lax.ppermute(down, 'pitch', [(b, a) for a, b in ring])  2.73 us
    ppermute x1, starting transfers between devices, local(): lower = lax.ppermute(up, 'pitch', ring)  2.02 us
    ppermute x1, waiting for transfers between devices, local(): low = high = lax.ppermute(packed[1], 'span', swap)  0.71 us
  transfers between devices with their start and end apart: 6, of which 2 were waited for; matrix products, arithmetic and copies ran while one was open for 0% of the time, Pallas kernels for 27%

profile of v7, /device:TPU:0, one launch (start us, length us, event | category | flops | bytes accessed | tf_op | source)
XLA Modules:
  0.0 25.6 jit_solution(12851615842711008136)
XLA Ops:
  0.6 1.4 %shard_map.95 = (bf16[64,256]{1,0:T(8,128)(2,1)S(1)}, bf16[128,256]{1,0:T(8,128)(2,1)S(1)}, f32[3,16,16,256]{3,2,1,0:T(8,128)S(1)}, f32[16,16,256]{2,1,0:T(8,128...) custom-call(f32[3,16,16,256]{3,2,1,0:T(8,128)} %refs_0_.1, ...), custom_call_target="tpu_custom_call" | custom-call | bytes 1048576 | tf_op jit(solution)/shard_map/pallas_call | solution.py:42
  2.0 3.0 %collective-permute-start = (bf16[64,256]{1,0:T(8,128)(2,1)S(1)}, bf16[64,256]{1,0:T(8,128)(2,1)S(1)}, u32[]{:S(2)}, u32[]{:S(2)}) collective-permute-start(bf16[64,256]{1,0:T(8,128)(2,1)S(1)} %get-tuple-element.42.refs_10_), channel_id=1, source_target_pairs={{0,2},{2,0},{1,3},{3,1},{4,6},{6,4},{5,7},{7,5},{8,10},{10,8},{9,1... | collective-permute-start | bytes 98312 | tf_op jit(solution)/shard_map/ppermute | solution.py:752
  5.0 0.1 collective-permute-start.1
  5.1 1.9 %shard_map.96 = (f32[8,2048]{1,0:T(8,128)S(1)}, bf16[256,2048]{1,0:T(8,128)(2,1)S(1)}, s32[1,2048]{1,0:T(1,128)S(1)}, bf16[256,2048]{1,0:T(8,128)(2,1)S(1)}) custom-call(f32[3,16,16,256]{3,2,1,0:T(8,128)S(1)} %get-tuple-element.31.refs_0_.refs_3_.refs_1_, s32[16,128]{1,0:T(8,128)S(1)} %get-tuple-element.35.refs_1_.refs_4_, ...), custom_call_target="tpu_custom_call" | custom-call | flops 1610612736 | bytes 1048576 | tf_op jit(solution)/shard_map/pallas_call | solution.py:42
  7.0 0.0 collective-permute-done.refs_11_
  7.0 1.6 %shard_map.97 = (bf16[8,2,40,128]{3,2,1,0:T(8,128)(2,1)}, f32[2,24,256]{2,1,0:T(8,128)S(1)}, f32[40,128]{1,0:T(8,128)S(1)}) custom-call(f32[3,16,16,256]{3,2,1,0:T(8,128)S(1)} %get-tuple-element.31.refs_0_.refs_3_.refs_1_, f32[16,16,256]{2,1,0:T(8,128)S(1)} %get-tuple-element.32.refs_1_.refs_4_.refs_2_, bf16[32,32]{1,0:T(8,128)(2,1)S(1)} %get-tuple-element.33.refs_2_, ...), custom_call_target="tpu_custom_call" | custom-call | flops 167772160 | bytes 2097152 | tf_op jit(solution)/shard_map/pallas_call | solution.py:42
  8.6 0.7 %collective-permute-done.1.refs_1_.refs_2_ = bf16[128,256]{1,0:T(8,128)(2,1)S(1)} collective-permute-done((bf16[128,256]{1,0:T(8,128)(2,1)S(1)}, bf16[128,256]{1,0:T(8,128)(2,1)S(1)}, u32[]{:S(2)}, u32[]{:S(2)}) %collective-permute-start.1) | collective-permute-done | bytes 65568 | tf_op jit(solution)/shard_map/ppermute | solution.py:753
  9.3 0.2 shard_map.98
  9.5 5.8 %all-to-all-start = ((bf16[8,2,40,128]{3,2,1,0:T(8,128)(2,1)}), bf16[8,2,40,128]{3,2,1,0:T(8,128)(2,1)S(1)}, u32[]{:S(2)}, u32[]{:S(2)}) async-start(bf16[8,2,40,128]{3,2,1,0:T(8,128)(2,1)} %get-tuple-element.50), calls=%async_computation | async-start | bytes 327680 | tf_op jit(solution)/shard_map/all_to_all | solution.py:824
  15.3 2.0 %collective-permute-start.2 = (bf16[144,256]{1,0:T(8,128)(2,1)S(1)}, bf16[144,256]{1,0:T(8,128)(2,1)S(1)}, u32[]{:S(2)}, u32[]{:S(2)}) collective-permute-start(bf16[144,256]{1,0:T(8,128)(2,1)S(1)} %get-tuple-element.52), channel_id=1, source_target_pairs={{0,4},{4,8},{8,12},{12,16},{16,20},{20,24},{24,28},{28,0},{1,5},{5... | collective-permute-start | bytes 221192 | tf_op jit(solution)/shard_map/ppermute | solution.py:826
  17.3 2.7 %collective-permute-start.3 = (bf16[144,256]{1,0:T(8,128)(2,1)S(1)}, bf16[144,256]{1,0:T(8,128)(2,1)S(1)}, u32[]{:S(2)}, u32[]{:S(2)}) collective-permute-start(bf16[144,256]{1,0:T(8,128)(2,1)S(1)} %get-tuple-element.53), channel_id=1, source_target_pairs={{4,0},{8,4},{12,8},{16,12},{20,16},{24,20},{28,24},{0,28},{5,1},{9... | collective-permute-start | bytes 221192 | tf_op jit(solution)/shard_map/ppermute | solution.py:827
  20.0 2.3 %shard_map.99 = (f32[3,16,16,256]{3,2,1,0:T(8,128)}, f32[3,12,16,256]{3,2,1,0:T(8,128)S(1)}, f32[3,2,24,256]{3,2,1,0:T(8,128)S(1)}, f32[3,4,24,256]{3,2,1,0:T(8,...) custom-call(f32[3,16,16,256]{3,2,1,0:T(8,128)S(1)} %get-tuple-element.31.refs_0_.refs_3_.refs_1_, ...), custom_call_target="tpu_custom_call" | custom-call | flops 16777216 | bytes 4194304 | tf_op jit(solution)/shard_map/pallas_call | solution.py:42
  22.3 0.5 %all-to-all-done.refs_1_ = bf16[8,2,40,128]{3,2,1,0:T(8,128)(2,1)S(1)} async-done(((bf16[8,2,40,128]{3,2,1,0:T(8,128)(2,1)}), bf16[8,2,40,128]{3,2,1,0:T(8,128)(2,1)S(1)}, u32[]{:S(2)}, u32[]{:S(2)}) %all-to-all-start) | async-done | bytes 163872 | tf_op jit(solution)/shard_map/all_to_all | solution.py:824
  22.9 0.1 shard_map.100.refs_0_
  23.0 0.1 collective-permute-start.4
  23.1 0.8 %shard_map.103 = f32[10,4096]{1,0:T(8,128)} custom-call(f32[3,24,128]{2,1,0:T(8,128)S(1)} %shard_map.100.refs_0_, bf16[8,2,40,128]{3,2,1,0:T(8,128)(2,1)S(1)} %all-to-all-done.refs_1_), custom_call_target="tpu_custom_call" | custom-call | bytes 1048576 | tf_op jit(solution)/shard_map/pallas_call | solution.py:42
  23.8 0.0 collective-permute-done.2.refs_5_
  23.9 0.0 collective-permute-done.3.refs_6_
  23.9 0.3 %shard_map.101 = (f32[3,4,16,256]{3,2,1,0:T(8,128)S(1)}, f32[16,128]{1,0:T(8,128)S(1)}, f32[8,128]{1,0:T(8,128)S(1)}) custom-call(f32[3,24,128]{2,1,0:T(8,128)S(1)} %shard_map.100.refs_0_, f32[3,16,16,256]{3,2,1,0:T(8,128)S(1)} %get-tuple-element.31.refs_0_.refs_3_.refs_1_, f32[16,16,256]{2,1,0:T(8,128)S(1)} %get-tuple-element.32.refs_1_.refs_4_.refs_2_, ...), custom_call_target="tpu_custom_call" | custom-call | flops 8388608 | bytes 2097152 | tf_op jit(solution)/shard_map/pallas_call | solution.py:42
  24.2 0.0 collective-permute-done.4.refs_6_
  24.3 1.3 %shard_map.102 = f32[3,16,16,256]{3,2,1,0:T(8,128)} custom-call(f32[3,16,16,256]{3,2,1,0:T(8,128)} %get-tuple-element.47.refs_0_, f32[3,12,16,256]{3,2,1,0:T(8,128)S(1)} %get-tuple-element.48.refs_1_, f32[3,4,16,256]{3,2,1,0:T(8,128)S(1)} %get-tuple-element.57.refs_2_, ...), custom_call_target="tpu_custom_call", output_to_operand_aliasing={{}: (0, {})} | custom-call | flops 4194304 | bytes 2097152 | tf_op jit(solution)/shard_map/pallas_call | solution.py:42
Async XLA Ops:
  2.0 5.0 %collective-permute-start = (bf16[64,256]{1,0:T(8,128)(2,1)S(1)}, bf16[64,256]{1,0:T(8,128)(2,1)S(1)}, u32[]{:S(2)}, u32[]{:S(2)}) collective-permute-start(bf16[64,256]{1,0:T(8,128)(2,1)S(1)} %get-tuple-element.42.refs_10_), channel_id=1, source_target_pairs={{0,2},{2,0},{1,3},{3,1},{4,6},{6,4},{5,7},{7,5},{8,10},{10,8},{9,1... | collective-permute-start | bytes 98312 | tf_op jit(solution)/shard_map/ppermute | solution.py:752
  5.0 4.3 %collective-permute-start.1 = (bf16[128,256]{1,0:T(8,128)(2,1)S(1)}, bf16[128,256]{1,0:T(8,128)(2,1)S(1)}, u32[]{:S(2)}, u32[]{:S(2)}) collective-permute-start(bf16[128,256]{1,0:T(8,128)(2,1)S(1)} %get-tuple-element.45), channel_id=1, source_target_pairs={{0,2},{2,0},{1,3},{3,1},{4,6},{6,4},{5,7},{7,5},{8,10},{10,8},{9,1... | collective-permute-start | bytes 196616 | tf_op jit(solution)/shard_map/ppermute | solution.py:753
  9.5 13.4 %all-to-all-start = ((bf16[8,2,40,128]{3,2,1,0:T(8,128)(2,1)}), bf16[8,2,40,128]{3,2,1,0:T(8,128)(2,1)S(1)}, u32[]{:S(2)}, u32[]{:S(2)}) async-start(bf16[8,2,40,128]{3,2,1,0:T(8,128)(2,1)} %get-tuple-element.50), calls=%async_computation | async-start | bytes 327680 | tf_op jit(solution)/shard_map/all_to_all | solution.py:824
  15.3 8.6 %collective-permute-start.2 = (bf16[144,256]{1,0:T(8,128)(2,1)S(1)}, bf16[144,256]{1,0:T(8,128)(2,1)S(1)}, u32[]{:S(2)}, u32[]{:S(2)}) collective-permute-start(bf16[144,256]{1,0:T(8,128)(2,1)S(1)} %get-tuple-element.52), channel_id=1, source_target_pairs={{0,4},{4,8},{8,12},{12,16},{16,20},{20,24},{24,28},{28,0},{1,5},{5... | collective-permute-start | bytes 221192 | tf_op jit(solution)/shard_map/ppermute | solution.py:826
  17.3 6.6 %collective-permute-start.3 = (bf16[144,256]{1,0:T(8,128)(2,1)S(1)}, bf16[144,256]{1,0:T(8,128)(2,1)S(1)}, u32[]{:S(2)}, u32[]{:S(2)}) collective-permute-start(bf16[144,256]{1,0:T(8,128)(2,1)S(1)} %get-tuple-element.53), channel_id=1, source_target_pairs={{4,0},{8,4},{12,8},{16,12},{20,16},{24,20},{28,24},{0,28},{5,1},{9... | collective-permute-start | bytes 221192 | tf_op jit(solution)/shard_map/ppermute | solution.py:827
  23.0 1.3 %collective-permute-start.4 = (f32[3,24,128]{2,1,0:T(8,128)S(1)}, f32[3,24,128]{2,1,0:T(8,128)S(1)}, u32[]{:S(2)}, u32[]{:S(2)}) collective-permute-start(f32[3,24,128]{2,1,0:T(8,128)S(1)} %shard_map.100.refs_0_), channel_id=1, source_target_pairs={{0,1},{1,0},{2,3},{3,2},{4,5},{5,4},{6,7},{7,6},{8,9},{9,8},{10,11... | collective-permute-start | bytes 110600 | tf_op jit(solution)/shard_map/ppermute | solution.py:891

commit v8 on v7

--- a/solution.py
+++ b/solution.py
@@ -686,8 +686,8 @@
             copies[-1].start()
     beyond = beyond_ref[0:1], beyond_ref[1:2]
     adds = contribution(nspan, pitch, radial, face_ref, beyond, rows_ref[...], window_ref)
-    part = pitch // 4
-    for n in range(4):
+    part = pitch // 8
+    for n in range(8):
         for i in range(n * part, (n + 1) * part):
             block = column(q == 0, adds, i)
             for f in range(nfield):
@@ -896,7 +896,7 @@
         [ANY] + [VMEM] * 6,
         [
             pltpu.VMEM((nfield, pitch, radial, LANES), F32),
-            pltpu.SemaphoreType.DMA((6,)),
+            pltpu.SemaphoreType.DMA((10,)),
         ],
         flops=2**22,
         nbytes=2**21,

time: 25.9 us -> 25.9 us (level)
  no operation moved by 1% of the time
where the time goes in v8:
time: 25.9 us; the launch traced here: 25.6 us
  starting transfers between devices  13.7 us (53%)
  Pallas kernels  9.86 us (38%)
  waiting for transfers between devices  1.3 us (5%)
  between operations  0.7 us (3%)
    pallas_call x9, Pallas kernels, call(): pl.pallas_call(body, out_shape=tuple((shape(s, d) for s, d in outs)), in_...  9.86 us
    all_to_all x1, starting transfers between devices, local(): buf = lax.all_to_all(buf, 'pitch', 0, 0)  5.82 us
    ppermute x1, starting transfers between devices, local(): span_got = (packed[0], lax.ppermute(packed[0], 'span', swap))  3.03 us
    ppermute x1, starting transfers between devices, local(): upper = lax.ppermute(down, 'pitch', [(b, a) for a, b in ring])  2.73 us
    ppermute x1, starting transfers between devices, local(): lower = lax.ppermute(up, 'pitch', ring)  2.02 us
    ppermute x1, waiting for transfers between devices, local(): low = high = lax.ppermute(packed[1], 'span', swap)  0.71 us
  transfers between devices with their start and end apart: 6, of which 2 were waited for; matrix products, arithmetic and copies ran while one was open for 0% of the time, Pallas kernels for 27%

profile of v8, /device:TPU:0, one launch (start us, length us, event | category | flops | bytes accessed | tf_op | source)
XLA Modules:
  0.0 25.6 jit_solution(12411819619599367364)
XLA Ops:
  0.6 1.4 %shard_map.95 = (bf16[64,256]{1,0:T(8,128)(2,1)S(1)}, bf16[128,256]{1,0:T(8,128)(2,1)S(1)}, f32[3,16,16,256]{3,2,1,0:T(8,128)S(1)}, f32[16,16,256]{2,1,0:T(8,128...) custom-call(f32[3,16,16,256]{3,2,1,0:T(8,128)} %refs_0_.1, ...), custom_call_target="tpu_custom_call" | custom-call | bytes 1048576 | tf_op jit(solution)/shard_map/pallas_call | solution.py:42
  2.0 3.0 %collective-permute-start = (bf16[64,256]{1,0:T(8,128)(2,1)S(1)}, bf16[64,256]{1,0:T(8,128)(2,1)S(1)}, u32[]{:S(2)}, u32[]{:S(2)}) collective-permute-start(bf16[64,256]{1,0:T(8,128)(2,1)S(1)} %get-tuple-element.42.refs_10_), channel_id=1, source_target_pairs={{0,2},{2,0},{1,3},{3,1},{4,6},{6,4},{5,7},{7,5},{8,10},{10,8},{9,1... | collective-permute-start | bytes 98312 | tf_op jit(solution)/shard_map/ppermute | solution.py:752
  5.0 0.1 collective-permute-start.1
  5.1 1.9 %shard_map.96 = (f32[8,2048]{1,0:T(8,128)S(1)}, bf16[256,2048]{1,0:T(8,128)(2,1)S(1)}, s32[1,2048]{1,0:T(1,128)S(1)}, bf16[256,2048]{1,0:T(8,128)(2,1)S(1)}) custom-call(f32[3,16,16,256]{3,2,1,0:T(8,128)S(1)} %get-tuple-element.31.refs_0_.refs_3_.refs_1_, s32[16,128]{1,0:T(8,128)S(1)} %get-tuple-element.35.refs_1_.refs_4_, ...), custom_call_target="tpu_custom_call" | custom-call | flops 1610612736 | bytes 1048576 | tf_op jit(solution)/shard_map/pallas_call | solution.py:42
  7.0 0.0 collective-permute-done.refs_11_
  7.0 1.6 %shard_map.97 = (bf16[8,2,40,128]{3,2,1,0:T(8,128)(2,1)}, f32[2,24,256]{2,1,0:T(8,128)S(1)}, f32[40,128]{1,0:T(8,128)S(1)}) custom-call(f32[3,16,16,256]{3,2,1,0:T(8,128)S(1)} %get-tuple-element.31.refs_0_.refs_3_.refs_1_, f32[16,16,256]{2,1,0:T(8,128)S(1)} %get-tuple-element.32.refs_1_.refs_4_.refs_2_, bf16[32,32]{1,0:T(8,128)(2,1)S(1)} %get-tuple-element.33.refs_2_, ...), custom_call_target="tpu_custom_call" | custom-call | flops 167772160 | bytes 2097152 | tf_op jit(solution)/shard_map/pallas_call | solution.py:42
  8.6 0.7 %collective-permute-done.1.refs_1_.refs_2_ = bf16[128,256]{1,0:T(8,128)(2,1)S(1)} collective-permute-done((bf16[128,256]{1,0:T(8,128)(2,1)S(1)}, bf16[128,256]{1,0:T(8,128)(2,1)S(1)}, u32[]{:S(2)}, u32[]{:S(2)}) %collective-permute-start.1) | collective-permute-done | bytes 65568 | tf_op jit(solution)/shard_map/ppermute | solution.py:753
  9.3 0.2 shard_map.98
  9.5 5.8 %all-to-all-start = ((bf16[8,2,40,128]{3,2,1,0:T(8,128)(2,1)}), bf16[8,2,40,128]{3,2,1,0:T(8,128)(2,1)S(1)}, u32[]{:S(2)}, u32[]{:S(2)}) async-start(bf16[8,2,40,128]{3,2,1,0:T(8,128)(2,1)} %get-tuple-element.50), calls=%async_computation | async-start | bytes 327680 | tf_op jit(solution)/shard_map/all_to_all | solution.py:824
  15.3 2.0 %collective-permute-start.2 = (bf16[144,256]{1,0:T(8,128)(2,1)S(1)}, bf16[144,256]{1,0:T(8,128)(2,1)S(1)}, u32[]{:S(2)}, u32[]{:S(2)}) collective-permute-start(bf16[144,256]{1,0:T(8,128)(2,1)S(1)} %get-tuple-element.52), channel_id=1, source_target_pairs={{0,4},{4,8},{8,12},{12,16},{16,20},{20,24},{24,28},{28,0},{1,5},{5... | collective-permute-start | bytes 221192 | tf_op jit(solution)/shard_map/ppermute | solution.py:826
  17.3 2.7 %collective-permute-start.3 = (bf16[144,256]{1,0:T(8,128)(2,1)S(1)}, bf16[144,256]{1,0:T(8,128)(2,1)S(1)}, u32[]{:S(2)}, u32[]{:S(2)}) collective-permute-start(bf16[144,256]{1,0:T(8,128)(2,1)S(1)} %get-tuple-element.53), channel_id=1, source_target_pairs={{4,0},{8,4},{12,8},{16,12},{20,16},{24,20},{28,24},{0,28},{5,1},{9... | collective-permute-start | bytes 221192 | tf_op jit(solution)/shard_map/ppermute | solution.py:827
  20.0 2.3 %shard_map.99 = (f32[3,16,16,256]{3,2,1,0:T(8,128)}, f32[3,12,16,256]{3,2,1,0:T(8,128)S(1)}, f32[3,2,24,256]{3,2,1,0:T(8,128)S(1)}, f32[3,4,24,256]{3,2,1,0:T(8,...) custom-call(f32[3,16,16,256]{3,2,1,0:T(8,128)S(1)} %get-tuple-element.31.refs_0_.refs_3_.refs_1_, ...), custom_call_target="tpu_custom_call" | custom-call | flops 16777216 | bytes 4194304 | tf_op jit(solution)/shard_map/pallas_call | solution.py:42
  22.3 0.5 %all-to-all-done.refs_1_ = bf16[8,2,40,128]{3,2,1,0:T(8,128)(2,1)S(1)} async-done(((bf16[8,2,40,128]{3,2,1,0:T(8,128)(2,1)}), bf16[8,2,40,128]{3,2,1,0:T(8,128)(2,1)S(1)}, u32[]{:S(2)}, u32[]{:S(2)}) %all-to-all-start) | async-done | bytes 163872 | tf_op jit(solution)/shard_map/all_to_all | solution.py:824
  22.9 0.1 shard_map.100.refs_0_
  23.0 0.1 collective-permute-start.4
  23.1 0.8 %shard_map.103 = f32[10,4096]{1,0:T(8,128)} custom-call(f32[3,24,128]{2,1,0:T(8,128)S(1)} %shard_map.100.refs_0_, bf16[8,2,40,128]{3,2,1,0:T(8,128)(2,1)S(1)} %all-to-all-done.refs_1_), custom_call_target="tpu_custom_call" | custom-call | bytes 1048576 | tf_op jit(solution)/shard_map/pallas_call | solution.py:42
  23.8 0.0 collective-permute-done.2.refs_5_
  23.9 0.0 collective-permute-done.3.refs_6_
  23.9 0.3 %shard_map.101 = (f32[3,4,16,256]{3,2,1,0:T(8,128)S(1)}, f32[16,128]{1,0:T(8,128)S(1)}, f32[8,128]{1,0:T(8,128)S(1)}) custom-call(f32[3,24,128]{2,1,0:T(8,128)S(1)} %shard_map.100.refs_0_, f32[3,16,16,256]{3,2,1,0:T(8,128)S(1)} %get-tuple-element.31.refs_0_.refs_3_.refs_1_, f32[16,16,256]{2,1,0:T(8,128)S(1)} %get-tuple-element.32.refs_1_.refs_4_.refs_2_, ...), custom_call_target="tpu_custom_call" | custom-call | flops 8388608 | bytes 2097152 | tf_op jit(solution)/shard_map/pallas_call | solution.py:42
  24.2 0.0 collective-permute-done.4.refs_6_
  24.3 1.4 %shard_map.102 = f32[3,16,16,256]{3,2,1,0:T(8,128)} custom-call(f32[3,16,16,256]{3,2,1,0:T(8,128)} %get-tuple-element.47.refs_0_, f32[3,12,16,256]{3,2,1,0:T(8,128)S(1)} %get-tuple-element.48.refs_1_, f32[3,4,16,256]{3,2,1,0:T(8,128)S(1)} %get-tuple-element.57.refs_2_, ...), custom_call_target="tpu_custom_call", output_to_operand_aliasing={{}: (0, {})} | custom-call | flops 4194304 | bytes 2097152 | tf_op jit(solution)/shard_map/pallas_call | solution.py:42
Async XLA Ops:
  2.0 5.0 %collective-permute-start = (bf16[64,256]{1,0:T(8,128)(2,1)S(1)}, bf16[64,256]{1,0:T(8,128)(2,1)S(1)}, u32[]{:S(2)}, u32[]{:S(2)}) collective-permute-start(bf16[64,256]{1,0:T(8,128)(2,1)S(1)} %get-tuple-element.42.refs_10_), channel_id=1, source_target_pairs={{0,2},{2,0},{1,3},{3,1},{4,6},{6,4},{5,7},{7,5},{8,10},{10,8},{9,1... | collective-permute-start | bytes 98312 | tf_op jit(solution)/shard_map/ppermute | solution.py:752
  5.0 4.3 %collective-permute-start.1 = (bf16[128,256]{1,0:T(8,128)(2,1)S(1)}, bf16[128,256]{1,0:T(8,128)(2,1)S(1)}, u32[]{:S(2)}, u32[]{:S(2)}) collective-permute-start(bf16[128,256]{1,0:T(8,128)(2,1)S(1)} %get-tuple-element.45), channel_id=1, source_target_pairs={{0,2},{2,0},{1,3},{3,1},{4,6},{6,4},{5,7},{7,5},{8,10},{10,8},{9,1... | collective-permute-start | bytes 196616 | tf_op jit(solution)/shard_map/ppermute | solution.py:753
  9.5 13.4 %all-to-all-start = ((bf16[8,2,40,128]{3,2,1,0:T(8,128)(2,1)}), bf16[8,2,40,128]{3,2,1,0:T(8,128)(2,1)S(1)}, u32[]{:S(2)}, u32[]{:S(2)}) async-start(bf16[8,2,40,128]{3,2,1,0:T(8,128)(2,1)} %get-tuple-element.50), calls=%async_computation | async-start | bytes 327680 | tf_op jit(solution)/shard_map/all_to_all | solution.py:824
  15.3 8.6 %collective-permute-start.2 = (bf16[144,256]{1,0:T(8,128)(2,1)S(1)}, bf16[144,256]{1,0:T(8,128)(2,1)S(1)}, u32[]{:S(2)}, u32[]{:S(2)}) collective-permute-start(bf16[144,256]{1,0:T(8,128)(2,1)S(1)} %get-tuple-element.52), channel_id=1, source_target_pairs={{0,4},{4,8},{8,12},{12,16},{16,20},{20,24},{24,28},{28,0},{1,5},{5... | collective-permute-start | bytes 221192 | tf_op jit(solution)/shard_map/ppermute | solution.py:826
  17.3 6.6 %collective-permute-start.3 = (bf16[144,256]{1,0:T(8,128)(2,1)S(1)}, bf16[144,256]{1,0:T(8,128)(2,1)S(1)}, u32[]{:S(2)}, u32[]{:S(2)}) collective-permute-start(bf16[144,256]{1,0:T(8,128)(2,1)S(1)} %get-tuple-element.53), channel_id=1, source_target_pairs={{4,0},{8,4},{12,8},{16,12},{20,16},{24,20},{28,24},{0,28},{5,1},{9... | collective-permute-start | bytes 221192 | tf_op jit(solution)/shard_map/ppermute | solution.py:827
  23.0 1.3 %collective-permute-start.4 = (f32[3,24,128]{2,1,0:T(8,128)S(1)}, f32[3,24,128]{2,1,0:T(8,128)S(1)}, u32[]{:S(2)}, u32[]{:S(2)}) collective-permute-start(f32[3,24,128]{2,1,0:T(8,128)S(1)} %shard_map.100.refs_0_), channel_id=1, source_target_pairs={{0,1},{1,0},{2,3},{3,2},{4,5},{5,4},{6,7},{7,6},{8,9},{9,8},{10,11... | collective-permute-start | bytes 110600 | tf_op jit(solution)/shard_map/ppermute | solution.py:891
